TPU v7x, 32 devices: a whole 2x2x4 slice. The times are simulated.
32 devices in a mesh: row: 4 (over x, core), col: 8 (over z, y).
Axes of the slice: x: 2, y: 2, z: 4, core: 2. Of those that a mesh axis runs over, the one named last changes fastest.
Arguments:
- specimen: float32 [2, 512, 2048], P(None, 'row', 'col'), may hold values from -6 to 6
- probe_field: float32 [2, 256, 256], replicated, may hold values from -6 to 6
- scan_offsets: int32 [4, 8, 2, 2], replicated, may hold values from -128 to 128, as said below
- live_counts: int32 [4, 8], replicated, may hold values from 1 to 2, as said below
- magnitudes: float32 [4, 8, 2, 256, 256], P('row', 'col'), may hold values from 0 to 2
Outputs:
- specimen_next: float32 [2, 512, 2048], P(None, 'row', 'col')
- probe_next: float32 [2, 256, 256], replicated
Inputs may be any that keep to these rules, and one draw needn't show every extreme that they name: `scan_offsets`: rows of a patch start within -128 to 0 of the tile's first row, columns within -128 to 128 of its first column. Tile (a, b) owns the positions in its first live_counts[a, b] slots.
All inputs are finite; a program needn't handle non-finite values.
Results may differ from a plain program's by a relative error of at most 0.0003.
Values sent between devices are 32-bit elements; how exact they have to be, the bound alone decides.
No kernel may reach another device: no remote copies, remote signals or barrier semaphores. Data moves between devices by JAX's collectives and lax.ppermute only.
A program may use at most 64 MiB of HBM per device.

v0:
```python
import math

import jax
import jax.numpy as jnp
from jax import lax
from jax.sharding import PartitionSpec as P

modulus_floor = 0.25
object_damping = 0.1
probe_damping = 0.1


def extended_2(block, sides, width):
    for axis, dim in sides:
        count = lax.axis_size(axis)
        forward = [(i, i + 1) for i in range(count - 1)]
        backward = [(target, source) for source, target in forward]
        low = lax.ppermute(
            lax.slice_in_dim(block, block.shape[dim] - width, None, axis=dim), axis, forward
        )
        high = lax.ppermute(lax.slice_in_dim(block, 0, width, axis=dim), axis, backward)
        block = jnp.concatenate([low, block, high], axis=dim)
    return block


def dft_tables(width):
    counter = jnp.arange(width, dtype=jnp.int32)
    phase = counter[:, None] * counter[None, :] % width
    angle = phase.astype(jnp.float32) * (2.0 * math.pi / width)
    factor = 1.0 / math.sqrt(width)
    return (jnp.cos(angle) * factor, jnp.sin(angle) * factor)


def matmul_right(left, table):
    return jnp.einsum("sjm,ml->sjl", left, table, precision=lax.Precision.HIGHEST)


def matmul_left(table, right):
    return jnp.einsum("kj,sjl->skl", table, right, precision=lax.Precision.HIGHEST)


def transform(wave_real, wave_imag, cosine, sine, direction):
    inner_real = matmul_right(wave_real, cosine) + direction * matmul_right(wave_imag, sine)
    inner_imag = matmul_right(wave_imag, cosine) - direction * matmul_right(wave_real, sine)
    outer_real = matmul_left(cosine, inner_real) + direction * matmul_left(sine, inner_imag)
    outer_imag = matmul_left(cosine, inner_imag) - direction * matmul_left(sine, inner_real)
    return (outer_real, outer_imag)


def fold_rims(wide, tile_r, tile_c, half):
    center = wide[:, 2 * half : 2 * half + tile_r, :]
    center = center.at[:, :half, :].add(wide[:, :half, :])
    center = center.at[:, tile_r - half :, :].add(wide[:, tile_r + 3 * half :, :])
    result = center[:, :, 2 * half : 2 * half + tile_c]
    result = result.at[:, :, :half].add(center[:, :, :half])
    result = result.at[:, :, tile_c - half :].add(center[:, :, tile_c + 3 * half :])
    return result


def shards(specimen, probe_field, scan_offsets, live_counts, magnitudes):
    width = probe_field.shape[1]
    half = width // 2
    tile_r = specimen.shape[1]
    tile_c = specimen.shape[2]
    slots = magnitudes.shape[2]
    row_place = lax.axis_index("row")
    col_place = lax.axis_index("col")
    zero_index = jnp.zeros((), jnp.int32)
    extended = extended_2(specimen, (("row", 1), ("col", 2)), half)
    offsets_here = scan_offsets[row_place, col_place]
    live = (jnp.arange(slots, dtype=jnp.int32) < live_counts[row_place, col_place]).astype(
        jnp.float32
    )[:, None, None]
    row_starts = offsets_here[:, 0] + half
    col_starts = offsets_here[:, 1] + half

    def extract(row_start, col_start):
        return lax.dynamic_slice(extended, (zero_index, row_start, col_start), (2, width, width))

    patches = jax.vmap(extract)(row_starts, col_starts)
    patch_real = patches[:, 0]
    patch_imag = patches[:, 1]
    probe_real = probe_field[0]
    probe_imag = probe_field[1]
    power = probe_real * probe_real + probe_imag * probe_imag
    cosine, sine = dft_tables(width)
    wave_real = probe_real * patch_real - probe_imag * patch_imag
    wave_imag = probe_real * patch_imag + probe_imag * patch_real
    far_real, far_imag = transform(wave_real, wave_imag, cosine, sine, 1.0)
    modulus = jnp.sqrt(far_real * far_real + far_imag * far_imag)
    factor = magnitudes[0, 0] / jnp.maximum(modulus, modulus_floor) - 1.0
    diff_real, diff_imag = transform(far_real * factor, far_imag * factor, cosine, sine, -1.0)
    diff_real = diff_real * live
    diff_imag = diff_imag * live
    grad_real = probe_real * diff_real + probe_imag * diff_imag
    grad_imag = probe_real * diff_imag - probe_imag * diff_real
    pieces = jnp.stack([grad_real, grad_imag, live * power], axis=1)
    layers = pieces.shape[1]

    def place(slot, total):
        start = (zero_index, row_starts[slot], col_starts[slot])
        current = lax.dynamic_slice(total, start, (layers, width, width))
        return lax.dynamic_update_slice(total, current + pieces[slot], start)

    start_total = jnp.zeros((layers, tile_r + 2 * half, tile_c + 2 * half), jnp.float32)
    buffer = lax.fori_loop(0, slots, place, start_total)
    wide = extended_2(buffer, (("row", 1), ("col", 2)), half)
    folded = fold_rims(wide, tile_r, tile_c, half)
    update = folded[:2]
    lighting = folded[2]
    damping = object_damping * jnp.max(power)
    specimen_next = specimen + update / (lighting + damping)
    local_terms = (
        jnp.sum(patch_real * diff_real + patch_imag * diff_imag, 0),
        jnp.sum(patch_real * diff_imag - patch_imag * diff_real, 0),
        jnp.sum(live * (patch_real * patch_real + patch_imag * patch_imag), 0),
    )
    sum_real, sum_imag, weight = lax.psum(
        (local_terms[0], local_terms[1], local_terms[2]), ("row", "col")
    )
    denominator = weight + probe_damping * jnp.mean(weight)
    probe_next = probe_field + jnp.stack([sum_real, sum_imag]) / denominator
    return (specimen_next, probe_next)


def solution(mesh):
    return jax.shard_map(
        shards,
        mesh=mesh,
        in_specs=(P(None, "row", "col"), P(), P(), P(), P("row", "col", None, None, None)),
        out_specs=(P(None, "row", "col"), P()),
        check_vma=False,
    )
```

profile of v0, /device:TPU:0, one launch (start us, length us, event | category | flops | bytes accessed | tf_op | source)
XLA Modules:
  0.0 299.0 jit_solution(12655990677331390585)
XLA Ops:
  7.2 2.5 collective-permute-start
  9.8 1.3 collective-permute-start.1
  11.1 1.1 slice_bitcast_fusion.1
  12.6 1.3 dynamic_slice.35
  13.9 1.6 collective-permute-done.1
  16.5 3.4 %collective-permute-start.2 = (f32[2,384,128]{2,1,0:T(8,128)}, f32[2,384,128]{2,1,0:T(8,128)S(1)}, u32[]{:S(2)}, u32[]{:S(2)}) collective-permute-start(f32[2,384,128]{2,1,0:T(8,128)} %get-tuple-element.217), channel_id=1, source_target_pairs={{0,1},{1,2},{2,3},{3,4},{4,5},{5,6},{6,7},{8,9},{9,10},{10,11},{11... | collective-permute-start | bytes 1179656 | tf_op jit(solution)/shard_map/ppermute | solution.py:18
  19.9 1.3 collective-permute-start.3
  21.9 1.0 copy.32
  23.1 2.7 collective-permute-done.2
  26.6 4.0 %collective-permute-done.3 = f32[2,384,128]{2,1,0:T(8,128)} collective-permute-done((f32[2,384,128]{2,1,0:T(8,128)}, f32[2,384,128]{2,1,0:T(8,128)}, u32[]{:S(2)}, u32[]{:S(2)}) %collective-permute-start.3) | collective-permute-done | bytes 393248 | tf_op jit(solution)/shard_map/ppermute | solution.py:21
  30.6 1.3 pad_maximum_fusion
  31.8 5.8 %while.21 = (s32[]{:T(128)}, f32[2,384,512]{2,1,0:T(8,128)S(1)}, s32[2,3]{1,0:T(2,128)S(1)}, f32[2,2,256,256]{3,2,0,1:T(8,128)}, s32[]{:T(128)}) while((s32[]{:T(128)}, f32[2,384,512]{2,1,0:T(8,128)S(1)}, s32[2,3]{1,0:T(2,128)S(1)}, f32[2,2,256,256]{3,2,0,1:T(8,128)}, s32[]{:T(128)}) %tuple.85), condition=%wide.while_cond.4, body=%wide.while_body.4.sunk | while | flops 2 | bytes 1050217 | solution.py:78
  32.5 2.3 bitcast_dynamic-update-slice_fusion.2
  35.4 2.2 bitcast_dynamic-update-slice_fusion.2
  37.7 2.9 fusion.49
  40.6 1.6 fusion.53
  42.2 1.6 convolution_subtract_fusion.1
  43.8 1.8 fusion.47
  45.6 1.6 convolution_add_fusion.1
  47.2 1.8 fusion.51
  49.0 2.0 fusion.8
  51.1 2.0 fusion.25
  53.1 1.6 fusion.41
  54.7 1.7 fusion.45
  56.4 1.7 fusion.5
  58.0 1.7 fusion.6
  59.7 1.6 fusion.43
  61.3 2.6 fusion.39
  63.9 2.4 fusion.4
  66.3 1.2 copy.44
  67.5 4.0 %fusion.16 = (f32[256,256]{1,0:T(8,128)}, f32[256,256]{1,0:T(8,128)}, f32[256,256]{1,0:T(8,128)}, f32[2,1,256,256]{3,2,0,1:T(8,128)S(1)}, f32[2,1,256,256]{3,2,0,1:T(8,128)S(1)}) fusion(f32[2,256,256]{1,2,0:T(8,128)S(1)} %copy.44, f32[2,2,256,256]{3,2,0,1:T(8,128)S(1)} %copy-done.4, f32[2]{0:T(128)S(1)} %compare_convert_fusion, ...), kind=kOutput, calls=%fused_computation.37 | convolution fusion | flops 406323200 | bytes 4981760 | tf_op jit(solution)/shard_map/kj,sjl->skl/dot_general | solution.py:39
  71.5 1.3 pad_maximum_fusion.1
  73.1 36.8 %while.20 = (s32[]{:T(128)}, f32[3,384,512]{2,1,0:T(8,128)S(1)}, s32[2]{0:T(128)S(1)}, s32[2]{0:T(128)S(1)}, f32[2,3,256,256]{3,2,0,1:T(8,128)}, /*index=5*/s32[]{:T(128)}, s32[]{:T(128)}, s32[]{:T(128)}, s32[]{:T(128)}) while((s32[]{:T(128)}, f32[3,384,512]{2,1,0:T(8,128)S(1)}, s32[2]{0:T(128)S(1)}, s32[2]{0:T(128)S(1)}, ...), condition=%wide.region_1.2_spmd, body=%wide.region_0.1_spmd.sunk | while | flops 196616 | bytes 3932361 | solution.py:106
  78.2 1.4 bitcast_add_fusion.2
  79.6 12.8 %dynamic_update_slice.8 = f32[3,384,512]{2,1,0:T(8,128)S(1)} dynamic-update-slice(f32[3,384,512]{2,1,0:T(8,128)S(1)} %get-tuple-element.311, f32[3,256,256]{2,1,0:T(8,128)S(1)} %bitcast_add_fusion.2, s32[]{:T(128)} %constant.194.clone.1..sunk, s32[]{:T(128)S(6)} %select_n.146, s32[]{:T(128)S(6)} %select_n.147) | dynamic-update-slice | bytes 1572868 | tf_op jit(solution)/shard_map/while/body/eval_jaxpr/dynamic_update_slice | solution.py:103
  97.5 1.4 bitcast_add_fusion.2
  99.0 10.9 %dynamic_update_slice.8 = f32[3,384,512]{2,1,0:T(8,128)S(1)} dynamic-update-slice(f32[3,384,512]{2,1,0:T(8,128)S(1)} %get-tuple-element.311, f32[3,256,256]{2,1,0:T(8,128)S(1)} %bitcast_add_fusion.2, s32[]{:T(128)} %constant.194.clone.1..sunk, s32[]{:T(128)S(6)} %select_n.146, s32[]{:T(128)S(6)} %select_n.147) | dynamic-update-slice | bytes 1572868 | tf_op jit(solution)/shard_map/while/body/eval_jaxpr/dynamic_update_slice | solution.py:103
  110.0 10.3 %collective-permute-start.4 = (f32[3,128,512]{2,1,0:T(8,128)S(1)}, f32[3,128,512]{2,1,0:T(8,128)S(1)}, u32[]{:S(2)}, u32[]{:S(2)}) collective-permute-start(f32[3,128,512]{2,1,0:T(8,128)S(1)} %get-tuple-element.210), channel_id=1, source_target_pairs={{0,8},{8,16},{16,24},{1,9},{9,17},{17,25},{2,10},{10,18},{18,26},{... | collective-permute-start | bytes 2359304 | tf_op jit(solution)/shard_map/ppermute | solution.py:18
  120.4 1.3 collective-permute-start.5
  122.5 2.3 collective-permute-done.5
  124.9 1.1 fusion.146
  126.0 1.1 copy-done.1
  127.1 5.3 %collective-permute-start.6 = (f32[3,640,128]{2,1,0:T(8,128)}, f32[3,640,128]{2,1,0:T(8,128)S(1)}, u32[]{:S(2)}, u32[]{:S(2)}) collective-permute-start(f32[3,640,128]{2,1,0:T(8,128)} %get-tuple-element.207), channel_id=1, source_target_pairs={{0,1},{1,2},{2,3},{3,4},{4,5},{5,6},{6,7},{8,9},{9,10},{10,11},{11... | collective-permute-start | bytes 2949128 | tf_op jit(solution)/shard_map/ppermute | solution.py:18
  132.4 1.3 collective-permute-start.7
  135.2 147.2 %all-reduce.3.cloned.1.call-done = (f32[1,256,256]{2,1,0:T(8,128)}, f32[1,256,256]{2,1,0:T(8,128)}, f32[256,256]{1,0:T(8,128)}) async-done(((f32[1,256,256]{2,1,0:T(8,128)}, f32[1,256,256]{2,1,0:T(8,128)}, f32[256,256]{1,0:T(8,128)}), (f32[1,256,256]{2,1,0:T(8,128)}, f32[1,256,256]{2,1,0:T(8,128)}, f32[256,256]{1,0:T(8,128)})) %all-reduce.3.cloned.1.call-update) | async-done | bytes 786448 | tf_op jit(solution)/shard_map/psum | solution.py:118
  282.4 1.6 reduce_sum.39
  285.6 1.9 fusion.10
  287.6 2.0 fusion.9
  (56 shorter events, 12.7 us)
Async XLA Ops:
  7.2 5.0 %copy-start = (s32[4,8,2,2]{1,3,2,0:T(2,128)S(1)}, s32[4,8,2,2]{1,3,2,0:T(2,128)}, u32[]{:S(2)}) copy-start(s32[4,8,2,2]{1,3,2,0:T(2,128)} %param.21) | copy-start | bytes 1540
  7.2 6.7 %copy-start.5 = (f32[2,128,256]{2,1,0:T(8,128)S(1)}, f32[2,128,256]{2,1,0:T(8,128)}, u32[]{:S(2)}) copy-start(f32[2,128,256]{2,1,0:T(8,128)} %param.19) | copy-start | bytes 786436
  7.2 275.2 %all-reduce.3.cloned.1.call-start = ((), (), s32[]{:S(2)}) async-start(), calls=%async_computation | async-start | bytes 1572864 | tf_op jit(solution)/shard_map/psum | solution.py:118
  7.2 6.6 %collective-permute-start = (f32[2,128,256]{2,1,0:T(8,128)}, f32[2,128,256]{2,1,0:T(8,128)S(1)}, u32[]{:S(2)}, u32[]{:S(2)}) collective-permute-start(f32[2,128,256]{2,1,0:T(8,128)} %param.19), channel_id=1, source_target_pairs={{0,8},{8,16},{16,24},{1,9},{9,17},{17,25},{2,10},{10,18},{18,26},{... | collective-permute-start | bytes 786440 | tf_op jit(solution)/shard_map/ppermute | solution.py:18
  9.8 5.7 %collective-permute-start.1 = (f32[2,128,256]{2,1,0:T(8,128)}, f32[2,128,256]{2,1,0:T(8,128)S(1)}, u32[]{:S(2)}, u32[]{:S(2)}) collective-permute-start(f32[2,128,256]{2,1,0:T(8,128)} %param.19), channel_id=1, source_target_pairs={{8,0},{16,8},{24,16},{9,1},{17,9},{25,17},{10,2},{18,10},{26,18},{... | collective-permute-start | bytes 786440 | tf_op jit(solution)/shard_map/ppermute | solution.py:21
  13.8 8.1 %copy-start.7 = (f32[1,1,2,256,256]{4,3,2,1,0:T(8,128)S(1)}, f32[1,1,2,256,256]{4,3,2,1,0:T(8,128)}, u32[]{:S(2)}) copy-start(f32[1,1,2,256,256]{4,3,2,1,0:T(8,128)} %param.23) | copy-start | bytes 1572868
  16.5 9.3 %collective-permute-start.2 = (f32[2,384,128]{2,1,0:T(8,128)}, f32[2,384,128]{2,1,0:T(8,128)S(1)}, u32[]{:S(2)}, u32[]{:S(2)}) collective-permute-start(f32[2,384,128]{2,1,0:T(8,128)} %get-tuple-element.217), channel_id=1, source_target_pairs={{0,1},{1,2},{2,3},{3,4},{4,5},{5,6},{6,7},{8,9},{9,10},{10,11},{11... | collective-permute-start | bytes 1179656 | tf_op jit(solution)/shard_map/ppermute | solution.py:18
  19.9 10.6 %collective-permute-start.3 = (f32[2,384,128]{2,1,0:T(8,128)}, f32[2,384,128]{2,1,0:T(8,128)}, u32[]{:S(2)}, u32[]{:S(2)}) collective-permute-start(f32[2,384,128]{2,1,0:T(8,128)} %get-tuple-element.218), channel_id=1, source_target_pairs={{1,0},{2,1},{3,2},{4,3},{5,4},{6,5},{7,6},{9,8},{10,9},{11,10},{12... | collective-permute-start | bytes 1179656 | tf_op jit(solution)/shard_map/ppermute | solution.py:21
  25.8 0.8 copy-start.9
  37.7 2.9 copy-start.4
  47.2 3.9 %copy-start.8 = (f32[1,1,2,256,256]{3,4,2,1,0:T(8,128)S(1)}, f32[1,1,2,256,256]{3,4,2,1,0:T(8,128)}, u32[]{:S(2)}) copy-start(f32[1,1,2,256,256]{3,4,2,1,0:T(8,128)} %copy.32) | copy-start | bytes 1572868
  110.0 12.2 %collective-permute-start.4 = (f32[3,128,512]{2,1,0:T(8,128)S(1)}, f32[3,128,512]{2,1,0:T(8,128)S(1)}, u32[]{:S(2)}, u32[]{:S(2)}) collective-permute-start(f32[3,128,512]{2,1,0:T(8,128)S(1)} %get-tuple-element.210), channel_id=1, source_target_pairs={{0,8},{8,16},{16,24},{1,9},{9,17},{17,25},{2,10},{10,18},{18,26},{... | collective-permute-start | bytes 2359304 | tf_op jit(solution)/shard_map/ppermute | solution.py:18
  120.4 4.5 %collective-permute-start.5 = (f32[3,128,512]{2,1,0:T(8,128)S(1)}, f32[3,128,512]{2,1,0:T(8,128)S(1)}, u32[]{:S(2)}, u32[]{:S(2)}) collective-permute-start(f32[3,128,512]{2,1,0:T(8,128)S(1)} %get-tuple-element.209), channel_id=1, source_target_pairs={{8,0},{16,8},{24,16},{9,1},{17,9},{25,17},{10,2},{18,10},{26,18},{... | collective-permute-start | bytes 2359304 | tf_op jit(solution)/shard_map/ppermute | solution.py:21
  124.9 2.2 copy-start.1
  124.9 8.8 %copy-start.3 = (f32[2,256,256]{2,1,0:T(8,128)S(1)}, f32[2,256,256]{2,1,0:T(8,128)}, u32[]{:S(2)}) copy-start(f32[2,256,256]{2,1,0:T(8,128)} %param.20) | copy-start | bytes 1572868
  127.1 160.5 %collective-permute-start.6 = (f32[3,640,128]{2,1,0:T(8,128)}, f32[3,640,128]{2,1,0:T(8,128)S(1)}, u32[]{:S(2)}, u32[]{:S(2)}) collective-permute-start(f32[3,640,128]{2,1,0:T(8,128)} %get-tuple-element.207), channel_id=1, source_target_pairs={{0,1},{1,2},{2,3},{3,4},{4,5},{5,6},{6,7},{8,9},{9,10},{10,11},{11... | collective-permute-start | bytes 2949128 | tf_op jit(solution)/shard_map/ppermute | solution.py:18
  132.4 155.2 %collective-permute-start.7 = (f32[3,640,128]{2,1,0:T(8,128)S(1)}, f32[3,640,128]{2,1,0:T(8,128)S(1)}, u32[]{:S(2)}, u32[]{:S(2)}) collective-permute-start(f32[3,640,128]{2,1,0:T(8,128)S(1)} %get-tuple-element.208), channel_id=1, source_target_pairs={{1,0},{2,1},{3,2},{4,3},{5,4},{6,5},{7,6},{9,8},{10,9},{11,10},{12... | collective-permute-start | bytes 2949128 | tf_op jit(solution)/shard_map/ppermute | solution.py:21
  287.6 2.8 copy-start.2
  290.5 1.0 copy-start.6
Sparse Core Ops, SparseCore 0:
  133.8 148.4 all-reduce.2
where the time goes:
time: 300 us; the launch traced here: 299 us
  waiting for transfers between devices  158 us (53%)
  local copies, waits for them, and re-layouts  42.2 us (14%)
  matrix products  32.5 us (11%)
  starting transfers between devices  26.8 us (9%)
  between operations  15.8 us (5%)
  other arithmetic  15.7 us (5%)
  loops' own time  7.67 us (3%)
    psum x1, waiting for transfers between devices, shards(): lax.psum((local_terms[0], local_terms[1], local_terms[2]), ('row', 'col'))  147 us
    dynamic_update_slice x2, local copies, waits for them, and re-layouts, place(): return lax.dynamic_update_slice(total, current + pieces[slot], start)  23.6 us
    ppermute x4, starting transfers between devices, extended_2(): lax.ppermute(lax.slice_in_dim(block, block.shape[dim] - width, None, axis...  21.6 us
    dot_general x8, matrix products, matmul_left(): jnp.einsum('kj,sjl->skl', table, right, precision=lax.Precision.HIGHEST)  18.2 us
    dot_general x8, matrix products, matmul_right(): jnp.einsum('sjm,ml->sjl', left, table, precision=lax.Precision.HIGHEST)  14.3 us
    ppermute x4, waiting for transfers between devices, extended_2(): lax.ppermute(lax.slice_in_dim(block, 0, width, axis=dim), axis, backward)  7.89 us
    another operation x1, loops' own time, shards(): buffer = lax.fori_loop(0, slots, place, start_total)  7.65 us
  transfers between devices with their start and end apart: 9, of which 6 were waited for; matrix products, arithmetic and copies ran while one was open for 3% of the time, Pallas kernels for 0%

commit v1 on v0

v1 whole, which is shorter than its diff:
```python
import functools
import math

import jax
import jax.numpy as jnp
import ml_dtypes
import numpy as np
from jax import lax
from jax.experimental import pallas as pl
from jax.experimental.pallas import tpu as pltpu
from jax.sharding import PartitionSpec as P

modulus_floor = 0.25
object_damping = 0.1
probe_damping = 0.1
LANES = 128
SUBLANES = 8
VMEM_LIMIT = 48 * 1024 * 1024


def split_table(table):
    high = table.astype(ml_dtypes.bfloat16)
    low = (table - high.astype(np.float64)).astype(ml_dtypes.bfloat16)
    return np.stack([high, low])


def dft_tables(width):
    counter = np.arange(width)
    angle = (counter[:, None] * counter[None, :] % width) * (2.0 * math.pi / width)
    cosine = np.cos(angle) / math.sqrt(width)
    sine = np.sin(angle) / math.sqrt(width)
    turn = np.block([[cosine, -sine], [sine, cosine]])
    return split_table(turn), split_table(turn.T)


def halves(value):
    high = value.astype(jnp.bfloat16)
    return high, (value - high.astype(jnp.float32)).astype(jnp.bfloat16)


def product(left, right):
    dot = functools.partial(jnp.dot, preferred_element_type=jnp.float32)
    return dot(left[0], right[0]) + (dot(left[1], right[0]) + dot(left[0], right[1]))


def split_start(start, step, last):
    aligned = jnp.minimum(start // step, last // step) * step
    return pl.multiple_of(aligned, step), start - aligned


def lane_groups(value):
    return [value[..., at : at + LANES] for at in range(0, value.shape[-1], LANES)]


def cut(value, row_shift, lane_shift):
    rows, lanes = value.shape
    value = value.reshape(rows // SUBLANES, SUBLANES, lanes)
    lane_turn = lax.rem(LANES - lane_shift, LANES)
    row_turn = lax.rem(SUBLANES - row_shift, SUBLANES)
    shape = (rows // SUBLANES, SUBLANES, LANES)
    keep_lane = lax.broadcasted_iota(jnp.int32, shape, 2) < LANES - lane_shift
    keep_row = lax.broadcasted_iota(jnp.int32, shape, 1)[1:] < SUBLANES - row_shift
    turned = [pltpu.roll(group, lane_turn, 2) for group in lane_groups(value)]
    parts = []
    for first, second in zip(turned[:-1], turned[1:]):
        part = pltpu.roll(jnp.where(keep_lane, first, second), row_turn, 1)
        part = jnp.where(keep_row, part[:-1], part[1:])
        parts.append(part.reshape(rows - SUBLANES, LANES))
    return jnp.concatenate(parts, 1)


def spread(value, row_shift, lane_shift):
    rows, lanes = value.shape
    value = value.reshape(rows // SUBLANES, SUBLANES, lanes)
    shape = (rows // SUBLANES + 1, SUBLANES, LANES)
    lane_turn = lax.rem(lane_shift, LANES)
    take_lane = lax.broadcasted_iota(jnp.int32, shape, 2) < lane_shift
    take_row = lax.broadcasted_iota(jnp.int32, shape, 1) < row_shift
    blank_row = jnp.zeros((1, SUBLANES, LANES), value.dtype)
    turned = []
    for group in lane_groups(value):
        group = pltpu.roll(group, row_shift, 1)
        group = jnp.where(
            take_row,
            jnp.concatenate([blank_row, group], 0),
            jnp.concatenate([group, blank_row], 0),
        )
        turned.append(pltpu.roll(group, lane_turn, 2))
    blank = jnp.zeros(shape, value.dtype)
    parts = [
        jnp.where(take_lane, first, second).reshape(rows + SUBLANES, LANES)
        for first, second in zip([blank] + turned, turned + [blank])
    ]
    return jnp.concatenate(parts, 1)


def lighting_kernel(offsets, counts, probe, out, pad):
    rows, cols, slots = offsets.shape[:3]
    tile_r, tile_c = out.shape
    width = probe.shape[1]
    half = width // 2
    row_place = lax.axis_index("row")
    col_place = lax.axis_index("col")
    power = probe[0] * probe[0] + probe[1] * probe[1]
    pad[...] = jnp.zeros_like(pad)
    pad[tile_r : tile_r + width, tile_c : tile_c + width] = power
    out[...] = jnp.full(out.shape, object_damping * jnp.max(power))
    wide = tile_c + LANES
    for row_step in (-1, 0, 1):
        for col_step in (-1, 0, 1):
            row, col = row_place + row_step, col_place + col_step
            inside = (row >= 0) & (row < rows) & (col >= 0) & (col < cols)
            row_at = jnp.clip(row, 0, rows - 1)
            col_at = jnp.clip(col, 0, cols - 1)
            for slot in range(slots):
                top = offsets[row_at, col_at, slot, 0] + row_step * tile_r
                left = offsets[row_at, col_at, slot, 1] + col_step * tile_c

                @pl.when(
                    inside
                    & (slot < counts[row_at, col_at])
                    & (left > -width)
                    & (left < tile_c)
                )
                def _():
                    row, row_shift = split_start(tile_r - top, SUBLANES, tile_r + width)
                    lane, lane_shift = split_start(tile_c - left, LANES, pad.shape[1] - wide)
                    part = pad[pl.ds(row, tile_r + SUBLANES), pl.ds(lane, wide)]
                    out[...] += cut(part, row_shift, lane_shift)


def lighting(offsets, counts, probe, tile_r, tile_c):
    width = probe.shape[1]
    smem = pl.BlockSpec(memory_space=pltpu.SMEM)
    vmem = pl.BlockSpec(memory_space=pltpu.VMEM)
    return pl.pallas_call(
        lighting_kernel,
        out_shape=jax.ShapeDtypeStruct((tile_r, tile_c), jnp.float32),
        in_specs=[smem, smem, vmem],
        out_specs=vmem,
        scratch_shapes=[
            pltpu.VMEM((2 * tile_r + width + SUBLANES, 2 * tile_c + width), jnp.float32)
        ],
        compiler_params=pltpu.CompilerParams(vmem_limit_bytes=VMEM_LIMIT),
        cost_estimate=pl.CostEstimate(flops=4000000, bytes_accessed=800000, transcendentals=0),
    )(offsets, counts, probe)


def update_kernel(
    offsets, counts, probe, magnitudes, table, table_t, own, rim, near, near_rim, far, far_rim,
    terms, total, above, center, below, ext, patches, left, right,
):
    slots, width = magnitudes.shape[0], magnitudes.shape[1]
    half = width // 2
    tile_r, tile_c = own.shape[1:]
    row_place = lax.axis_index("row")
    col_place = lax.axis_index("col")
    row_odd = lax.rem(row_place, 2)
    col_odd = lax.rem(col_place, 2)
    near_row = pl.multiple_of((1 - row_odd) * (tile_r + half), half)
    far_row = pl.multiple_of(row_odd * (tile_r + half), half)
    pair_col = pl.multiple_of((1 - col_odd) * (tile_c + half), half)
    other_col = pl.multiple_of(col_odd * (tile_c + half), half)
    for part in range(2):
        for rows, mid, edge in ((half, own, rim), (near_row, near, near_rim), (far_row, far, far_rim)):
            at = pl.ds(rows, tile_r)
            ext[part, at, half : half + tile_c] = mid[part]
            ext[part, at, pl.ds(pair_col, half)] = edge[0, part]
            ext[part, at, pl.ds(other_col, half)] = edge[1, part]
    wide = width + LANES
    live_count = counts[row_place, col_place]
    places = []
    for slot in range(slots):
        row, row_shift = split_start(
            offsets[row_place, col_place, slot, 0] + half, SUBLANES, tile_r
        )
        lane, lane_shift = split_start(
            offsets[row_place, col_place, slot, 1] + half, LANES, 2 * half - LANES
        )
        block = (pl.ds(row, width + SUBLANES), pl.ds(lane, wide))
        places.append((block, row_shift, lane_shift))
        for part in range(2):
            patches[slot, part] = cut(ext[part, *block], row_shift, lane_shift)
    probe_real, probe_imag = probe[0], probe[1]
    for slot in range(slots):
        patch_real, patch_imag = patches[slot, 0], patches[slot, 1]
        at = slice(slot * width, (slot + 1) * width)
        for part, wave in enumerate(
            (
                probe_real * patch_real - probe_imag * patch_imag,
                probe_real * patch_imag + probe_imag * patch_real,
            )
        ):
            left[0, at, part * width : (part + 1) * width], left[1, at, part * width : (part + 1) * width] = halves(wave)
    inner = product((left[0], left[1]), (table[0], table[1]))
    for slot in range(slots):
        here = inner[slot * width : (slot + 1) * width]
        for part in range(2):
            at = slice(part * width, (part + 1) * width)
            right[0, at, :], right[1, at, :] = halves(here[:, at])
        far_field = product((table_t[0], table_t[1]), (right[0], right[1]))
        far_real, far_imag = far_field[:width], far_field[width:]
        inverse = jnp.minimum(
            lax.rsqrt(far_real * far_real + far_imag * far_imag), 1.0 / modulus_floor
        )
        factor = magnitudes[slot] * inverse - 1.0
        at = slice(slot * width, (slot + 1) * width)
        left[0, at, :width], left[1, at, :width] = halves(far_real * factor)
        left[0, at, width:], left[1, at, width:] = halves(far_imag * factor)
    inner = product((left[0], left[1]), (table_t[0], table_t[1]))
    ext[...] = jnp.zeros_like(ext)
    sums = [jnp.zeros((width, width), jnp.float32)] * 3
    for slot in range(slots):
        here = inner[slot * width : (slot + 1) * width]
        for part in range(2):
            at = slice(part * width, (part + 1) * width)
            right[0, at, :], right[1, at, :] = halves(here[:, at])
        live = jnp.where(slot < live_count, 1.0, 0.0)
        delta = product((table[0], table[1]), (right[0], right[1])) * live
        real, imag = delta[:width], delta[width:]
        patch_real, patch_imag = patches[slot, 0], patches[slot, 1]
        sums = [
            sums[0] + (patch_real * real + patch_imag * imag),
            sums[1] + (patch_real * imag - patch_imag * real),
            sums[2] + live * (patch_real * patch_real + patch_imag * patch_imag),
        ]
        block, row_shift, lane_shift = places[slot]
        for part, grad in enumerate(
            (probe_real * real + probe_imag * imag, probe_real * imag - probe_imag * real)
        ):
            ext[part, *block] += spread(grad, row_shift, lane_shift)
    for layer in range(3):
        for side in range(width // LANES):
            terms[side, layer] = sums[layer][:, side * LANES : (side + 1) * LANES]
    total[...] = jnp.full(total.shape, jnp.sum(sums[2]))
    above[...] = ext[:, :half, :]
    center[...] = ext[:, half : half + tile_r, :]
    below[...] = ext[:, half + tile_r : 2 * half + tile_r, :]


def update(offsets, counts, probe, magnitudes, own, rim, near, near_rim, far, far_rim):
    slots, width = magnitudes.shape[:2]
    half = width // 2
    tile_r, tile_c = own.shape[1:]
    table, table_t = dft_tables(width)
    smem = pl.BlockSpec(memory_space=pltpu.SMEM)
    vmem = pl.BlockSpec(memory_space=pltpu.VMEM)
    strip = jax.ShapeDtypeStruct((2, tile_r, tile_c + 2 * half), jnp.float32)
    return pl.pallas_call(
        update_kernel,
        out_shape=[
            jax.ShapeDtypeStruct((width // LANES, 3, width, LANES), jnp.float32),
            jax.ShapeDtypeStruct((8, LANES), jnp.float32),
            strip,
            strip,
            strip,
        ],
        in_specs=[smem, smem] + [vmem] * 10,
        out_specs=[vmem] * 5,
        scratch_shapes=[
            pltpu.VMEM((2, tile_r + 2 * half + SUBLANES, tile_c + 2 * half), jnp.float32),
            pltpu.VMEM((slots, 2, width, width), jnp.float32),
            pltpu.VMEM((2, slots * width, 2 * width), jnp.bfloat16),
            pltpu.VMEM((2, 2 * width, width), jnp.bfloat16),
        ],
        compiler_params=pltpu.CompilerParams(vmem_limit_bytes=VMEM_LIMIT),
        cost_estimate=pl.CostEstimate(
            flops=3200000000, bytes_accessed=8000000, transcendentals=131072
        ),
    )(offsets, counts, probe, magnitudes, table, table_t, own, rim, near, near_rim, far, far_rim)


def exchange(value, axis, count, bit):
    return lax.ppermute(value, axis, [(i, i ^ bit) for i in range(count)])


def shards(specimen, probe_field, scan_offsets, live_counts, magnitudes):
    rows, cols = lax.axis_size("row"), lax.axis_size("col")
    width = probe_field.shape[1]
    half = width // 2
    tile_r, tile_c = specimen.shape[1:]
    row_place = lax.axis_index("row")
    col_place = lax.axis_index("col")
    row_odd = row_place % 2
    col_odd = col_place % 2
    pairs = [(i, i ^ 1) for i in range(cols)]
    others = [(i, i + 1) for i in range(1, cols - 1, 2)] + [(i + 1, i) for i in range(1, cols - 1, 2)]
    toward = [(i, i + 2) for i in range(1, rows - 2, 2)] + [(i, i - 2) for i in range(2, rows, 2)]
    onward = [(i, i + 2) for i in range(0, rows - 2, 2)] + [(i, i - 2) for i in range(3, rows, 2)]

    low, high = specimen[:, :, :half], specimen[:, :, tile_c - half :]
    pair_rim = lax.ppermute(jnp.where(col_odd == 0, high, low), "col", pairs)
    other_rim = lax.ppermute(jnp.where(col_odd == 0, low, high), "col", others)
    beyond = lax.ppermute(specimen, "row", toward)
    rim = jnp.stack([pair_rim, other_rim])
    beyond_rim = lax.ppermute(rim, "row", toward)
    near = exchange(specimen, "row", rows, 1)
    near_rim = exchange(rim, "row", rows, 1)
    far = exchange(beyond, "row", rows, 1)
    far_rim = exchange(beyond_rim, "row", rows, 1)

    light = lighting(scan_offsets, live_counts, probe_field, tile_r, tile_c)
    terms, total, above, center, below = update(
        scan_offsets, live_counts, probe_field, magnitudes[0, 0],
        specimen, rim, near, near_rim, far, far_rim,
    )

    got_above = exchange(above, "row", rows, 1)
    got_below = exchange(below, "row", rows, 1)
    forward = jnp.where(row_odd == 0, got_below, got_above)
    beyond = lax.ppermute(forward, "row", onward)
    summed = center + jnp.where(row_odd == 0, got_above, got_below) + beyond
    low, high = summed[:, :, :half], summed[:, :, tile_c + half :]
    pair_part = lax.ppermute(jnp.where(col_odd == 0, high, low), "col", pairs)
    other_part = lax.ppermute(jnp.where(col_odd == 0, low, high), "col", others)
    low_part = jnp.where(col_odd == 0, other_part, pair_part)
    high_part = jnp.where(col_odd == 0, pair_part, other_part)
    middle = summed[:, :, half : half + tile_c]
    middle = middle + jnp.concatenate([low_part, high_part], 2)
    specimen_next = specimen + middle / light

    def send(value, total, axis, pairs_here):
        size = value.shape[0] * value.shape[1]
        flat = jnp.concatenate([value.reshape(size, LANES), total])
        got = lax.ppermute(flat, axis, pairs_here)
        return got[:size].reshape(value.shape), total + got[size:]

    def pick(condition, first, second):
        return jnp.where(condition, first, second)

    steps = [("row", rows, 2), ("col", cols, 1)]
    mine = pick(row_odd == 0, terms[0], terms[1])
    given = pick(row_odd == 0, terms[1], terms[0])
    got, total = send(given, total, "row", [(i, i ^ 1) for i in range(rows)])
    value = mine + got
    for axis, count, bit in steps:
        place = (lax.axis_index(axis) // bit) % 2
        size = value.shape[1] // 2
        first, second = value[:, :size], value[:, size:]
        got, total = send(
            pick(place == 0, second, first), total, axis, [(i, i ^ bit) for i in range(count)]
        )
        value = pick(place == 0, first, second) + got
    for bit in (1 << k for k in range(2, rows.bit_length() - 1)):
        got, total = send(value, total, "row", [(i, i ^ bit) for i in range(rows)])
        value = value + got
    line = cols // 2
    chain = line == 4
    if chain:
        around = [(i, i ^ 2) for i in range(cols)]
        got, total = send(value, total, "col", around)
        value = value + got
        across = [(i, (i ^ 6)) for i in range(cols) if (i // 2) in (1, 2)]
        got, total = send(value, total, "col", across)
        value = value + got
    else:
        for bit in (1 << k for k in range(1, cols.bit_length() - 1)):
            got, total = send(value, total, "col", [(i, i ^ bit) for i in range(cols)])
            value = value + got
    size = value.shape[1]
    first_row = (
        ((row_place // 2) % 2) * (width // 2) + col_odd * (width // 4)
    )
    mean = total[0, 0] / (width * width)
    sides = probe_field.reshape(2, width, width // LANES, LANES)
    own_probe = pick(row_odd == 0, sides[:, :, 0], sides[:, :, 1])
    own_probe = lax.dynamic_slice(own_probe, (0, first_row, 0), (2, size, LANES))
    fresh = own_probe + value[:2] / (value[2] + probe_damping * mean)
    if chain:
        inner = ((col_place // 2) == 1) | ((col_place // 2) == 2)
        outward = [(i, i ^ 2) for i in range(cols) if (i // 2) in (1, 2)]
        got = lax.ppermute(fresh, "col", outward)
        fresh = pick(inner, fresh, got)
    for axis, count, bit in reversed(steps):
        place = (lax.axis_index(axis) // bit) % 2
        got = exchange(fresh, axis, count, bit)
        fresh = pick(
            place == 0, jnp.concatenate([fresh, got], 1), jnp.concatenate([got, fresh], 1)
        )
    got = exchange(fresh, "row", rows, 1)
    probe_next = pick(
        row_odd == 0, jnp.concatenate([fresh, got], 2), jnp.concatenate([got, fresh], 2)
    )
    return (specimen_next, probe_next)


def solution(mesh):
    return jax.shard_map(
        shards,
        mesh=mesh,
        in_specs=(P(None, "row", "col"), P(), P(), P(), P("row", "col", None, None, None)),
        out_specs=(P(None, "row", "col"), P()),
        check_vma=False,
    )
```

time: 300 us -> 87.9 us (0.29)
  waiting for transfers between devices: 158 us -> 32.2 us
  matrix products: 32.5 us -> 0 us
  local copies, waits for them, and re-layouts: 42.2 us -> 12.7 us
  between operations: 15.8 us -> 1.69 us
  Pallas kernels: 0 us -> 8.21 us
  other arithmetic: 15.7 us -> 7.82 us
  loops' own time: 7.67 us -> 0 us
    psum x1 -> x0, waiting for transfers between devices: 147 us -> none  [shards(): lax.psum((local_terms[0], local_terms[1], local_terms[2]), ('row', 'col'))]
    dot_general x16 -> x0, matrix products: 32.5 us -> none  [the longest x8 18.2 us: matmul_left(): jnp.einsum('kj,sjl->skl', table, right, precision=lax.Precision.HIGHEST)]
    dynamic_update_slice x2 -> x0, local copies, waits for them, and re-layouts: 23.6 us -> none  [place(): return lax.dynamic_update_slice(total, current + pieces[slot], start)]
    ppermute x8 -> x22, waiting for transfers between devices: 11.2 us -> 32.2 us  [the longest x5 12.3 us: send(): got = lax.ppermute(flat, axis, pairs_here)]
    pallas_call x0 -> x2, Pallas kernels: none -> 8.21 us  [the longest x1 6.17 us: update(): pl.pallas_call(update_kernel, out_shape=[jax.ShapeDtypeStruct((width // L...]
    another operation x2 -> x0, loops' own time: 7.67 us -> none  [the longest x1 7.65 us: shards(): buffer = lax.fori_loop(0, slots, place, start_total)]
    gather x6 -> x0, local copies, waits for them, and re-layouts: 5.81 us -> none
    unnamed x25 -> x29, local copies, waits for them, and re-layouts: 4.82 us -> 9.71 us
  transfers between devices with their start and end apart: 9 -> 22, of which waited for: 6 -> 10; matrix products, arithmetic and copies ran while one was open for 3% -> 7% of each run, Pallas kernels for 0% -> 2%
where the time goes in v1:
time: 87.9 us; the launch traced here: 87.1 us
  waiting for transfers between devices  32.2 us (37%)
  starting transfers between devices  24.5 us (28%)
  local copies, waits for them, and re-layouts  12.7 us (14%)
  Pallas kernels  8.21 us (9%)
  other arithmetic  7.82 us (9%)
  between operations  1.69 us (2%)
    ppermute x5, waiting for transfers between devices, send(): got = lax.ppermute(flat, axis, pairs_here)  12.3 us
    unnamed x29, local copies, waits for them, and re-layouts  9.71 us
    ppermute x5, starting transfers between devices, send(): got = lax.ppermute(flat, axis, pairs_here)  9.17 us
    ppermute x1, waiting for transfers between devices, shards(): got = lax.ppermute(fresh, 'col', outward)  7.09 us
    pallas_call x1, Pallas kernels, update(): pl.pallas_call(update_kernel, out_shape=[jax.ShapeDtypeStruct((width // L...  6.17 us
    ppermute x9, waiting for transfers between devices, exchange(): return lax.ppermute(value, axis, [(i, i ^ bit) for i in range(count)])  3.78 us
    ppermute x1, starting transfers between devices, shards(): pair_rim = lax.ppermute(jnp.where(col_odd == 0, high, low), 'col', pairs)  3.03 us
    ppermute x1, waiting for transfers between devices, shards(): beyond = lax.ppermute(specimen, 'row', toward)  2.95 us
  transfers between devices with their start and end apart: 22, of which 10 were waited for; matrix products, arithmetic and copies ran while one was open for 7% of the time, Pallas kernels for 2%

profile of v1, /device:TPU:0, one launch (start us, length us, event | category | flops | bytes accessed | tf_op | source)
XLA Modules:
  0.0 87.1 jit_solution(12221967071775271355)
XLA Ops:
  0.7 1.1 %slice_select_fusion.5 = (f32[2,128,128]{2,1,0:T(8,128)S(1)}, f32[2,128,128]{2,1,0:T(8,128)S(1)}) fusion(f32[2,128,256]{2,1,0:T(8,128)} %own.1, pred[]{:T(512)S(6)} %eq.18), kind=kLoop, calls=%fused_computation.18 | loop fusion | flops 65536 | bytes 524289 | tf_op jit(solution)/shard_map/jit(_where)/select_n | solution.py:292
  1.7 3.0 %collective-permute-start = (f32[2,128,128]{2,1,0:T(8,128)S(1)}, f32[2,128,128]{2,1,0:T(8,128)S(1)}, u32[]{:S(2)}, u32[]{:S(2)}) collective-permute-start(f32[2,128,128]{2,1,0:T(8,128)S(1)} %get-tuple-element.18), channel_id=1, source_target_pairs={{0,1},{1,0},{2,3},{3,2},{4,5},{5,4},{6,7},{7,6},{8,9},{9,8},{10,11... | collective-permute-start | bytes 393224 | tf_op jit(solution)/shard_map/ppermute | solution.py:292
  4.8 0.7 collective-permute-start.1
  5.4 1.3 %collective-permute-start.4 = (f32[2,128,256]{2,1,0:T(8,128)S(1)}, f32[2,128,256]{2,1,0:T(8,128)S(1)}, u32[]{:S(2)}, u32[]{:S(2)}) collective-permute-start(f32[2,128,256]{2,1,0:T(8,128)S(1)} %copy-done.1), channel_id=1, source_target_pairs={{8,24},{16,0},{9,25},{17,1},{10,26},{18,2},{11,27},{19,3},{12,28},... | collective-permute-start | bytes 786440 | tf_op jit(solution)/shard_map/ppermute | solution.py:294
  6.7 1.5 %collective-permute-done = f32[2,128,128]{2,1,0:T(8,128)S(1)} collective-permute-done((f32[2,128,128]{2,1,0:T(8,128)S(1)}, f32[2,128,128]{2,1,0:T(8,128)S(1)}, u32[]{:S(2)}, u32[]{:S(2)}) %collective-permute-start) | collective-permute-done | bytes 131104 | tf_op jit(solution)/shard_map/ppermute | solution.py:292
  8.3 1.3 %collective-permute-start.6 = (f32[2,2,128,128]{3,2,1,0:T(8,128)S(1)}, f32[2,2,128,128]{3,2,1,0:T(8,128)S(1)}, u32[]{:S(2)}, u32[]{:S(2)}) collective-permute-start(f32[2,2,128,128]{3,2,1,0:T(8,128)S(1)} %pad_maximum_fusion.1.rim), channel_id=1, source_target_pairs={{8,24},{16,0},{9,25},{17,1},{10,26},{18,2},{11,27},{19,3},{12,28},... | collective-permute-start | bytes 786440 | tf_op jit(solution)/shard_map/ppermute | solution.py:296
  9.6 1.1 %collective-permute-start.2 = (f32[2,128,256]{2,1,0:T(8,128)S(1)}, f32[2,128,256]{2,1,0:T(8,128)S(1)}, u32[]{:S(2)}, u32[]{:S(2)}) collective-permute-start(f32[2,128,256]{2,1,0:T(8,128)S(1)} %copy-done.1), channel_id=1, source_target_pairs={{0,8},{8,0},{16,24},{24,16},{1,9},{9,1},{17,25},{25,17},{2,10},{10... | collective-permute-start | bytes 786440 | tf_op jit(solution)/shard_map/ppermute | solution.py:274
  10.7 3.0 %collective-permute-done.4 = f32[2,128,256]{2,1,0:T(8,128)S(1)} collective-permute-done((f32[2,128,256]{2,1,0:T(8,128)S(1)}, f32[2,128,256]{2,1,0:T(8,128)S(1)}, u32[]{:S(2)}, u32[]{:S(2)}) %collective-permute-start.4) | collective-permute-done | bytes 262176 | tf_op jit(solution)/shard_map/ppermute | solution.py:294
  13.7 2.8 %collective-permute-done.6 = f32[2,2,128,128]{3,2,1,0:T(8,128)S(1)} collective-permute-done((f32[2,2,128,128]{3,2,1,0:T(8,128)S(1)}, f32[2,2,128,128]{3,2,1,0:T(8,128)S(1)}, u32[]{:S(2)}, u32[]{:S(2)}) %collective-permute-start.6) | collective-permute-done | bytes 262176 | tf_op jit(solution)/shard_map/ppermute | solution.py:296
  16.6 0.7 copy-done.13
  17.4 0.7 copy-done.4
  18.1 0.7 copy-done.6
  18.8 0.7 copy-done.8
  19.5 0.7 copy-done.10
  20.2 1.0 %copy-done.3 = f32[1,1,2,256,256]{4,3,2,1,0:T(8,128)S(1)} copy-done((f32[1,1,2,256,256]{4,3,2,1,0:T(8,128)S(1)}, f32[1,1,2,256,256]{4,3,2,1,0:T(8,128)}, u32[]{:S(2)}) %copy-start.3) | copy-done | bytes 524312
  21.3 0.9 %copy-done.5 = f32[2,128,256]{2,1,0:T(8,128)S(1)} copy-done((f32[2,128,256]{2,1,0:T(8,128)S(1)}, f32[2,128,256]{2,1,0:T(8,128)}, u32[]{:S(2)}) %copy-start.5) | copy-done | bytes 262168
  22.2 0.9 %copy-done.7 = f32[2,2,128,128]{3,2,1,0:T(8,128)S(1)} copy-done((f32[2,2,128,128]{3,2,1,0:T(8,128)S(1)}, f32[2,2,128,128]{3,2,1,0:T(8,128)}, u32[]{:S(2)}) %copy-start.7) | copy-done | bytes 262168
  23.2 0.9 %copy-done.9 = f32[2,128,256]{2,1,0:T(8,128)S(1)} copy-done((f32[2,128,256]{2,1,0:T(8,128)S(1)}, f32[2,128,256]{2,1,0:T(8,128)}, u32[]{:S(2)}) %copy-start.9) | copy-done | bytes 262168
  24.1 0.9 %copy-done.11 = f32[2,2,128,128]{3,2,1,0:T(8,128)S(1)} copy-done((f32[2,2,128,128]{3,2,1,0:T(8,128)S(1)}, f32[2,2,128,128]{3,2,1,0:T(8,128)}, u32[]{:S(2)}) %copy-start.11) | copy-done | bytes 262168
  25.1 1.2 %copy-done.12 = bf16[2,512,512]{2,1,0:T(8,128)(2,1)S(1)} copy-done((bf16[2,512,512]{2,1,0:T(8,128)(2,1)S(1)}, bf16[2,512,512]{2,1,0:T(8,128)(2,1)}, u32[]{:S(2)}) %copy-start.12) | copy-done | bytes 1048600
  26.3 6.2 %shard_map.86 = (f32[2,3,256,128]{3,2,1,0:T(8,128)S(1)}, f32[8,128]{1,0:T(8,128)S(1)}, f32[2,128,512]{2,1,0:T(8,128)S(1)}, f32[2,128,512]{2,1,0:T(8,128)S(1)}, f32[2,128,512]{2,1,0:T(8,128)S(1)}) custom-call(s32[4,8,2,2]{3,2,1,0:T(2,128)S(1)} %copy.9.offsets, s32[4,8]{1,0:T(4,128)S(1)} %copy-done.2, f32[2,256,256]{2,1,0:T(8,128)S(1)} %copy-done, ...), custom_call_target="tpu_custom_call" | custom-call | flops 3200000000 | bytes 8000000 | tf_op jit(solution)/shard_map/pallas_call | solution.py:249
  32.5 0.8 pad_maximum_fusion
  33.7 1.7 %collective-permute-done.13 = f32[776,128]{1,0:T(8,128)} collective-permute-done((f32[776,128]{1,0:T(8,128)}, f32[776,128]{1,0:T(8,128)}, u32[]{:S(2)}, u32[]{:S(2)}) %collective-permute-start.13) | collective-permute-done | bytes 397344 | tf_op jit(solution)/shard_map/ppermute | solution.py:325
  35.4 1.0 %slice.111 = f32[768,128]{1,0:T(8,128)S(1)} slice(f32[776,128]{1,0:T(8,128)} %collective-permute-done.13), slice={[0:768], [0:128]} | slice | bytes 786432 | tf_op jit(solution)/shard_map/slice | solution.py:326
  36.6 0.7 slice_add_fusion.6
  37.4 7.3 %collective-permute-done.14 = f32[392,128]{1,0:T(8,128)S(1)} collective-permute-done((f32[392,128]{1,0:T(8,128)S(1)}, f32[392,128]{1,0:T(8,128)S(1)}, u32[]{:S(2)}, u32[]{:S(2)}) %collective-permute-start.14) | collective-permute-done | bytes 200736 | tf_op jit(solution)/shard_map/ppermute | solution.py:325
  44.7 4.8 %collective-permute-start.15 = (f32[200,128]{1,0:T(8,128)S(1)}, f32[200,128]{1,0:T(8,128)S(1)}, u32[]{:S(2)}, u32[]{:S(2)}) collective-permute-start(f32[200,128]{1,0:T(8,128)S(1)} %pad_maximum_fusion.3), channel_id=1, source_target_pairs={{0,1},{1,0},{2,3},{3,2},{4,5},{5,4},{6,7},{7,6},{8,9},{9,8},{10,11... | collective-permute-start | bytes 307208 | tf_op jit(solution)/shard_map/ppermute | solution.py:325
  49.9 0.5 collective-permute-start.9
  50.4 1.8 %collective-permute-done.15 = f32[200,128]{1,0:T(8,128)S(1)} collective-permute-done((f32[200,128]{1,0:T(8,128)S(1)}, f32[200,128]{1,0:T(8,128)S(1)}, u32[]{:S(2)}, u32[]{:S(2)}) %collective-permute-start.15) | collective-permute-done | bytes 102432 | tf_op jit(solution)/shard_map/ppermute | solution.py:325
  52.2 3.2 %collective-permute-start.16 = (f32[200,128]{1,0:T(8,128)S(1)}, f32[200,128]{1,0:T(8,128)S(1)}, u32[]{:S(2)}, u32[]{:S(2)}) collective-permute-start(f32[200,128]{1,0:T(8,128)S(1)} %pad_maximum_fusion.4), channel_id=1, source_target_pairs={{0,2},{1,3},{2,0},{3,1},{4,6},{5,7},{6,4},{7,5},{8,10},{9,11},{10,... | collective-permute-start | bytes 307208 | tf_op jit(solution)/shard_map/ppermute | solution.py:325
  55.4 1.1 %fusion.5 = (f32[2,256,1,128]{3,2,1,0:T(1,128)S(1)}, f32[2,256,1,128]{3,2,1,0:T(1,128)}) fusion(f32[2,256,2,128]{3,2,1,0:T(2,128)S(1)} %reshape.47), kind=kLoop, calls=%fused_computation.38 | loop fusion | bytes 1048576 | tf_op jit(solution)/shard_map/slice | solution.py:366
  56.5 1.5 %collective-permute-done.16 = f32[200,128]{1,0:T(8,128)S(1)} collective-permute-done((f32[200,128]{1,0:T(8,128)S(1)}, f32[200,128]{1,0:T(8,128)S(1)}, u32[]{:S(2)}, u32[]{:S(2)}) %collective-permute-start.16) | collective-permute-done | bytes 102432 | tf_op jit(solution)/shard_map/ppermute | solution.py:325
  58.1 0.7 collective-permute-start.17
  58.8 1.1 %broadcast_select_fusion = f32[2,128,512]{2,1,0:T(8,128)S(1)} fusion(f32[2,128,512]{2,1,0:T(8,128)} %collective-permute-done.9, f32[2,128,512]{2,1,0:T(8,128)} %collective-permute-done.8, pred[]{:T(512)S(6)} %eq.19), kind=kLoop, calls=%fused_computation.10 | loop fusion | flops 131072 | bytes 1572865 | tf_op jit(solution)/shard_map/jit(_where)/select_n | solution.py:310
  60.0 2.2 %collective-permute-start.10 = (f32[2,128,512]{2,1,0:T(8,128)S(1)}, f32[2,128,512]{2,1,0:T(8,128)S(1)}, u32[]{:S(2)}, u32[]{:S(2)}) collective-permute-start(f32[2,128,512]{2,1,0:T(8,128)S(1)} %broadcast_select_fusion), channel_id=1, source_target_pairs={{0,16},{24,8},{1,17},{25,9},{2,18},{26,10},{3,19},{27,11},{4,20},{... | collective-permute-start | bytes 1572872 | tf_op jit(solution)/shard_map/ppermute | solution.py:311
  62.2 0.5 slice.105
  63.4 0.9 fusion.2
  64.3 1.3 %collective-permute-start.18 = (f32[2,64,128]{2,1,0:T(8,128)S(1)}, f32[2,64,128]{2,1,0:T(8,128)S(1)}, u32[]{:S(2)}, u32[]{:S(2)}) collective-permute-start(f32[2,64,128]{2,1,0:T(8,128)S(1)} %fusion.2), channel_id=1, source_target_pairs={{2,0},{3,1},{4,6},{5,7},{10,8},{11,9},{12,14},{13,15},{18,16},{19,... | collective-permute-start | bytes 196616 | tf_op jit(solution)/shard_map/ppermute | solution.py:372
  65.6 7.1 %collective-permute-done.18 = f32[2,64,128]{2,1,0:T(8,128)S(1)} collective-permute-done((f32[2,64,128]{2,1,0:T(8,128)S(1)}, f32[2,64,128]{2,1,0:T(8,128)S(1)}, u32[]{:S(2)}, u32[]{:S(2)}) %collective-permute-start.18) | collective-permute-done | bytes 65568 | tf_op jit(solution)/shard_map/ppermute | solution.py:372
  72.7 0.6 collective-permute-start.19
  73.3 3.8 %collective-permute-done.19 = f32[2,64,128]{2,1,0:T(8,128)S(1)} collective-permute-done((f32[2,64,128]{2,1,0:T(8,128)S(1)}, f32[2,64,128]{2,1,0:T(8,128)S(1)}, u32[]{:S(2)}, u32[]{:S(2)}) %collective-permute-start.19) | collective-permute-done | bytes 65568 | tf_op jit(solution)/shard_map/ppermute | solution.py:274
  77.1 1.3 %add_add_fusion = f32[2,128,512]{2,1,0:T(8,128)S(1)} fusion(f32[2,128,512]{2,1,0:T(8,128)S(1)} %collective-permute-done.10, f32[2,128,512]{2,1,0:T(8,128)S(1)} %get-tuple-element.7, f32[2,128,512]{2,1,0:T(8,128)} %collective-permute-done.8, f32[2,128,512]{2,1,0:T(8,128)} %collective-permute-done.9, pred[]{:T(512)S(6)} %eq.19), kind=kLoop, calls=%fused_computation.1 | loop fusion | flops 393216 | bytes 2621441 | tf_op jit(solution)/shard_map/add | solution.py:312
  78.4 0.7 collective-permute-start.11
  79.1 2.4 %collective-permute-start.12 = (f32[2,128,128]{2,1,0:T(8,128)S(1)}, f32[2,128,128]{2,1,0:T(8,128)S(1)}, u32[]{:S(2)}, u32[]{:S(2)}) collective-permute-start(f32[2,128,128]{2,1,0:T(8,128)S(1)} %get-tuple-element.15), channel_id=1, source_target_pairs={{0,1},{1,0},{2,3},{3,2},{4,5},{5,4},{6,7},{7,6},{8,9},{9,8},{10,11... | collective-permute-start | bytes 393224 | tf_op jit(solution)/shard_map/ppermute | solution.py:314
  81.6 2.0 %shard_map.87 = f32[128,256]{1,0:T(8,128)S(1)} custom-call(s32[4,8,2,2]{3,2,1,0:T(2,128)S(1)} %copy.9.offsets, s32[4,8]{1,0:T(4,128)S(1)} %copy-done.2, f32[2,256,256]{2,1,0:T(8,128)S(1)} %copy-done), custom_call_target="tpu_custom_call" | custom-call | flops 4000000 | bytes 800000 | tf_op jit(solution)/shard_map/pallas_call | solution.py:136
  83.7 1.7 %collective-permute-done.12 = f32[2,128,128]{2,1,0:T(8,128)S(1)} collective-permute-done((f32[2,128,128]{2,1,0:T(8,128)S(1)}, f32[2,128,128]{2,1,0:T(8,128)S(1)}, u32[]{:S(2)}, u32[]{:S(2)}) %collective-permute-start.12) | collective-permute-done | bytes 131104 | tf_op jit(solution)/shard_map/ppermute | solution.py:314
  85.5 0.8 fusion.1
  86.2 0.8 maximum_select_fusion
  (66 shorter events, 1.7 us)
Async XLA Ops:
  0.6 4.8 %copy-start.1 = (f32[2,128,256]{2,1,0:T(8,128)S(1)}, f32[2,128,256]{2,1,0:T(8,128)}, u32[]{:S(2)}) copy-start(f32[2,128,256]{2,1,0:T(8,128)} %own.1) | copy-start | bytes 786436
  0.7 19.6 %copy-start = (f32[2,256,256]{2,1,0:T(8,128)S(1)}, f32[2,256,256]{2,1,0:T(8,128)}, u32[]{:S(2)}) copy-start(f32[2,256,256]{2,1,0:T(8,128)} %probe.3) | copy-start | bytes 1572868
  1.7 6.5 %collective-permute-start = (f32[2,128,128]{2,1,0:T(8,128)S(1)}, f32[2,128,128]{2,1,0:T(8,128)S(1)}, u32[]{:S(2)}, u32[]{:S(2)}) collective-permute-start(f32[2,128,128]{2,1,0:T(8,128)S(1)} %get-tuple-element.18), channel_id=1, source_target_pairs={{0,1},{1,0},{2,3},{3,2},{4,5},{5,4},{6,7},{7,6},{8,9},{9,8},{10,11... | collective-permute-start | bytes 393224 | tf_op jit(solution)/shard_map/ppermute | solution.py:292
  4.8 3.5 %collective-permute-start.1 = (f32[2,128,128]{2,1,0:T(8,128)S(1)}, f32[2,128,128]{2,1,0:T(8,128)S(1)}, u32[]{:S(2)}, u32[]{:S(2)}) collective-permute-start(f32[2,128,128]{2,1,0:T(8,128)S(1)} %get-tuple-element.19), channel_id=1, source_target_pairs={{1,2},{3,4},{5,6},{2,1},{4,3},{6,5},{9,10},{11,12},{13,14},{10,9},... | collective-permute-start | bytes 393224 | tf_op jit(solution)/shard_map/ppermute | solution.py:293
  5.4 8.3 %collective-permute-start.4 = (f32[2,128,256]{2,1,0:T(8,128)S(1)}, f32[2,128,256]{2,1,0:T(8,128)S(1)}, u32[]{:S(2)}, u32[]{:S(2)}) collective-permute-start(f32[2,128,256]{2,1,0:T(8,128)S(1)} %copy-done.1), channel_id=1, source_target_pairs={{8,24},{16,0},{9,25},{17,1},{10,26},{18,2},{11,27},{19,3},{12,28},... | collective-permute-start | bytes 786440 | tf_op jit(solution)/shard_map/ppermute | solution.py:294
  8.3 8.3 %collective-permute-start.6 = (f32[2,2,128,128]{3,2,1,0:T(8,128)S(1)}, f32[2,2,128,128]{3,2,1,0:T(8,128)S(1)}, u32[]{:S(2)}, u32[]{:S(2)}) collective-permute-start(f32[2,2,128,128]{3,2,1,0:T(8,128)S(1)} %pad_maximum_fusion.1.rim), channel_id=1, source_target_pairs={{8,24},{16,0},{9,25},{17,1},{10,26},{18,2},{11,27},{19,3},{12,28},... | collective-permute-start | bytes 786440 | tf_op jit(solution)/shard_map/ppermute | solution.py:296
  9.6 7.8 %collective-permute-start.2 = (f32[2,128,256]{2,1,0:T(8,128)S(1)}, f32[2,128,256]{2,1,0:T(8,128)S(1)}, u32[]{:S(2)}, u32[]{:S(2)}) collective-permute-start(f32[2,128,256]{2,1,0:T(8,128)S(1)} %copy-done.1), channel_id=1, source_target_pairs={{0,8},{8,0},{16,24},{24,16},{1,9},{9,1},{17,25},{25,17},{2,10},{10... | collective-permute-start | bytes 786440 | tf_op jit(solution)/shard_map/ppermute | solution.py:274
  10.7 7.4 %collective-permute-start.3 = (f32[2,2,128,128]{3,2,1,0:T(8,128)S(1)}, f32[2,2,128,128]{3,2,1,0:T(8,128)S(1)}, u32[]{:S(2)}, u32[]{:S(2)}) collective-permute-start(f32[2,2,128,128]{3,2,1,0:T(8,128)S(1)} %pad_maximum_fusion.1.rim), channel_id=1, source_target_pairs={{0,8},{8,0},{16,24},{24,16},{1,9},{9,1},{17,25},{25,17},{2,10},{10... | collective-permute-start | bytes 786440 | tf_op jit(solution)/shard_map/ppermute | solution.py:274
  13.7 5.1 %collective-permute-start.5 = (f32[2,128,256]{2,1,0:T(8,128)S(1)}, f32[2,128,256]{2,1,0:T(8,128)S(1)}, u32[]{:S(2)}, u32[]{:S(2)}) collective-permute-start(f32[2,128,256]{2,1,0:T(8,128)S(1)} %collective-permute-done.4), channel_id=1, source_target_pairs={{0,8},{8,0},{16,24},{24,16},{1,9},{9,1},{17,25},{25,17},{2,10},{10... | collective-permute-start | bytes 786440 | tf_op jit(solution)/shard_map/ppermute | solution.py:274
  16.5 3.0 %collective-permute-start.7 = (f32[2,2,128,128]{3,2,1,0:T(8,128)S(1)}, f32[2,2,128,128]{3,2,1,0:T(8,128)S(1)}, u32[]{:S(2)}, u32[]{:S(2)}) collective-permute-start(f32[2,2,128,128]{3,2,1,0:T(8,128)S(1)} %collective-permute-done.6), channel_id=1, source_target_pairs={{0,8},{8,0},{16,24},{24,16},{1,9},{9,1},{17,25},{25,17},{2,10},{10... | collective-permute-start | bytes 786440 | tf_op jit(solution)/shard_map/ppermute | solution.py:274
  16.6 0.7 copy-start.13
  17.4 2.8 %copy-start.2 = (s32[4,8]{1,0:T(4,128)S(1)}, s32[4,8]{1,0:T(4,128)}, u32[]{:S(2)}) copy-start(s32[4,8]{1,0:T(4,128)} %counts.3) | copy-start | bytes 388
  17.4 0.7 copy-start.4
  18.1 0.7 copy-start.6
  18.8 0.7 copy-start.8
  19.5 0.7 copy-start.10
  20.2 1.0 %copy-start.3 = (f32[1,1,2,256,256]{4,3,2,1,0:T(8,128)S(1)}, f32[1,1,2,256,256]{4,3,2,1,0:T(8,128)}, u32[]{:S(2)}) copy-start(f32[1,1,2,256,256]{4,3,2,1,0:T(8,128)} %param.11) | copy-start | bytes 1572868
  21.3 0.9 %copy-start.5 = (f32[2,128,256]{2,1,0:T(8,128)S(1)}, f32[2,128,256]{2,1,0:T(8,128)}, u32[]{:S(2)}) copy-start(f32[2,128,256]{2,1,0:T(8,128)} %copy-done.4) | copy-start | bytes 786436
  22.2 0.9 %copy-start.7 = (f32[2,2,128,128]{3,2,1,0:T(8,128)S(1)}, f32[2,2,128,128]{3,2,1,0:T(8,128)}, u32[]{:S(2)}) copy-start(f32[2,2,128,128]{3,2,1,0:T(8,128)} %copy-done.6) | copy-start | bytes 786436
  23.2 0.9 %copy-start.9 = (f32[2,128,256]{2,1,0:T(8,128)S(1)}, f32[2,128,256]{2,1,0:T(8,128)}, u32[]{:S(2)}) copy-start(f32[2,128,256]{2,1,0:T(8,128)} %copy-done.8) | copy-start | bytes 786436
  24.1 0.9 %copy-start.11 = (f32[2,2,128,128]{3,2,1,0:T(8,128)S(1)}, f32[2,2,128,128]{3,2,1,0:T(8,128)}, u32[]{:S(2)}) copy-start(f32[2,2,128,128]{3,2,1,0:T(8,128)} %copy-done.10) | copy-start | bytes 786436
  25.1 1.2 %copy-start.12 = (bf16[2,512,512]{2,1,0:T(8,128)(2,1)S(1)}, bf16[2,512,512]{2,1,0:T(8,128)(2,1)}, u32[]{:S(2)}) copy-start(bf16[2,512,512]{2,1,0:T(8,128)(2,1)} %constant.92.clone.table) | copy-start | bytes 3145732
  33.3 2.1 %collective-permute-start.13 = (f32[776,128]{1,0:T(8,128)}, f32[776,128]{1,0:T(8,128)}, u32[]{:S(2)}, u32[]{:S(2)}) collective-permute-start(f32[776,128]{1,0:T(8,128)} %pad_maximum_fusion), channel_id=1, source_target_pairs={{0,8},{8,0},{16,24},{24,16},{1,9},{9,1},{17,25},{25,17},{2,10},{10... | collective-permute-start | bytes 1191944 | tf_op jit(solution)/shard_map/ppermute | solution.py:325
  37.3 7.3 %collective-permute-start.14 = (f32[392,128]{1,0:T(8,128)S(1)}, f32[392,128]{1,0:T(8,128)S(1)}, u32[]{:S(2)}, u32[]{:S(2)}) collective-permute-start(f32[392,128]{1,0:T(8,128)S(1)} %pad_maximum_fusion.2), channel_id=1, source_target_pairs={{0,16},{8,24},{16,0},{24,8},{1,17},{9,25},{17,1},{25,9},{2,18},{10... | collective-permute-start | bytes 602120 | tf_op jit(solution)/shard_map/ppermute | solution.py:325
  44.7 7.4 %collective-permute-start.15 = (f32[200,128]{1,0:T(8,128)S(1)}, f32[200,128]{1,0:T(8,128)S(1)}, u32[]{:S(2)}, u32[]{:S(2)}) collective-permute-start(f32[200,128]{1,0:T(8,128)S(1)} %pad_maximum_fusion.3), channel_id=1, source_target_pairs={{0,1},{1,0},{2,3},{3,2},{4,5},{5,4},{6,7},{7,6},{8,9},{9,8},{10,11... | collective-permute-start | bytes 307208 | tf_op jit(solution)/shard_map/ppermute | solution.py:325
  49.8 9.0 %collective-permute-start.8 = (f32[2,128,512]{2,1,0:T(8,128)S(1)}, f32[2,128,512]{2,1,0:T(8,128)}, u32[]{:S(2)}, u32[]{:S(2)}) collective-permute-start(f32[2,128,512]{2,1,0:T(8,128)S(1)} %get-tuple-element.8), channel_id=1, source_target_pairs={{0,8},{8,0},{16,24},{24,16},{1,9},{9,1},{17,25},{25,17},{2,10},{10... | collective-permute-start | bytes 1572872 | tf_op jit(solution)/shard_map/ppermute | solution.py:274
  49.9 9.0 %collective-permute-start.9 = (f32[2,128,512]{2,1,0:T(8,128)S(1)}, f32[2,128,512]{2,1,0:T(8,128)}, u32[]{:S(2)}, u32[]{:S(2)}) collective-permute-start(f32[2,128,512]{2,1,0:T(8,128)S(1)} %get-tuple-element.9), channel_id=1, source_target_pairs={{0,8},{8,0},{16,24},{24,16},{1,9},{9,1},{17,25},{25,17},{2,10},{10... | collective-permute-start | bytes 1572872 | tf_op jit(solution)/shard_map/ppermute | solution.py:274
  52.2 5.9 %collective-permute-start.16 = (f32[200,128]{1,0:T(8,128)S(1)}, f32[200,128]{1,0:T(8,128)S(1)}, u32[]{:S(2)}, u32[]{:S(2)}) collective-permute-start(f32[200,128]{1,0:T(8,128)S(1)} %pad_maximum_fusion.4), channel_id=1, source_target_pairs={{0,2},{1,3},{2,0},{3,1},{4,6},{5,7},{6,4},{7,5},{8,10},{9,11},{10,... | collective-permute-start | bytes 307208 | tf_op jit(solution)/shard_map/ppermute | solution.py:325
  58.1 4.1 %collective-permute-start.17 = (f32[200,128]{1,0:T(8,128)S(1)}, f32[200,128]{1,0:T(8,128)S(1)}, u32[]{:S(2)}, u32[]{:S(2)}) collective-permute-start(f32[200,128]{1,0:T(8,128)S(1)} %pad_maximum_fusion.5), channel_id=1, source_target_pairs={{2,4},{3,5},{4,2},{5,3},{10,12},{11,13},{12,10},{13,11},{18,20},{1... | collective-permute-start | bytes 307208 | tf_op jit(solution)/shard_map/ppermute | solution.py:325
  60.0 17.2 %collective-permute-start.10 = (f32[2,128,512]{2,1,0:T(8,128)S(1)}, f32[2,128,512]{2,1,0:T(8,128)S(1)}, u32[]{:S(2)}, u32[]{:S(2)}) collective-permute-start(f32[2,128,512]{2,1,0:T(8,128)S(1)} %broadcast_select_fusion), channel_id=1, source_target_pairs={{0,16},{24,8},{1,17},{25,9},{2,18},{26,10},{3,19},{27,11},{4,20},{... | collective-permute-start | bytes 1572872 | tf_op jit(solution)/shard_map/ppermute | solution.py:311
  64.3 8.4 %collective-permute-start.18 = (f32[2,64,128]{2,1,0:T(8,128)S(1)}, f32[2,64,128]{2,1,0:T(8,128)S(1)}, u32[]{:S(2)}, u32[]{:S(2)}) collective-permute-start(f32[2,64,128]{2,1,0:T(8,128)S(1)} %fusion.2), channel_id=1, source_target_pairs={{2,0},{3,1},{4,6},{5,7},{10,8},{11,9},{12,14},{13,15},{18,16},{19,... | collective-permute-start | bytes 196616 | tf_op jit(solution)/shard_map/ppermute | solution.py:372
  72.7 4.3 %collective-permute-start.19 = (f32[2,64,128]{2,1,0:T(8,128)S(1)}, f32[2,64,128]{2,1,0:T(8,128)S(1)}, u32[]{:S(2)}, u32[]{:S(2)}) collective-permute-start(f32[2,64,128]{2,1,0:T(8,128)S(1)} %broadcast_select_fusion.3), channel_id=1, source_target_pairs={{0,1},{1,0},{2,3},{3,2},{4,5},{5,4},{6,7},{7,6},{8,9},{9,8},{10,11... | collective-permute-start | bytes 196616 | tf_op jit(solution)/shard_map/ppermute | solution.py:274
  77.1 6.6 %collective-permute-start.20 = (f32[2,128,128]{2,1,0:T(8,128)S(1)}, f32[2,128,128]{2,1,0:T(8,128)S(1)}, u32[]{:S(2)}, u32[]{:S(2)}) collective-permute-start(f32[2,128,128]{2,1,0:T(8,128)S(1)} %maximum_select_fusion.2), channel_id=1, source_target_pairs={{0,16},{8,24},{16,0},{24,8},{1,17},{9,25},{17,1},{25,9},{2,18},{10... | collective-permute-start | bytes 393224 | tf_op jit(solution)/shard_map/ppermute | solution.py:274
  78.4 5.3 %collective-permute-start.11 = (f32[2,128,128]{2,1,0:T(8,128)S(1)}, f32[2,128,128]{2,1,0:T(8,128)S(1)}, u32[]{:S(2)}, u32[]{:S(2)}) collective-permute-start(f32[2,128,128]{2,1,0:T(8,128)S(1)} %get-tuple-element.14), channel_id=1, source_target_pairs={{1,2},{3,4},{5,6},{2,1},{4,3},{6,5},{9,10},{11,12},{13,14},{10,9},... | collective-permute-start | bytes 393224 | tf_op jit(solution)/shard_map/ppermute | solution.py:315
  79.1 6.3 %collective-permute-start.12 = (f32[2,128,128]{2,1,0:T(8,128)S(1)}, f32[2,128,128]{2,1,0:T(8,128)S(1)}, u32[]{:S(2)}, u32[]{:S(2)}) collective-permute-start(f32[2,128,128]{2,1,0:T(8,128)S(1)} %get-tuple-element.15), channel_id=1, source_target_pairs={{0,1},{1,0},{2,3},{3,2},{4,5},{5,4},{6,7},{7,6},{8,9},{9,8},{10,11... | collective-permute-start | bytes 393224 | tf_op jit(solution)/shard_map/ppermute | solution.py:314
  83.6 2.6 %collective-permute-start.21 = (f32[2,256,128]{2,1,0:T(8,128)S(1)}, f32[2,256,128]{2,1,0:T(8,128)S(1)}, u32[]{:S(2)}, u32[]{:S(2)}) collective-permute-start(f32[2,256,128]{2,1,0:T(8,128)S(1)} %maximum_select_fusion.1), channel_id=1, source_target_pairs={{0,8},{8,0},{16,24},{24,16},{1,9},{9,1},{17,25},{25,17},{2,10},{10... | collective-permute-start | bytes 786440 | tf_op jit(solution)/shard_map/ppermute | solution.py:274

commit v2 on v1

v2 whole, which is shorter than its diff:
```python
import functools
import math

import jax
import jax.numpy as jnp
import ml_dtypes
import numpy as np
from jax import lax
from jax.experimental import pallas as pl
from jax.experimental.pallas import tpu as pltpu
from jax.sharding import PartitionSpec as P

modulus_floor = 0.25
object_damping = 0.1
probe_damping = 0.1
LANES = 128
SUBLANES = 8
VMEM_LIMIT = 20 * 1024 * 1024


def dft_table(width):
    counter = np.arange(width)
    angle = (counter[:, None] * counter[None, :] % width) * (2.0 * math.pi / width)
    table = np.concatenate([np.cos(angle), np.sin(angle)], 1) / math.sqrt(width)
    high = table.astype(ml_dtypes.bfloat16)
    low = (table - high.astype(np.float64)).astype(ml_dtypes.bfloat16)
    return np.stack([high, low])


def halves(value):
    high = value.astype(jnp.bfloat16)
    return high, (value - high.astype(jnp.float32)).astype(jnp.bfloat16)


def product(left, right):
    dot = functools.partial(jnp.dot, preferred_element_type=jnp.float32)
    return dot(left[0], right[0]) + (dot(left[1], right[0]) + dot(left[0], right[1]))


def turn(first, second, third, ref, at):
    for place, block in zip(at, (first, second, third)):
        for half_at, half in enumerate(halves(block)):
            ref[half_at, *place] = half


def split_start(start, step, last):
    aligned = jnp.minimum(start // step, last // step) * step
    return pl.multiple_of(aligned, step), start - aligned


def lane_groups(value):
    return [value[..., at : at + LANES] for at in range(0, value.shape[-1], LANES)]


def cut(value, row_shift, lane_shift):
    rows, lanes = value.shape
    value = value.reshape(rows // SUBLANES, SUBLANES, lanes)
    lane_turn = lax.rem(LANES - lane_shift, LANES)
    row_turn = lax.rem(SUBLANES - row_shift, SUBLANES)
    shape = (rows // SUBLANES, SUBLANES, LANES)
    keep_lane = lax.broadcasted_iota(jnp.int32, shape, 2) < LANES - lane_shift
    keep_row = lax.broadcasted_iota(jnp.int32, shape, 1)[1:] < SUBLANES - row_shift
    turned = [pltpu.roll(group, lane_turn, 2) for group in lane_groups(value)]
    parts = []
    for first, second in zip(turned[:-1], turned[1:]):
        part = pltpu.roll(jnp.where(keep_lane, first, second), row_turn, 1)
        part = jnp.where(keep_row, part[:-1], part[1:])
        parts.append(part.reshape(rows - SUBLANES, LANES))
    return jnp.concatenate(parts, 1)


def spread(value, row_shift, lane_shift):
    rows, lanes = value.shape
    value = value.reshape(rows // SUBLANES, SUBLANES, lanes)
    shape = (rows // SUBLANES + 1, SUBLANES, LANES)
    lane_turn = lax.rem(lane_shift, LANES)
    take_lane = lax.broadcasted_iota(jnp.int32, shape, 2) < lane_shift
    take_row = lax.broadcasted_iota(jnp.int32, shape, 1) < row_shift
    blank_row = jnp.zeros((1, SUBLANES, LANES), value.dtype)
    turned = []
    for group in lane_groups(value):
        group = pltpu.roll(group, row_shift, 1)
        group = jnp.where(
            take_row,
            jnp.concatenate([blank_row, group], 0),
            jnp.concatenate([group, blank_row], 0),
        )
        turned.append(pltpu.roll(group, lane_turn, 2))
    blank = jnp.zeros(shape, value.dtype)
    parts = [
        jnp.where(take_lane, first, second).reshape(rows + SUBLANES, LANES)
        for first, second in zip([blank] + turned, turned + [blank])
    ]
    return jnp.concatenate(parts, 1)


def lighting_kernel(offsets, counts, probe, out, pad):
    rows, cols, slots = offsets.shape[:3]
    tile_r, tile_c = out.shape
    width = probe.shape[1]
    half = width // 2
    row_place = lax.axis_index("row")
    col_place = lax.axis_index("col")
    power = probe[0] * probe[0] + probe[1] * probe[1]
    pad[...] = jnp.zeros_like(pad)
    pad[tile_r : tile_r + width, tile_c : tile_c + width] = power
    out[...] = jnp.full(out.shape, object_damping * jnp.max(power))
    wide = tile_c + LANES
    for row_step in (-1, 0, 1):
        for col_step in (-1, 0, 1):
            row, col = row_place + row_step, col_place + col_step
            inside = (row >= 0) & (row < rows) & (col >= 0) & (col < cols)
            row_at = jnp.clip(row, 0, rows - 1)
            col_at = jnp.clip(col, 0, cols - 1)
            for slot in range(slots):
                top = offsets[row_at, col_at, slot, 0] + row_step * tile_r
                left = offsets[row_at, col_at, slot, 1] + col_step * tile_c

                @pl.when(
                    inside
                    & (slot < counts[row_at, col_at])
                    & (left > -width)
                    & (left < tile_c)
                )
                def _():
                    row, row_shift = split_start(tile_r - top, SUBLANES, tile_r + width)
                    lane, lane_shift = split_start(tile_c - left, LANES, pad.shape[1] - wide)
                    part = pad[pl.ds(row, tile_r + SUBLANES), pl.ds(lane, wide)]
                    out[...] += cut(part, row_shift, lane_shift)


def lighting(offsets, counts, probe, tile_r, tile_c):
    width = probe.shape[1]
    smem = pl.BlockSpec(memory_space=pltpu.SMEM)
    vmem = pl.BlockSpec(memory_space=pltpu.VMEM)
    return pl.pallas_call(
        lighting_kernel,
        out_shape=jax.ShapeDtypeStruct((tile_r, tile_c), jnp.float32),
        in_specs=[smem, smem, vmem],
        out_specs=vmem,
        scratch_shapes=[
            pltpu.VMEM((2 * tile_r + width + SUBLANES, 2 * tile_c + width), jnp.float32)
        ],
        compiler_params=pltpu.CompilerParams(vmem_limit_bytes=VMEM_LIMIT),
        cost_estimate=pl.CostEstimate(flops=4000000, bytes_accessed=800000, transcendentals=0),
    )(offsets, counts, probe)


def patch_block(offsets, row_place, col_place, slot, half, tile_r, width):
    row, row_shift = split_start(offsets[row_place, col_place, slot, 0] + half, SUBLANES, tile_r)
    lane, lane_shift = split_start(
        offsets[row_place, col_place, slot, 1] + half, LANES, 2 * half - LANES
    )
    return (pl.ds(row, width + SUBLANES), pl.ds(lane, width + LANES)), row_shift, lane_shift


def delta_kernel(
    offsets, counts, probe, magnitudes, table, own, rim, near, near_rim, far, far_rim,
    kept, given, own_probe, delta, ext, patches, left, right, stack, basis_in, measured, arrived,
):
    table_copy = pltpu.make_async_copy(table, basis_in, arrived.at[0])
    measured_copy = pltpu.make_async_copy(magnitudes, measured, arrived.at[1])
    table_copy.start()
    measured_copy.start()
    slots, width = magnitudes.shape[0], magnitudes.shape[1]
    half = width // 2
    tile_r, tile_c = own.shape[1:]
    row_place = lax.axis_index("row")
    col_place = lax.axis_index("col")
    row_odd = lax.rem(row_place, 2)
    col_odd = lax.rem(col_place, 2)
    near_row = pl.multiple_of((1 - row_odd) * (tile_r + half), half)
    far_row = pl.multiple_of(row_odd * (tile_r + half), half)
    pair_col = pl.multiple_of((1 - col_odd) * (tile_c + half), half)
    other_col = pl.multiple_of(col_odd * (tile_c + half), half)
    far_at = row_place + 2 * row_odd - 1
    inside = (far_at >= 0) & (far_at < lax.axis_size("row"))
    for part in range(2):
        for rows, mid, edge in ((half, own, rim), (near_row, near, near_rim)):
            at = pl.ds(rows, tile_r)
            ext[part, at, half : half + tile_c] = mid[part]
            ext[part, at, pl.ds(pair_col, half)] = edge[0, part]
            ext[part, at, pl.ds(other_col, half)] = edge[1, part]
        at = pl.ds(far_row, tile_r)
        ext[part, at, half : half + tile_c] = jnp.where(inside, far[part], 0.0)
        ext[part, at, pl.ds(pair_col, half)] = jnp.where(inside, far_rim[0, part], 0.0)
        ext[part, at, pl.ds(other_col, half)] = jnp.where(inside, far_rim[1, part], 0.0)
    live_count = counts[row_place, col_place]
    probe_real, probe_imag = probe[0], probe[1]
    first = slice(0, 2 * width)
    second = slice(width, 3 * width)
    places = [slice(k * width, (k + 1) * width) for k in range(3)]
    for slot in range(slots):
        block, row_shift, lane_shift = patch_block(
            offsets, row_place, col_place, slot, half, tile_r, width
        )
        for part in range(2):
            patches[slot, part] = cut(ext[part, *block], row_shift, lane_shift)
        patch_real, patch_imag = patches[slot, 0], patches[slot, 1]
        real = probe_real * patch_real - probe_imag * patch_imag
        imag = probe_real * patch_imag + probe_imag * patch_real
        at = slice(slot * width, (slot + 1) * width)
        turn(real, imag, -real, left, [(at, place) for place in places])
    table_copy.wait()
    stack[:, :width] = basis_in[:, :, :width]
    stack[:, width:] = basis_in[:, :, width:]
    basis = (stack[0], stack[1])
    basis_left = (basis_in[0], basis_in[1])
    real = product((left[0, :, first], left[1, :, first]), basis)
    imag = product((left[0, :, second], left[1, :, second]), basis)
    measured_copy.wait()
    for slot in range(slots):
        at = slice(slot * width, (slot + 1) * width)
        turn(real[at], imag[at], -real[at], right, [(place,) for place in places])
        far_real = product(basis_left, (right[0, first], right[1, first]))
        far_imag = product(basis_left, (right[0, second], right[1, second]))
        inverse = jnp.minimum(
            lax.rsqrt(far_real * far_real + far_imag * far_imag), 1.0 / modulus_floor
        )
        factor = measured[slot] * inverse - 1.0
        back_real, back_imag = far_real * factor, far_imag * factor
        turn(back_imag, back_real, -back_imag, left, [(at, place) for place in places])
    imag = product((left[0, :, first], left[1, :, first]), basis)
    real = product((left[0, :, second], left[1, :, second]), basis)
    sums = [jnp.zeros((width, width), jnp.float32)] * 3
    for slot in range(slots):
        at = slice(slot * width, (slot + 1) * width)
        turn(imag[at], real[at], -imag[at], right, [(place,) for place in places])
        live = jnp.where(slot < live_count, 1.0, 0.0)
        delta_imag = product(basis_left, (right[0, first], right[1, first])) * live
        delta_real = product(basis_left, (right[0, second], right[1, second])) * live
        delta[slot, 0] = delta_real
        delta[slot, 1] = delta_imag
        patch_real, patch_imag = patches[slot, 0], patches[slot, 1]
        sums = [
            sums[0] + (patch_real * delta_real + patch_imag * delta_imag),
            sums[1] + (patch_real * delta_imag - patch_imag * delta_real),
            sums[2] + live * (patch_real * patch_real + patch_imag * patch_imag),
        ]
    even = row_odd == 0
    for layer in range(3):
        low, high = lane_groups(sums[layer])
        kept[layer * width : (layer + 1) * width] = jnp.where(even, low, high)
        given[layer * width : (layer + 1) * width] = jnp.where(even, high, low)
    total = jnp.full((SUBLANES, LANES), jnp.sum(sums[2]))
    kept[3 * width :] = total
    given[3 * width :] = total
    size = own_probe.shape[1]
    row = pl.multiple_of(lax.rem(row_place // 2, 2) * (2 * size) + col_odd * size, size)
    for part in range(2):
        low, high = lane_groups(probe[part, pl.ds(row, size), :])
        own_probe[part] = jnp.where(even, low, high)


def place_kernel(
    offsets, probe, delta, center, close, onward, center_rim, close_rim, onward_rim, ext
):
    slots, width = delta.shape[0], delta.shape[2]
    half = width // 2
    tile_r, tile_c = center.shape[1:]
    row_place = lax.axis_index("row")
    col_place = lax.axis_index("col")
    row_odd = lax.rem(row_place, 2)
    col_odd = lax.rem(col_place, 2)
    ext[...] = jnp.zeros_like(ext)
    probe_real, probe_imag = probe[0], probe[1]
    for slot in range(slots):
        real, imag = delta[slot, 0], delta[slot, 1]
        block, row_shift, lane_shift = patch_block(
            offsets, row_place, col_place, slot, half, tile_r, width
        )
        for part, grad in enumerate(
            (probe_real * real + probe_imag * imag, probe_real * imag - probe_imag * real)
        ):
            ext[part, *block] += spread(grad, row_shift, lane_shift)
    near_row = pl.multiple_of((1 - row_odd) * (tile_r + half), half)
    far_row = pl.multiple_of(row_odd * (tile_r + half), half)
    pair_col = pl.multiple_of((1 - col_odd) * (tile_c + half), half)
    other_col = pl.multiple_of(col_odd * (tile_c + half), half)
    for row, mid, rim in (
        (half, center, center_rim),
        (near_row, close, close_rim),
        (far_row, onward, onward_rim),
    ):
        at = pl.ds(row, tile_r)
        mid[...] = ext[:, at, half : half + tile_c]
        rim[0] = ext[:, at, pl.ds(pair_col, half)]
        rim[1] = ext[:, at, pl.ds(other_col, half)]


def exit_update(offsets, counts, probe, magnitudes, own, rim, near, near_rim, far, far_rim):
    slots, width = magnitudes.shape[:2]
    half = width // 2
    tile_r, tile_c = own.shape[1:]
    smem = pl.BlockSpec(memory_space=pltpu.SMEM)
    vmem = pl.BlockSpec(memory_space=pltpu.VMEM)
    return pl.pallas_call(
        delta_kernel,
        out_shape=[
            jax.ShapeDtypeStruct((3 * width + SUBLANES, LANES), jnp.float32),
            jax.ShapeDtypeStruct((3 * width + SUBLANES, LANES), jnp.float32),
            jax.ShapeDtypeStruct((2, width // 4, LANES), jnp.float32),
            jax.ShapeDtypeStruct((slots, 2, width, width), jnp.float32),
        ],
        in_specs=[smem, smem, vmem] + [pl.BlockSpec(memory_space=pltpu.HBM)] * 2 + [vmem] * 6,
        out_specs=[vmem] * 4,
        scratch_shapes=[
            pltpu.VMEM((2, tile_r + 2 * half + SUBLANES, tile_c + 2 * half), jnp.float32),
            pltpu.VMEM((slots, 2, width, width), jnp.float32),
            pltpu.VMEM((2, slots * width, 3 * width), jnp.bfloat16),
            pltpu.VMEM((2, 3 * width, width), jnp.bfloat16),
            pltpu.VMEM((2, 2 * width, width), jnp.bfloat16),
            pltpu.VMEM((2, width, 2 * width), jnp.bfloat16),
            pltpu.VMEM((slots, width, width), jnp.float32),
            pltpu.SemaphoreType.DMA((2,)),
        ],
        compiler_params=pltpu.CompilerParams(vmem_limit_bytes=VMEM_LIMIT),
        cost_estimate=pl.CostEstimate(
            flops=3200000000, bytes_accessed=8000000, transcendentals=131072
        ),
    )(
        offsets, counts, probe, in_hbm(magnitudes), in_hbm(jnp.asarray(dft_table(width))),
        *map(in_vmem, (own, rim, near, near_rim, far, far_rim)),
    )


def in_hbm(value):
    return pltpu.with_memory_space_constraint(value, pltpu.HBM)


def in_vmem(value):
    return pltpu.with_memory_space_constraint(value, pltpu.VMEM)


def fold_kernel(axis, bit, kept_in, got, kept, given):
    layers = 3
    size = (kept.shape[0] - SUBLANES) // layers
    odd = lax.rem(lax.axis_index(axis) // bit, 2)
    for layer in range(layers):
        first = 2 * layer * size
        mine = pl.ds(pl.multiple_of(first + odd * size, SUBLANES), size)
        other = pl.ds(pl.multiple_of(first + (1 - odd) * size, SUBLANES), size)
        at = slice(layer * size, (layer + 1) * size)
        kept[at] = kept_in[mine] + got[mine]
        given[at] = kept_in[other] + got[other]
    total = kept_in[2 * layers * size :] + got[2 * layers * size :]
    kept[layers * size :] = total
    given[layers * size :] = total


def fold(kept, got, axis, bit):
    vmem = pl.BlockSpec(memory_space=pltpu.VMEM)
    shape = jax.ShapeDtypeStruct(((kept.shape[0] + SUBLANES) // 2, LANES), jnp.float32)
    return pl.pallas_call(
        functools.partial(fold_kernel, axis, bit),
        out_shape=[shape] * 2,
        in_specs=[vmem] * 2,
        out_specs=[vmem] * 2,
        compiler_params=pltpu.CompilerParams(vmem_limit_bytes=VMEM_LIMIT),
        cost_estimate=pl.CostEstimate(flops=100000, bytes_accessed=400000, transcendentals=0),
    )(in_vmem(kept), in_vmem(got))


def place(offsets, probe, delta, tile_r, tile_c):
    width = probe.shape[1]
    half = width // 2
    smem = pl.BlockSpec(memory_space=pltpu.SMEM)
    vmem = pl.BlockSpec(memory_space=pltpu.VMEM)
    middle = jax.ShapeDtypeStruct((2, tile_r, tile_c), jnp.float32)
    rim = jax.ShapeDtypeStruct((2, 2, tile_r, half), jnp.float32)
    return pl.pallas_call(
        place_kernel,
        out_shape=[middle] * 3 + [rim] * 3,
        in_specs=[smem, vmem, vmem],
        out_specs=[vmem] * 6,
        scratch_shapes=[
            pltpu.VMEM((2, tile_r + 2 * half + SUBLANES, tile_c + 2 * half), jnp.float32),
        ],
        compiler_params=pltpu.CompilerParams(vmem_limit_bytes=VMEM_LIMIT),
        cost_estimate=pl.CostEstimate(flops=4000000, bytes_accessed=4000000, transcendentals=0),
    )(offsets, probe, delta)


def exchange(value, axis, count, bit):
    return lax.ppermute(value, axis, [(i, i ^ bit) for i in range(count)])


def shards(specimen, probe_field, scan_offsets, live_counts, magnitudes):
    rows, cols = lax.axis_size("row"), lax.axis_size("col")
    width = probe_field.shape[1]
    half = width // 2
    tile_r, tile_c = specimen.shape[1:]
    row_place = lax.axis_index("row")
    col_place = lax.axis_index("col")
    row_odd = row_place % 2
    col_odd = col_place % 2
    pairs = [(i, i ^ 1) for i in range(cols)]
    others = [(i, i + 1) for i in range(1, cols - 1, 2)] + [(i + 1, i) for i in range(1, cols - 1, 2)]
    toward = [(i, i + 2) for i in range(1, rows - 2, 2)] + [(i, i - 2) for i in range(2, rows, 2)]
    toward += [(rows - 1, rows - 2), (0, 1)]
    onward_pairs = [(target, source) for source, target in toward]

    low, high = specimen[:, :, :half], specimen[:, :, tile_c - half :]
    pair_rim = lax.ppermute(jnp.where(col_odd == 0, high, low), "col", pairs)
    other_rim = lax.ppermute(jnp.where(col_odd == 0, low, high), "col", others)
    beyond = lax.ppermute(specimen, "row", toward)
    rim = jnp.stack([pair_rim, other_rim])
    beyond_rim = lax.ppermute(rim, "row", toward)
    near = exchange(specimen, "row", rows, 1)
    near_rim = exchange(rim, "row", rows, 1)
    far = exchange(beyond, "row", rows, 1)
    far_rim = exchange(beyond_rim, "row", rows, 1)

    kept, given, own_probe, delta = exit_update(
        scan_offsets, live_counts, probe_field, magnitudes[0, 0],
        specimen, rim, near, near_rim, far, far_rim,
    )

    def pick(condition, first, second):
        return jnp.where(condition, first, second)

    def join(value, axis, count, bit):
        place_here = (lax.axis_index(axis) // bit) % 2
        got = exchange(value, axis, count, bit)
        return pick(
            place_here == 0,
            jnp.concatenate([value, got], 1),
            jnp.concatenate([got, value], 1),
        )

    tie = lax.optimization_barrier
    got = exchange(given, "row", rows, 1)
    center, close, onward, center_rim, close_rim, onward_rim = place(
        scan_offsets, probe_field, delta, tile_r, tile_c
    )
    got, close, onward, close_rim, onward_rim = tie((got, close, onward, close_rim, onward_rim))
    kept, given = fold(kept, got, "row", 2)
    got_close_rim = exchange(close_rim, "row", rows, 1)
    got_onward_rim = exchange(onward_rim, "row", rows, 1)
    got_close = exchange(close, "row", rows, 1)
    got_onward = exchange(onward, "row", rows, 1)
    probe_late, given = tie((probe_field, given))
    light = lighting(scan_offsets, live_counts, probe_late, tile_r, tile_c)
    got = exchange(given, "row", rows, 2)
    got, got_onward_rim, got_onward, light = tie((got, got_onward_rim, got_onward, light))
    kept, given = fold(kept, got, "col", 1)
    value = kept + exchange(given, "col", cols, 1)
    value, got_onward_rim, got_onward = tie((value, got_onward_rim, got_onward))
    beyond_rim = lax.ppermute(got_onward_rim, "row", onward_pairs)
    beyond = lax.ppermute(got_onward, "row", onward_pairs)
    for bit in (1 << k for k in range(1, cols.bit_length() - 1)):
        value = value + exchange(value, "col", cols, 2 * bit - 2)
    for bit in (1 << k for k in range(2, rows.bit_length() - 1)):
        value = value + exchange(value, "row", rows, bit)
    value, beyond_rim = tie((value, beyond_rim))
    inside = (row_place + 2 * row_odd - 1 >= 0) & (row_place + 2 * row_odd - 1 < rows)
    rim_sum = center_rim + got_close_rim + pick(inside, beyond_rim, 0.0)
    pair_part = lax.ppermute(rim_sum[0], "col", pairs)
    other_part = lax.ppermute(rim_sum[1], "col", others)
    size = own_probe.shape[1]
    real, imag, weight, total = (value[k * size : (k + 1) * size] for k in range(4))
    update = jnp.stack([real, imag]) / (weight + probe_damping * (total[:1] / (width * width)))
    fresh = own_probe + update
    fresh = join(fresh, "col", cols, 1)
    fresh, pair_part = tie((fresh, pair_part))
    fresh = join(fresh, "row", rows, 2)
    fresh, other_part, beyond = tie((fresh, other_part, beyond))
    got = exchange(fresh, "row", rows, 1)
    low_part = pick(col_odd == 0, other_part, pair_part)
    high_part = pick(col_odd == 0, pair_part, other_part)
    middle = center + got_close + pick(inside, beyond, 0.0)
    middle = middle + jnp.concatenate([low_part, high_part], 2)
    specimen_next = specimen + middle / light
    probe_next = pick(
        row_odd == 0, jnp.concatenate([fresh, got], 2), jnp.concatenate([got, fresh], 2)
    )
    return (specimen_next, probe_next)


def solution(mesh):
    return jax.shard_map(
        shards,
        mesh=mesh,
        in_specs=(P(None, "row", "col"), P(), P(), P(), P("row", "col", None, None, None)),
        out_specs=(P(None, "row", "col"), P()),
        check_vma=False,
    )
```

time: 87.9 us -> 71.8 us (0.82)
  the two profiles are of different devices: /device:TPU:0 before, /device:TPU:11 now
where the time goes in v2:
time: 71.8 us; the launch traced here: 71.5 us
  starting transfers between devices  37.1 us (52%)
  waiting for transfers between devices  19.5 us (27%)
  Pallas kernels  11 us (15%)
  other arithmetic  2.9 us (4%)
  between operations  0.86 us (1%)
    ppermute x16, starting transfers between devices, exchange(): return lax.ppermute(value, axis, [(i, i ^ bit) for i in range(count)])  23.2 us
    ppermute x16, waiting for transfers between devices, exchange(): return lax.ppermute(value, axis, [(i, i ^ bit) for i in range(count)])  10.3 us
    pallas_call x1, Pallas kernels, exit_update(): pl.pallas_call(delta_kernel, out_shape=[jax.ShapeDtypeStruct((3 * width +...  6.77 us
    ppermute x1, waiting for transfers between devices, shards(): pair_rim = lax.ppermute(jnp.where(col_odd == 0, high, low), 'col', pairs)  3.86 us
    ppermute x1, waiting for transfers between devices, shards(): beyond_rim = lax.ppermute(rim, 'row', toward)  3.68 us
    ppermute x1, starting transfers between devices, shards(): beyond = lax.ppermute(got_onward, 'row', onward_pairs)  3.52 us
    ppermute x1, starting transfers between devices, shards(): other_rim = lax.ppermute(jnp.where(col_odd == 0, low, high), 'col', others)  3.03 us
    ppermute x1, starting transfers between devices, shards(): other_part = lax.ppermute(rim_sum[1], 'col', others)  2.75 us
  transfers between devices with their start and end apart: 24, of which 9 were waited for; matrix products, arithmetic and copies ran while one was open for 2% of the time, Pallas kernels for 6%

profile of v2, /device:TPU:11, one launch (start us, length us, event | category | flops | bytes accessed | tf_op | source)
XLA Modules:
  0.0 71.5 jit_solution(15300283343081699031)
XLA Ops:
  0.7 1.1 %slice_select_fusion.1 = (f32[2,128,128]{2,1,0:T(8,128)S(1)}, f32[2,128,128]{2,1,0:T(8,128)S(1)}) fusion(f32[2,128,256]{2,1,0:T(8,128)} %own.1, pred[]{:T(512)S(6)} %eq.18), kind=kLoop, calls=%fused_computation.11 | loop fusion | flops 65536 | bytes 524289 | tf_op jit(solution)/shard_map/jit(_where)/select_n | solution.py:404
  1.7 3.0 %collective-permute-start.1 = (f32[2,128,128]{2,1,0:T(8,128)S(1)}, f32[2,128,128]{2,1,0:T(8,128)S(1)}, u32[]{:S(2)}, u32[]{:S(2)}) collective-permute-start(f32[2,128,128]{2,1,0:T(8,128)S(1)} %get-tuple-element.77), channel_id=1, source_target_pairs={{1,2},{3,4},{5,6},{2,1},{4,3},{6,5},{9,10},{11,12},{13,14},{10,9},... | collective-permute-start | bytes 393224 | tf_op jit(solution)/shard_map/ppermute | solution.py:405
  4.8 1.4 %collective-permute-start = (f32[2,128,128]{2,1,0:T(8,128)S(1)}, f32[2,128,128]{2,1,0:T(8,128)S(1)}, u32[]{:S(2)}, u32[]{:S(2)}) collective-permute-start(f32[2,128,128]{2,1,0:T(8,128)S(1)} %get-tuple-element.76), channel_id=1, source_target_pairs={{0,1},{1,0},{2,3},{3,2},{4,5},{5,4},{6,7},{7,6},{8,9},{9,8},{10,11... | collective-permute-start | bytes 393224 | tf_op jit(solution)/shard_map/ppermute | solution.py:404
  6.2 1.2 %collective-permute-start.4 = (f32[2,128,256]{2,1,0:T(8,128)S(1)}, f32[2,128,256]{2,1,0:T(8,128)S(1)}, u32[]{:S(2)}, u32[]{:S(2)}) collective-permute-start(f32[2,128,256]{2,1,0:T(8,128)S(1)} %copy-done.1), channel_id=1, source_target_pairs={{8,24},{16,0},{24,16},{0,8},{9,25},{17,1},{25,17},{1,9},{10,26},{1... | collective-permute-start | bytes 786440 | tf_op jit(solution)/shard_map/ppermute | solution.py:406
  7.4 1.5 %collective-permute-done.1 = f32[2,128,128]{2,1,0:T(8,128)S(1)} collective-permute-done((f32[2,128,128]{2,1,0:T(8,128)S(1)}, f32[2,128,128]{2,1,0:T(8,128)S(1)}, u32[]{:S(2)}, u32[]{:S(2)}) %collective-permute-start.1) | collective-permute-done | bytes 131104 | tf_op jit(solution)/shard_map/ppermute | solution.py:405
  8.9 3.9 %collective-permute-done = f32[2,128,128]{2,1,0:T(8,128)S(1)} collective-permute-done((f32[2,128,128]{2,1,0:T(8,128)S(1)}, f32[2,128,128]{2,1,0:T(8,128)S(1)}, u32[]{:S(2)}, u32[]{:S(2)}) %collective-permute-start) | collective-permute-done | bytes 131104 | tf_op jit(solution)/shard_map/ppermute | solution.py:404
  12.8 0.0 copy-start.2
  12.8 0.5 collective-permute-start.6
  13.3 0.5 collective-permute-start.2
  13.8 0.5 collective-permute-start.5
  14.3 3.7 %collective-permute-done.6 = f32[2,2,128,128]{3,2,1,0:T(8,128)S(1)} collective-permute-done((f32[2,2,128,128]{3,2,1,0:T(8,128)S(1)}, f32[2,2,128,128]{3,2,1,0:T(8,128)S(1)}, u32[]{:S(2)}, u32[]{:S(2)}) %collective-permute-start.6) | collective-permute-done | bytes 262176 | tf_op jit(solution)/shard_map/ppermute | solution.py:408
  18.0 0.0 collective-permute-start.7
  18.0 0.1 copy.9.offsets
  18.2 0.0 collective-permute-done.2.near
  18.2 1.4 %collective-permute-done.7.far_rim = f32[2,2,128,128]{3,2,1,0:T(8,128)S(1)} collective-permute-done((f32[2,2,128,128]{3,2,1,0:T(8,128)S(1)}, f32[2,2,128,128]{3,2,1,0:T(8,128)S(1)}, u32[]{:S(2)}, u32[]{:S(2)}) %collective-permute-start.7) | collective-permute-done | bytes 262176 | tf_op jit(solution)/shard_map/ppermute | solution.py:385
  19.6 6.8 %shard_map.77 = (f32[776,128]{1,0:T(8,128)S(1)}, f32[776,128]{1,0:T(8,128)S(1)}, f32[2,64,128]{2,1,0:T(8,128)S(1)}, f32[2,2,256,256]{3,2,1,0:T(8,128)S(1)}) custom-call(s32[4,8,2,2]{3,2,1,0:T(2,128)S(1)} %copy.9.offsets, s32[4,8]{1,0:T(4,128)S(1)} %copy-done.2, f32[2,256,256]{2,1,0:T(8,128)S(1)} %copy-done, f32[2,256,256]{2,1,0:T(8,128)} %bitcast.15, ...), custom_call_target="tpu_custom_call" | custom-call | flops 3200000000 | bytes 8000000 | tf_op jit(solution)/shard_map/pallas_call | solution.py:297
  26.3 0.2 collective-permute-start.8
  26.5 1.7 %shard_map.78 = (f32[2,128,256]{2,1,0:T(8,128)S(1)}, f32[2,128,256]{2,1,0:T(8,128)S(1)}, f32[2,128,256]{2,1,0:T(8,128)S(1)}, f32[2,2,128,128]{3,2,1,0:T(8,128)S(...) custom-call(s32[4,8,2,2]{3,2,1,0:T(2,128)S(1)} %copy.9.offsets, f32[2,256,256]{2,1,0:T(8,128)S(1)} %copy-done, ...), custom_call_target="tpu_custom_call" | custom-call | flops 4000000 | bytes 4000000 | tf_op jit(solution)/shard_map/pallas_call | solution.py:371
  28.3 0.0 collective-permute-done.8.got
  28.3 0.4 collective-permute-start.11
  28.7 0.1 collective-permute-start.12
  28.9 1.9 %collective-permute-start.10 = (f32[392,128]{1,0:T(8,128)S(1)}, f32[392,128]{1,0:T(8,128)S(1)}, u32[]{:S(2)}, u32[]{:S(2)}) collective-permute-start(f32[392,128]{1,0:T(8,128)S(1)} %get-tuple-element.50), channel_id=1, source_target_pairs={{0,16},{8,24},{16,0},{24,8},{1,17},{9,25},{17,1},{25,9},{2,18},{10... | collective-permute-start | bytes 602120 | tf_op jit(solution)/shard_map/ppermute | solution.py:385
  30.8 2.4 %shard_map.80 = f32[128,256]{1,0:T(8,128)S(1)} custom-call(s32[4,8,2,2]{3,2,1,0:T(2,128)S(1)} %copy.9.offsets, s32[4,8]{1,0:T(4,128)S(1)} %copy-done.2, f32[2,256,256]{2,1,0:T(8,128)S(1)} %copy-done), custom_call_target="tpu_custom_call" | custom-call | flops 4000000 | bytes 800000 | tf_op jit(solution)/shard_map/pallas_call | solution.py:136
  33.2 2.7 %collective-permute-done.10.got = f32[392,128]{1,0:T(8,128)S(1)} collective-permute-done((f32[392,128]{1,0:T(8,128)S(1)}, f32[392,128]{1,0:T(8,128)S(1)}, u32[]{:S(2)}, u32[]{:S(2)}) %collective-permute-start.10) | collective-permute-done | bytes 200736 | tf_op jit(solution)/shard_map/ppermute | solution.py:385
  35.9 0.0 collective-permute-done.12
  35.9 1.3 %collective-permute-start.13 = (f32[200,128]{1,0:T(8,128)S(1)}, f32[200,128]{1,0:T(8,128)S(1)}, u32[]{:S(2)}, u32[]{:S(2)}) collective-permute-start(f32[200,128]{1,0:T(8,128)S(1)} %get-tuple-element.56), channel_id=1, source_target_pairs={{0,1},{1,0},{2,3},{3,2},{4,5},{5,4},{6,7},{7,6},{8,9},{9,8},{10,11... | collective-permute-start | bytes 307208 | tf_op jit(solution)/shard_map/ppermute | solution.py:385
  37.2 2.3 %collective-permute-done.13 = f32[200,128]{1,0:T(8,128)S(1)} collective-permute-done((f32[200,128]{1,0:T(8,128)S(1)}, f32[200,128]{1,0:T(8,128)S(1)}, u32[]{:S(2)}, u32[]{:S(2)}) %collective-permute-start.13) | collective-permute-done | bytes 102432 | tf_op jit(solution)/shard_map/ppermute | solution.py:385
  39.5 1.3 %collective-permute-start.16 = (f32[2,2,128,128]{3,2,1,0:T(8,128)S(1)}, f32[2,2,128,128]{3,2,1,0:T(8,128)S(1)}, u32[]{:S(2)}, u32[]{:S(2)}) collective-permute-start(f32[2,2,128,128]{3,2,1,0:T(8,128)S(1)} %collective-permute-done.11), channel_id=1, source_target_pairs={{24,8},{0,16},{16,24},{8,0},{25,9},{1,17},{17,25},{9,1},{26,10},{2... | collective-permute-start | bytes 786440 | tf_op jit(solution)/shard_map/ppermute | solution.py:449
  40.9 0.0 collective-permute-start.14
  40.9 3.5 %collective-permute-done.14 = f32[200,128]{1,0:T(8,128)S(1)} collective-permute-done((f32[200,128]{1,0:T(8,128)S(1)}, f32[200,128]{1,0:T(8,128)S(1)}, u32[]{:S(2)}, u32[]{:S(2)}) %collective-permute-start.14) | collective-permute-done | bytes 102432 | tf_op jit(solution)/shard_map/ppermute | solution.py:385
  44.4 1.4 %collective-permute-start.15 = (f32[200,128]{1,0:T(8,128)S(1)}, f32[200,128]{1,0:T(8,128)S(1)}, u32[]{:S(2)}, u32[]{:S(2)}) collective-permute-start(f32[200,128]{1,0:T(8,128)S(1)} %add.64), channel_id=1, source_target_pairs={{0,6},{1,7},{2,4},{3,5},{4,2},{5,3},{6,0},{7,1},{8,14},{9,15},{10,... | collective-permute-start | bytes 307208 | tf_op jit(solution)/shard_map/ppermute | solution.py:385
  45.8 2.1 %collective-permute-start.18 = (f32[2,2,128,128]{3,2,1,0:T(8,128)S(1)}, f32[2,2,128,128]{3,2,1,0:T(8,128)S(1)}, u32[]{:S(2)}, u32[]{:S(2)}) collective-permute-start(f32[2,2,128,128]{3,2,1,0:T(8,128)S(1)} %get-tuple-element.63), channel_id=1, source_target_pairs={{0,8},{8,0},{16,24},{24,16},{1,9},{9,1},{17,25},{25,17},{2,10},{10... | collective-permute-start | bytes 786440 | tf_op jit(solution)/shard_map/ppermute | solution.py:385
  47.9 0.0 collective-permute-done.15
  48.0 2.4 %collective-permute-start.17 = (f32[2,64,128]{2,1,0:T(8,128)S(1)}, f32[2,64,128]{2,1,0:T(8,128)S(1)}, u32[]{:S(2)}, u32[]{:S(2)}) collective-permute-start(f32[2,64,128]{2,1,0:T(8,128)S(1)} %fusion.2), channel_id=1, source_target_pairs={{0,1},{1,0},{2,3},{3,2},{4,5},{5,4},{6,7},{7,6},{8,9},{9,8},{10,11... | collective-permute-start | bytes 196616 | tf_op jit(solution)/shard_map/ppermute | solution.py:385
  50.4 0.0 collective-permute-done.18
  50.4 0.1 select_add_fusion
  50.5 0.1 collective-permute-start.19
  50.6 3.5 %collective-permute-start.22 = (f32[2,128,256]{2,1,0:T(8,128)S(1)}, f32[2,128,256]{2,1,0:T(8,128)S(1)}, u32[]{:S(2)}, u32[]{:S(2)}) collective-permute-start(f32[2,128,256]{2,1,0:T(8,128)S(1)} %collective-permute-done.12), channel_id=1, source_target_pairs={{24,8},{0,16},{16,24},{8,0},{25,9},{1,17},{17,25},{9,1},{26,10},{2... | collective-permute-start | bytes 786440 | tf_op jit(solution)/shard_map/ppermute | solution.py:450
  54.1 0.0 collective-permute-done.17
  54.1 0.3 collective-permute-done.19
  54.4 3.2 %collective-permute-start.20 = (f32[2,128,128]{2,1,0:T(8,128)S(1)}, f32[2,128,128]{2,1,0:T(8,128)S(1)}, u32[]{:S(2)}, u32[]{:S(2)}) collective-permute-start(f32[2,128,128]{2,1,0:T(8,128)S(1)} %maximum_select_fusion.2), channel_id=1, source_target_pairs={{0,16},{8,24},{16,0},{24,8},{1,17},{9,25},{17,1},{25,9},{2,18},{10... | collective-permute-start | bytes 393224 | tf_op jit(solution)/shard_map/ppermute | solution.py:385
  57.6 2.8 %collective-permute-start.21 = (f32[2,128,128]{2,1,0:T(8,128)S(1)}, f32[2,128,128]{2,1,0:T(8,128)S(1)}, u32[]{:S(2)}, u32[]{:S(2)}) collective-permute-start(f32[2,128,128]{2,1,0:T(8,128)S(1)} %get-tuple-element.74), channel_id=1, source_target_pairs={{1,2},{3,4},{5,6},{2,1},{4,3},{6,5},{9,10},{11,12},{13,14},{10,9},... | collective-permute-start | bytes 393224 | tf_op jit(solution)/shard_map/ppermute | solution.py:459
  60.4 4.0 %collective-permute-start.9 = (f32[2,128,256]{2,1,0:T(8,128)S(1)}, f32[2,128,256]{2,1,0:T(8,128)S(1)}, u32[]{:S(2)}, u32[]{:S(2)}) collective-permute-start(f32[2,128,256]{2,1,0:T(8,128)S(1)} %get-tuple-element.44), channel_id=1, source_target_pairs={{0,8},{8,0},{16,24},{24,16},{1,9},{9,1},{17,25},{25,17},{2,10},{10... | collective-permute-start | bytes 786440 | tf_op jit(solution)/shard_map/ppermute | solution.py:385
  64.4 0.0 collective-permute-done.21
  64.4 5.1 %collective-permute-start.23 = (f32[2,256,128]{2,1,0:T(8,128)S(1)}, f32[2,256,128]{2,1,0:T(8,128)S(1)}, u32[]{:S(2)}, u32[]{:S(2)}) collective-permute-start(f32[2,256,128]{2,1,0:T(8,128)S(1)} %maximum_select_fusion.1), channel_id=1, source_target_pairs={{0,8},{8,0},{16,24},{24,16},{1,9},{9,1},{17,25},{25,17},{2,10},{10... | collective-permute-start | bytes 786440 | tf_op jit(solution)/shard_map/ppermute | solution.py:385
  69.6 0.8 %fusion.1 = f32[2,128,256]{2,1,0:T(8,128)} fusion(f32[2,128,256]{2,1,0:T(8,128)S(1)} %copy-done.1, f32[2,128,128]{2,1,0:T(8,128)S(1)} %get-tuple-element.73, f32[2,128,128]{2,1,0:T(8,128)S(1)} %get-tuple-element.72, f32[2,128,256]{2,1,0:T(8,128)S(1)} %collective-permute-done.22, f32[2,128,256]{2,1,0:T(8,128)S(1)} %get-tuple-element.38, ...), kind=kLoop, calls=%fused_computation.5 | loop fusion | flops 458752 | bytes 1703937 | tf_op jit(solution)/shard_map/add | solution.py:473
  70.4 0.3 collective-permute-done.23
  70.7 0.8 %maximum_select_fusion = f32[2,256,256]{2,1,0:T(8,128)} fusion(f32[2,256,128]{2,1,0:T(8,128)S(1)} %collective-permute-done.23, f32[2,256,128]{2,1,0:T(8,128)S(1)} %maximum_select_fusion.1, pred[]{:T(512)S(6)} %eq.20), kind=kLoop, calls=%fused_computation | loop fusion | flops 393216 | bytes 1048577 | tf_op jit(solution)/shard_map/jit(_where)/select_n | solution.py:420
  (29 shorter events, 0.3 us)
Async XLA Ops:
  0.6 5.5 %copy-start.1 = (f32[2,128,256]{2,1,0:T(8,128)S(1)}, f32[2,128,256]{2,1,0:T(8,128)}, u32[]{:S(2)}) copy-start(f32[2,128,256]{2,1,0:T(8,128)} %own.1) | copy-start | bytes 786436
  0.7 18.9 %copy-start = (f32[2,256,256]{2,1,0:T(8,128)S(1)}, f32[2,256,256]{2,1,0:T(8,128)}, u32[]{:S(2)}) copy-start(f32[2,256,256]{2,1,0:T(8,128)} %probe.4) | copy-start | bytes 1572868
  1.7 7.2 %collective-permute-start.1 = (f32[2,128,128]{2,1,0:T(8,128)S(1)}, f32[2,128,128]{2,1,0:T(8,128)S(1)}, u32[]{:S(2)}, u32[]{:S(2)}) collective-permute-start(f32[2,128,128]{2,1,0:T(8,128)S(1)} %get-tuple-element.77), channel_id=1, source_target_pairs={{1,2},{3,4},{5,6},{2,1},{4,3},{6,5},{9,10},{11,12},{13,14},{10,9},... | collective-permute-start | bytes 393224 | tf_op jit(solution)/shard_map/ppermute | solution.py:405
  4.8 8.0 %collective-permute-start = (f32[2,128,128]{2,1,0:T(8,128)S(1)}, f32[2,128,128]{2,1,0:T(8,128)S(1)}, u32[]{:S(2)}, u32[]{:S(2)}) collective-permute-start(f32[2,128,128]{2,1,0:T(8,128)S(1)} %get-tuple-element.76), channel_id=1, source_target_pairs={{0,1},{1,0},{2,3},{3,2},{4,5},{5,4},{6,7},{7,6},{8,9},{9,8},{10,11... | collective-permute-start | bytes 393224 | tf_op jit(solution)/shard_map/ppermute | solution.py:404
  6.2 7.6 %collective-permute-start.4 = (f32[2,128,256]{2,1,0:T(8,128)S(1)}, f32[2,128,256]{2,1,0:T(8,128)S(1)}, u32[]{:S(2)}, u32[]{:S(2)}) collective-permute-start(f32[2,128,256]{2,1,0:T(8,128)S(1)} %copy-done.1), channel_id=1, source_target_pairs={{8,24},{16,0},{24,16},{0,8},{9,25},{17,1},{25,17},{1,9},{10,26},{1... | collective-permute-start | bytes 786440 | tf_op jit(solution)/shard_map/ppermute | solution.py:406
  12.7 5.3 %copy-start.3 = (s32[4,8,2,2]{1,3,2,0:T(2,128)S(1)}, s32[4,8,2,2]{1,3,2,0:T(2,128)}, u32[]{:S(2)}) copy-start(s32[4,8,2,2]{1,3,2,0:T(2,128)} %param.8) | copy-start | bytes 1540
  12.8 6.8 %copy-start.2 = (s32[4,8]{1,0:T(4,128)S(1)}, s32[4,8]{1,0:T(4,128)}, u32[]{:S(2)}) copy-start(s32[4,8]{1,0:T(4,128)} %counts.3) | copy-start | bytes 388
  12.8 5.2 %collective-permute-start.6 = (f32[2,2,128,128]{3,2,1,0:T(8,128)S(1)}, f32[2,2,128,128]{3,2,1,0:T(8,128)S(1)}, u32[]{:S(2)}, u32[]{:S(2)}) collective-permute-start(f32[2,2,128,128]{3,2,1,0:T(8,128)S(1)} %pad_maximum_fusion.rim), channel_id=1, source_target_pairs={{8,24},{16,0},{24,16},{0,8},{9,25},{17,1},{25,17},{1,9},{10,26},{1... | collective-permute-start | bytes 786440 | tf_op jit(solution)/shard_map/ppermute | solution.py:408
  13.3 4.9 %collective-permute-start.2 = (f32[2,128,256]{2,1,0:T(8,128)S(1)}, f32[2,128,256]{2,1,0:T(8,128)S(1)}, u32[]{:S(2)}, u32[]{:S(2)}) collective-permute-start(f32[2,128,256]{2,1,0:T(8,128)S(1)} %copy-done.1), channel_id=1, source_target_pairs={{0,8},{8,0},{16,24},{24,16},{1,9},{9,1},{17,25},{25,17},{2,10},{10... | collective-permute-start | bytes 786440 | tf_op jit(solution)/shard_map/ppermute | solution.py:385
  13.8 4.3 %collective-permute-start.3 = (f32[2,2,128,128]{3,2,1,0:T(8,128)S(1)}, f32[2,2,128,128]{3,2,1,0:T(8,128)S(1)}, u32[]{:S(2)}, u32[]{:S(2)}) collective-permute-start(f32[2,2,128,128]{3,2,1,0:T(8,128)S(1)} %pad_maximum_fusion.rim), channel_id=1, source_target_pairs={{0,8},{8,0},{16,24},{24,16},{1,9},{9,1},{17,25},{25,17},{2,10},{10... | collective-permute-start | bytes 786440 | tf_op jit(solution)/shard_map/ppermute | solution.py:385
  13.8 4.3 %collective-permute-start.5 = (f32[2,128,256]{2,1,0:T(8,128)S(1)}, f32[2,128,256]{2,1,0:T(8,128)S(1)}, u32[]{:S(2)}, u32[]{:S(2)}) collective-permute-start(f32[2,128,256]{2,1,0:T(8,128)S(1)} %collective-permute-done.4), channel_id=1, source_target_pairs={{0,8},{8,0},{16,24},{24,16},{1,9},{9,1},{17,25},{25,17},{2,10},{10... | collective-permute-start | bytes 786440 | tf_op jit(solution)/shard_map/ppermute | solution.py:385
  18.0 1.5 %collective-permute-start.7 = (f32[2,2,128,128]{3,2,1,0:T(8,128)S(1)}, f32[2,2,128,128]{3,2,1,0:T(8,128)S(1)}, u32[]{:S(2)}, u32[]{:S(2)}) collective-permute-start(f32[2,2,128,128]{3,2,1,0:T(8,128)S(1)} %collective-permute-done.6), channel_id=1, source_target_pairs={{0,8},{8,0},{16,24},{24,16},{1,9},{9,1},{17,25},{25,17},{2,10},{10... | collective-permute-start | bytes 786440 | tf_op jit(solution)/shard_map/ppermute | solution.py:385
  26.3 1.9 %collective-permute-start.8 = (f32[776,128]{1,0:T(8,128)S(1)}, f32[776,128]{1,0:T(8,128)S(1)}, u32[]{:S(2)}, u32[]{:S(2)}) collective-permute-start(f32[776,128]{1,0:T(8,128)S(1)} %get-tuple-element.39), channel_id=1, source_target_pairs={{0,8},{8,0},{16,24},{24,16},{1,9},{9,1},{17,25},{25,17},{2,10},{10... | collective-permute-start | bytes 1191944 | tf_op jit(solution)/shard_map/ppermute | solution.py:385
  28.3 7.6 %collective-permute-start.11 = (f32[2,2,128,128]{3,2,1,0:T(8,128)S(1)}, f32[2,2,128,128]{3,2,1,0:T(8,128)S(1)}, u32[]{:S(2)}, u32[]{:S(2)}) collective-permute-start(f32[2,2,128,128]{3,2,1,0:T(8,128)S(1)} %get-tuple-element.51), channel_id=1, source_target_pairs={{0,8},{8,0},{16,24},{24,16},{1,9},{9,1},{17,25},{25,17},{2,10},{10... | collective-permute-start | bytes 786440 | tf_op jit(solution)/shard_map/ppermute | solution.py:385
  28.7 7.2 %collective-permute-start.12 = (f32[2,128,256]{2,1,0:T(8,128)S(1)}, f32[2,128,256]{2,1,0:T(8,128)S(1)}, u32[]{:S(2)}, u32[]{:S(2)}) collective-permute-start(f32[2,128,256]{2,1,0:T(8,128)S(1)} %get-tuple-element.52), channel_id=1, source_target_pairs={{0,8},{8,0},{16,24},{24,16},{1,9},{9,1},{17,25},{25,17},{2,10},{10... | collective-permute-start | bytes 786440 | tf_op jit(solution)/shard_map/ppermute | solution.py:385
  28.9 7.0 %collective-permute-start.10 = (f32[392,128]{1,0:T(8,128)S(1)}, f32[392,128]{1,0:T(8,128)S(1)}, u32[]{:S(2)}, u32[]{:S(2)}) collective-permute-start(f32[392,128]{1,0:T(8,128)S(1)} %get-tuple-element.50), channel_id=1, source_target_pairs={{0,16},{8,24},{16,0},{24,8},{1,17},{9,25},{17,1},{25,9},{2,18},{10... | collective-permute-start | bytes 602120 | tf_op jit(solution)/shard_map/ppermute | solution.py:385
  35.9 3.6 %collective-permute-start.13 = (f32[200,128]{1,0:T(8,128)S(1)}, f32[200,128]{1,0:T(8,128)S(1)}, u32[]{:S(2)}, u32[]{:S(2)}) collective-permute-start(f32[200,128]{1,0:T(8,128)S(1)} %get-tuple-element.56), channel_id=1, source_target_pairs={{0,1},{1,0},{2,3},{3,2},{4,5},{5,4},{6,7},{7,6},{8,9},{9,8},{10,11... | collective-permute-start | bytes 307208 | tf_op jit(solution)/shard_map/ppermute | solution.py:385
  39.5 8.5 %collective-permute-start.16 = (f32[2,2,128,128]{3,2,1,0:T(8,128)S(1)}, f32[2,2,128,128]{3,2,1,0:T(8,128)S(1)}, u32[]{:S(2)}, u32[]{:S(2)}) collective-permute-start(f32[2,2,128,128]{3,2,1,0:T(8,128)S(1)} %collective-permute-done.11), channel_id=1, source_target_pairs={{24,8},{0,16},{16,24},{8,0},{25,9},{1,17},{17,25},{9,1},{26,10},{2... | collective-permute-start | bytes 786440 | tf_op jit(solution)/shard_map/ppermute | solution.py:449
  40.9 3.5 %collective-permute-start.14 = (f32[200,128]{1,0:T(8,128)S(1)}, f32[200,128]{1,0:T(8,128)S(1)}, u32[]{:S(2)}, u32[]{:S(2)}) collective-permute-start(f32[200,128]{1,0:T(8,128)S(1)} %add.63), channel_id=1, source_target_pairs={{0,2},{1,3},{2,0},{3,1},{4,6},{5,7},{6,4},{7,5},{8,10},{9,11},{10,... | collective-permute-start | bytes 307208 | tf_op jit(solution)/shard_map/ppermute | solution.py:385
  44.4 3.6 %collective-permute-start.15 = (f32[200,128]{1,0:T(8,128)S(1)}, f32[200,128]{1,0:T(8,128)S(1)}, u32[]{:S(2)}, u32[]{:S(2)}) collective-permute-start(f32[200,128]{1,0:T(8,128)S(1)} %add.64), channel_id=1, source_target_pairs={{0,6},{1,7},{2,4},{3,5},{4,2},{5,3},{6,0},{7,1},{8,14},{9,15},{10,... | collective-permute-start | bytes 307208 | tf_op jit(solution)/shard_map/ppermute | solution.py:385
  45.8 4.6 %collective-permute-start.18 = (f32[2,2,128,128]{3,2,1,0:T(8,128)S(1)}, f32[2,2,128,128]{3,2,1,0:T(8,128)S(1)}, u32[]{:S(2)}, u32[]{:S(2)}) collective-permute-start(f32[2,2,128,128]{3,2,1,0:T(8,128)S(1)} %get-tuple-element.63), channel_id=1, source_target_pairs={{0,8},{8,0},{16,24},{24,16},{1,9},{9,1},{17,25},{25,17},{2,10},{10... | collective-permute-start | bytes 786440 | tf_op jit(solution)/shard_map/ppermute | solution.py:385
  48.0 6.1 %collective-permute-start.17 = (f32[2,64,128]{2,1,0:T(8,128)S(1)}, f32[2,64,128]{2,1,0:T(8,128)S(1)}, u32[]{:S(2)}, u32[]{:S(2)}) collective-permute-start(f32[2,64,128]{2,1,0:T(8,128)S(1)} %fusion.2), channel_id=1, source_target_pairs={{0,1},{1,0},{2,3},{3,2},{4,5},{5,4},{6,7},{7,6},{8,9},{9,8},{10,11... | collective-permute-start | bytes 196616 | tf_op jit(solution)/shard_map/ppermute | solution.py:385
  50.5 3.9 %collective-permute-start.19 = (f32[2,128,128]{2,1,0:T(8,128)S(1)}, f32[2,128,128]{2,1,0:T(8,128)S(1)}, u32[]{:S(2)}, u32[]{:S(2)}) collective-permute-start(f32[2,128,128]{2,1,0:T(8,128)S(1)} %get-tuple-element.75), channel_id=1, source_target_pairs={{0,1},{1,0},{2,3},{3,2},{4,5},{5,4},{6,7},{7,6},{8,9},{9,8},{10,11... | collective-permute-start | bytes 393224 | tf_op jit(solution)/shard_map/ppermute | solution.py:458
  50.6 13.8 %collective-permute-start.22 = (f32[2,128,256]{2,1,0:T(8,128)S(1)}, f32[2,128,256]{2,1,0:T(8,128)S(1)}, u32[]{:S(2)}, u32[]{:S(2)}) collective-permute-start(f32[2,128,256]{2,1,0:T(8,128)S(1)} %collective-permute-done.12), channel_id=1, source_target_pairs={{24,8},{0,16},{16,24},{8,0},{25,9},{1,17},{17,25},{9,1},{26,10},{2... | collective-permute-start | bytes 786440 | tf_op jit(solution)/shard_map/ppermute | solution.py:450
  54.4 10.0 %collective-permute-start.20 = (f32[2,128,128]{2,1,0:T(8,128)S(1)}, f32[2,128,128]{2,1,0:T(8,128)S(1)}, u32[]{:S(2)}, u32[]{:S(2)}) collective-permute-start(f32[2,128,128]{2,1,0:T(8,128)S(1)} %maximum_select_fusion.2), channel_id=1, source_target_pairs={{0,16},{8,24},{16,0},{24,8},{1,17},{9,25},{17,1},{25,9},{2,18},{10... | collective-permute-start | bytes 393224 | tf_op jit(solution)/shard_map/ppermute | solution.py:385
  57.6 6.8 %collective-permute-start.21 = (f32[2,128,128]{2,1,0:T(8,128)S(1)}, f32[2,128,128]{2,1,0:T(8,128)S(1)}, u32[]{:S(2)}, u32[]{:S(2)}) collective-permute-start(f32[2,128,128]{2,1,0:T(8,128)S(1)} %get-tuple-element.74), channel_id=1, source_target_pairs={{1,2},{3,4},{5,6},{2,1},{4,3},{6,5},{9,10},{11,12},{13,14},{10,9},... | collective-permute-start | bytes 393224 | tf_op jit(solution)/shard_map/ppermute | solution.py:459
  60.4 9.2 %collective-permute-start.9 = (f32[2,128,256]{2,1,0:T(8,128)S(1)}, f32[2,128,256]{2,1,0:T(8,128)S(1)}, u32[]{:S(2)}, u32[]{:S(2)}) collective-permute-start(f32[2,128,256]{2,1,0:T(8,128)S(1)} %get-tuple-element.44), channel_id=1, source_target_pairs={{0,8},{8,0},{16,24},{24,16},{1,9},{9,1},{17,25},{25,17},{2,10},{10... | collective-permute-start | bytes 786440 | tf_op jit(solution)/shard_map/ppermute | solution.py:385
  64.4 6.3 %collective-permute-start.23 = (f32[2,256,128]{2,1,0:T(8,128)S(1)}, f32[2,256,128]{2,1,0:T(8,128)S(1)}, u32[]{:S(2)}, u32[]{:S(2)}) collective-permute-start(f32[2,256,128]{2,1,0:T(8,128)S(1)} %maximum_select_fusion.1), channel_id=1, source_target_pairs={{0,8},{8,0},{16,24},{24,16},{1,9},{9,1},{17,25},{25,17},{2,10},{10... | collective-permute-start | bytes 786440 | tf_op jit(solution)/shard_map/ppermute | solution.py:385

commit v3 on v2

--- a/solution.py
+++ b/solution.py
@@ -18,13 +18,19 @@
 VMEM_LIMIT = 20 * 1024 * 1024
 
 
-def dft_table(width):
-    counter = np.arange(width)
-    angle = (counter[:, None] * counter[None, :] % width) * (2.0 * math.pi / width)
-    table = np.concatenate([np.cos(angle), np.sin(angle)], 1) / math.sqrt(width)
-    high = table.astype(ml_dtypes.bfloat16)
-    low = (table - high.astype(np.float64)).astype(ml_dtypes.bfloat16)
-    return np.stack([high, low])
+def dft_tables(width):
+    half = width // 2
+    counter = np.arange(half)
+    tables = []
+    for odd in range(2):
+        phase = counter[:, None] * (2 * counter[None, :] + odd) % width
+        angle = phase * (2.0 * math.pi / width)
+        real, imag = np.cos(angle) / math.sqrt(width), -np.sin(angle) / math.sqrt(width)
+        tables.append(np.block([[real, imag], [-imag, real]]))
+    tables = np.stack(tables + [table.T for table in tables])
+    high = tables.astype(ml_dtypes.bfloat16)
+    low = (tables - high.astype(np.float64)).astype(ml_dtypes.bfloat16)
+    return np.stack([high, low], 1)
 
 
 def halves(value):
@@ -37,10 +43,13 @@
     return dot(left[0], right[0]) + (dot(left[1], right[0]) + dot(left[0], right[1]))
 
 
-def turn(first, second, third, ref, at):
-    for place, block in zip(at, (first, second, third)):
-        for half_at, half in enumerate(halves(block)):
-            ref[half_at, *place] = half
+def keep(ref, rows, lanes, value):
+    for place, half in enumerate(halves(value)):
+        ref[place, rows, lanes] = half
+
+
+def product_of(left, right):
+    return product((left[0], left[1]), (right[0], right[1]))
 
 
 def split_start(start, step, last):
@@ -142,7 +151,7 @@
             pltpu.VMEM((2 * tile_r + width + SUBLANES, 2 * tile_c + width), jnp.float32)
         ],
         compiler_params=pltpu.CompilerParams(vmem_limit_bytes=VMEM_LIMIT),
-        cost_estimate=pl.CostEstimate(flops=4000000, bytes_accessed=800000, transcendentals=0),
+        cost_estimate=pl.CostEstimate(flops=40000000, bytes_accessed=8000000, transcendentals=0),
     )(offsets, counts, probe)
 
 
@@ -155,13 +164,10 @@
 
 
 def delta_kernel(
-    offsets, counts, probe, magnitudes, table, own, rim, near, near_rim, far, far_rim,
-    kept, given, own_probe, delta, ext, patches, left, right, stack, basis_in, measured, arrived,
+    offsets, counts, probe, magnitudes, tables,
+    own, pair_rim, other_rim, near, near_pair, near_other, far, far_pair, far_other,
+    kept, given, own_probe, delta, ext, patches, tall_even, tall_odd, wide_even, wide_odd,
 ):
-    table_copy = pltpu.make_async_copy(table, basis_in, arrived.at[0])
-    measured_copy = pltpu.make_async_copy(magnitudes, measured, arrived.at[1])
-    table_copy.start()
-    measured_copy.start()
     slots, width = magnitudes.shape[0], magnitudes.shape[1]
     half = width // 2
     tile_r, tile_c = own.shape[1:]
@@ -175,21 +181,25 @@
     other_col = pl.multiple_of(col_odd * (tile_c + half), half)
     far_at = row_place + 2 * row_odd - 1
     inside = (far_at >= 0) & (far_at < lax.axis_size("row"))
+    strips = (
+        (half, True, own, pair_rim, other_rim),
+        (near_row, True, near, near_pair, near_other),
+        (far_row, inside, far, far_pair, far_other),
+    )
     for part in range(2):
-        for rows, mid, edge in ((half, own, rim), (near_row, near, near_rim)):
-            at = pl.ds(rows, tile_r)
-            ext[part, at, half : half + tile_c] = mid[part]
-            ext[part, at, pl.ds(pair_col, half)] = edge[0, part]
-            ext[part, at, pl.ds(other_col, half)] = edge[1, part]
-        at = pl.ds(far_row, tile_r)
-        ext[part, at, half : half + tile_c] = jnp.where(inside, far[part], 0.0)
-        ext[part, at, pl.ds(pair_col, half)] = jnp.where(inside, far_rim[0, part], 0.0)
-        ext[part, at, pl.ds(other_col, half)] = jnp.where(inside, far_rim[1, part], 0.0)
+        for row, valid, *blocks in strips:
+            at = pl.ds(row, tile_r)
+            mid, pair, other = (
+                block[part] if valid is True else jnp.where(valid, block[part], 0.0)
+                for block in blocks
+            )
+            ext[part, at, half : half + tile_c] = mid
+            ext[part, at, pl.ds(pair_col, half)] = pair
+            ext[part, at, pl.ds(other_col, half)] = other
     live_count = counts[row_place, col_place]
     probe_real, probe_imag = probe[0], probe[1]
-    first = slice(0, 2 * width)
-    second = slice(width, 3 * width)
-    places = [slice(k * width, (k + 1) * width) for k in range(3)]
+    right_even, right_odd, left_even, left_odd = (tables.at[k] for k in range(4))
+    low, high = slice(0, half), slice(half, width)
     for slot in range(slots):
         block, row_shift, lane_shift = patch_block(
             offsets, row_place, col_place, slot, half, tile_r, width
@@ -197,40 +207,54 @@
         for part in range(2):
             patches[slot, part] = cut(ext[part, *block], row_shift, lane_shift)
         patch_real, patch_imag = patches[slot, 0], patches[slot, 1]
-        real = probe_real * patch_real - probe_imag * patch_imag
-        imag = probe_real * patch_imag + probe_imag * patch_real
         at = slice(slot * width, (slot + 1) * width)
-        turn(real, imag, -real, left, [(at, place) for place in places])
-    table_copy.wait()
-    stack[:, :width] = basis_in[:, :, :width]
-    stack[:, width:] = basis_in[:, :, width:]
-    basis = (stack[0], stack[1])
-    basis_left = (basis_in[0], basis_in[1])
-    real = product((left[0, :, first], left[1, :, first]), basis)
-    imag = product((left[0, :, second], left[1, :, second]), basis)
-    measured_copy.wait()
-    for slot in range(slots):
-        at = slice(slot * width, (slot + 1) * width)
-        turn(real[at], imag[at], -real[at], right, [(place,) for place in places])
-        far_real = product(basis_left, (right[0, first], right[1, first]))
-        far_imag = product(basis_left, (right[0, second], right[1, second]))
-        inverse = jnp.minimum(
-            lax.rsqrt(far_real * far_real + far_imag * far_imag), 1.0 / modulus_floor
-        )
-        factor = measured[slot] * inverse - 1.0
-        back_real, back_imag = far_real * factor, far_imag * factor
-        turn(back_imag, back_real, -back_imag, left, [(at, place) for place in places])
-    imag = product((left[0, :, first], left[1, :, first]), basis)
-    real = product((left[0, :, second], left[1, :, second]), basis)
+        for part, wave in (
+            (low, probe_real * patch_real - probe_imag * patch_imag),
+            (high, probe_real * patch_imag + probe_imag * patch_real),
+        ):
+            keep(tall_even, at, part, wave[:, low] + wave[:, high])
+            keep(tall_odd, at, part, wave[:, low] - wave[:, high])
+    inner = (product_of(tall_even, right_even), product_of(tall_odd, right_odd))
+    for slot in range(slots):
+        top = slice(slot * width, slot * width + half)
+        bottom = slice(slot * width + half, (slot + 1) * width)
+        for odd in range(2):
+            at = slice(slot * width + odd * half, slot * width + (odd + 1) * half)
+            for part in (low, high):
+                upper, lower = inner[odd][top, part], inner[odd][bottom, part]
+                keep(wide_even, part, at, upper + lower)
+                keep(wide_odd, part, at, upper - lower)
+    outer = (product_of(left_even, wide_even), product_of(left_odd, wide_odd))
+    for slot in range(slots):
+        lanes = slice(slot * width, (slot + 1) * width)
+        for odd in range(2):
+            far_real, far_imag = outer[odd][low, lanes], outer[odd][high, lanes]
+            inverse = jnp.minimum(
+                lax.rsqrt(far_real * far_real + far_imag * far_imag), 1.0 / modulus_floor
+            )
+            factor = magnitudes[slot, odd * half : (odd + 1) * half] * inverse - 1.0
+            at = slice(slot * width + odd * half, slot * width + (odd + 1) * half)
+            for part, back in ((low, far_real * factor), (high, far_imag * factor)):
+                keep(tall_even, at, part, back[:, low])
+                keep(tall_odd, at, part, back[:, high])
+    inner = (product_of(tall_even, left_even), product_of(tall_odd, left_odd))
+    for slot in range(slots):
+        for odd, ref in enumerate((wide_even, wide_odd)):
+            at = slice(slot * width + odd * half, slot * width + (odd + 1) * half)
+            for part in (low, high):
+                one, other = inner[0][at, part], inner[1][at, part]
+                keep(ref, part, slice(slot * width, slot * width + half), one + other)
+                keep(ref, part, slice(slot * width + half, (slot + 1) * width), one - other)
+    outer = (product_of(right_even, wide_even), product_of(right_odd, wide_odd))
     sums = [jnp.zeros((width, width), jnp.float32)] * 3
     for slot in range(slots):
-        at = slice(slot * width, (slot + 1) * width)
-        turn(imag[at], real[at], -imag[at], right, [(place,) for place in places])
         live = jnp.where(slot < live_count, 1.0, 0.0)
-        delta_imag = product(basis_left, (right[0, first], right[1, first])) * live
-        delta_real = product(basis_left, (right[0, second], right[1, second])) * live
-        delta[slot, 0] = delta_real
-        delta[slot, 1] = delta_imag
+        lanes = slice(slot * width, (slot + 1) * width)
+        for part, rows in enumerate((low, high)):
+            one, other = outer[0][rows, lanes], outer[1][rows, lanes]
+            delta[slot, part, low] = (one + other) * live
+            delta[slot, part, high] = (one - other) * live
+        delta_real, delta_imag = delta[slot, 0], delta[slot, 1]
         patch_real, patch_imag = patches[slot, 0], patches[slot, 1]
         sums = [
             sums[0] + (patch_real * delta_real + patch_imag * delta_imag),
@@ -239,25 +263,27 @@
         ]
     even = row_odd == 0
     for layer in range(3):
-        low, high = lane_groups(sums[layer])
-        kept[layer * width : (layer + 1) * width] = jnp.where(even, low, high)
-        given[layer * width : (layer + 1) * width] = jnp.where(even, high, low)
+        one, other = lane_groups(sums[layer])
+        kept[layer * width : (layer + 1) * width] = jnp.where(even, one, other)
+        given[layer * width : (layer + 1) * width] = jnp.where(even, other, one)
     total = jnp.full((SUBLANES, LANES), jnp.sum(sums[2]))
     kept[3 * width :] = total
     given[3 * width :] = total
     size = own_probe.shape[1]
     row = pl.multiple_of(lax.rem(row_place // 2, 2) * (2 * size) + col_odd * size, size)
     for part in range(2):
-        low, high = lane_groups(probe[part, pl.ds(row, size), :])
-        own_probe[part] = jnp.where(even, low, high)
+        one, other = lane_groups(probe[part, pl.ds(row, size), :])
+        own_probe[part] = jnp.where(even, one, other)
 
 
 def place_kernel(
-    offsets, probe, delta, center, close, onward, center_rim, close_rim, onward_rim, ext
+    offsets, probe, delta, *blocks_and_ext
 ):
+    *blocks, ext = blocks_and_ext
     slots, width = delta.shape[0], delta.shape[2]
     half = width // 2
-    tile_r, tile_c = center.shape[1:]
+    tile_r = blocks[0].shape[1]
+    tile_c = ext.shape[2] - 2 * half
     row_place = lax.axis_index("row")
     col_place = lax.axis_index("col")
     row_odd = lax.rem(row_place, 2)
@@ -277,19 +303,70 @@
     far_row = pl.multiple_of(row_odd * (tile_r + half), half)
     pair_col = pl.multiple_of((1 - col_odd) * (tile_c + half), half)
     other_col = pl.multiple_of(col_odd * (tile_c + half), half)
-    for row, mid, rim in (
-        (half, center, center_rim),
-        (near_row, close, close_rim),
-        (far_row, onward, onward_rim),
-    ):
+    for k, row in enumerate((half, near_row, far_row)):
+        low, high, pair, other = blocks[4 * k : 4 * k + 4]
         at = pl.ds(row, tile_r)
-        mid[...] = ext[:, at, half : half + tile_c]
-        rim[0] = ext[:, at, pl.ds(pair_col, half)]
-        rim[1] = ext[:, at, pl.ds(other_col, half)]
-
-
-def exit_update(offsets, counts, probe, magnitudes, own, rim, near, near_rim, far, far_rim):
+        low[...] = ext[:, at, half : half + tile_c // 2]
+        high[...] = ext[:, at, half + tile_c // 2 : half + tile_c]
+        pair[...] = ext[:, at, pl.ds(pair_col, half)]
+        other[...] = ext[:, at, pl.ds(other_col, half)]
+
+
+def stage_kernel(magnitudes, tables, ordered, held, measured, arrived):
     slots, width = magnitudes.shape[:2]
+    copies = [
+        pltpu.make_async_copy(tables, held, arrived.at[0]),
+        pltpu.make_async_copy(magnitudes, measured, arrived.at[1]),
+    ]
+    for copy in copies:
+        copy.start()
+    line = lax.broadcasted_iota(jnp.int32, (width, width), 0)
+    place = lax.broadcasted_iota(jnp.int32, (width, width), 1)
+
+    def chosen(here, there):
+        source = jnp.where(here < width // 2, 2 * here, 2 * here - (width - 1))
+        return jnp.where(source == there, 1.0, 0.0).astype(jnp.bfloat16)
+
+    by_row, by_lane = chosen(line, place), chosen(place, line)
+    copies[1].wait()
+    for slot in range(slots):
+        rest = measured[slot]
+        total = jnp.zeros((width, width), jnp.float32)
+        for _ in range(3):
+            piece = rest.astype(jnp.bfloat16)
+            rest = rest - piece.astype(jnp.float32)
+            piece = jnp.dot(by_row, piece, preferred_element_type=jnp.float32)
+            total += jnp.dot(
+                piece.astype(jnp.bfloat16), by_lane, preferred_element_type=jnp.float32
+            )
+        ordered[slot] = total
+    copies[0].wait()
+
+
+def stage(magnitudes):
+    width = magnitudes.shape[-1]
+    hbm = pl.BlockSpec(memory_space=pltpu.HBM)
+    vmem = pl.BlockSpec(memory_space=pltpu.VMEM)
+    return pl.pallas_call(
+        stage_kernel,
+        out_shape=[
+            jax.ShapeDtypeStruct(magnitudes.shape, jnp.float32),
+            jax.ShapeDtypeStruct((4, 2, width, width), jnp.bfloat16),
+        ],
+        in_specs=[hbm] * 2,
+        out_specs=[vmem] * 2,
+        scratch_shapes=[
+            pltpu.VMEM(magnitudes.shape, jnp.float32),
+            pltpu.SemaphoreType.DMA((2,)),
+        ],
+        compiler_params=pltpu.CompilerParams(vmem_limit_bytes=VMEM_LIMIT),
+        cost_estimate=pl.CostEstimate(flops=400000000, bytes_accessed=3000000, transcendentals=0),
+    )(in_hbm(magnitudes), in_hbm(jnp.asarray(dft_tables(width))))
+
+
+def exit_update(offsets, counts, probe, staged, blocks):
+    slots, width = staged[0].shape[:2]
+    own = blocks[0]
     half = width // 2
     tile_r, tile_c = own.shape[1:]
     smem = pl.BlockSpec(memory_space=pltpu.SMEM)
@@ -302,26 +379,62 @@
             jax.ShapeDtypeStruct((2, width // 4, LANES), jnp.float32),
             jax.ShapeDtypeStruct((slots, 2, width, width), jnp.float32),
         ],
-        in_specs=[smem, smem, vmem] + [pl.BlockSpec(memory_space=pltpu.HBM)] * 2 + [vmem] * 6,
+        in_specs=[smem, smem] + [vmem] * 12,
         out_specs=[vmem] * 4,
         scratch_shapes=[
             pltpu.VMEM((2, tile_r + 2 * half + SUBLANES, tile_c + 2 * half), jnp.float32),
             pltpu.VMEM((slots, 2, width, width), jnp.float32),
-            pltpu.VMEM((2, slots * width, 3 * width), jnp.bfloat16),
-            pltpu.VMEM((2, 3 * width, width), jnp.bfloat16),
-            pltpu.VMEM((2, 2 * width, width), jnp.bfloat16),
-            pltpu.VMEM((2, width, 2 * width), jnp.bfloat16),
-            pltpu.VMEM((slots, width, width), jnp.float32),
-            pltpu.SemaphoreType.DMA((2,)),
+            pltpu.VMEM((2, slots * width, width), jnp.bfloat16),
+            pltpu.VMEM((2, slots * width, width), jnp.bfloat16),
+            pltpu.VMEM((2, width, slots * width), jnp.bfloat16),
+            pltpu.VMEM((2, width, slots * width), jnp.bfloat16),
         ],
         compiler_params=pltpu.CompilerParams(vmem_limit_bytes=VMEM_LIMIT),
         cost_estimate=pl.CostEstimate(
             flops=3200000000, bytes_accessed=8000000, transcendentals=131072
         ),
-    )(
-        offsets, counts, probe, in_hbm(magnitudes), in_hbm(jnp.asarray(dft_table(width))),
-        *map(in_vmem, (own, rim, near, near_rim, far, far_rim)),
-    )
+    )(offsets, counts, probe, *map(in_vmem, staged), *map(in_vmem, blocks))
+
+
+def finish_kernel(*refs):
+    (
+        specimen, light, low, high, close_low, close_high, far_low, far_high, pair, other,
+        fresh, got, specimen_next, probe_next,
+    ) = refs
+    half = pair.shape[2]
+    row_place = lax.axis_index("row")
+    col_place = lax.axis_index("col")
+    row_odd = lax.rem(row_place, 2)
+    col_odd = lax.rem(col_place, 2)
+    far_at = row_place + 2 * row_odd - 1
+    inside = (far_at >= 0) & (far_at < lax.axis_size("row"))
+    for part in range(2):
+        sides = (
+            (low, close_low, far_low, jnp.where(col_odd == 0, other[part], pair[part])),
+            (high, close_high, far_high, jnp.where(col_odd == 0, pair[part], other[part])),
+        )
+        for side, (own, close, far, rim) in enumerate(sides):
+            at = slice(side * half, (side + 1) * half)
+            total = own[part] + close[part] + jnp.where(inside, far[part], 0.0) + rim
+            specimen_next[part, :, at] = specimen[part, :, at] + total / light[:, at]
+        mine, theirs = fresh[part], got[part]
+        probe_next[part, :, :LANES] = jnp.where(row_odd == 0, mine, theirs)
+        probe_next[part, :, LANES:] = jnp.where(row_odd == 0, theirs, mine)
+
+
+def finish(specimen, probe, *values):
+    vmem = pl.BlockSpec(memory_space=pltpu.VMEM)
+    return pl.pallas_call(
+        finish_kernel,
+        out_shape=[
+            jax.ShapeDtypeStruct(specimen.shape, jnp.float32),
+            jax.ShapeDtypeStruct(probe.shape, jnp.float32),
+        ],
+        in_specs=[vmem] * (1 + len(values)),
+        out_specs=[vmem] * 2,
+        compiler_params=pltpu.CompilerParams(vmem_limit_bytes=VMEM_LIMIT),
+        cost_estimate=pl.CostEstimate(flops=1000000, bytes_accessed=3000000, transcendentals=0),
+    )(*map(in_vmem, (specimen, *values)))
 
 
 def in_hbm(value):
@@ -366,13 +479,13 @@
     half = width // 2
     smem = pl.BlockSpec(memory_space=pltpu.SMEM)
     vmem = pl.BlockSpec(memory_space=pltpu.VMEM)
-    middle = jax.ShapeDtypeStruct((2, tile_r, tile_c), jnp.float32)
-    rim = jax.ShapeDtypeStruct((2, 2, tile_r, half), jnp.float32)
+    middle = jax.ShapeDtypeStruct((2, tile_r, tile_c // 2), jnp.float32)
+    rim = jax.ShapeDtypeStruct((2, tile_r, half), jnp.float32)
     return pl.pallas_call(
         place_kernel,
-        out_shape=[middle] * 3 + [rim] * 3,
+        out_shape=[middle, middle, rim, rim] * 3,
         in_specs=[smem, vmem, vmem],
-        out_specs=[vmem] * 6,
+        out_specs=[vmem] * 12,
         scratch_shapes=[
             pltpu.VMEM((2, tile_r + 2 * half + SUBLANES, tile_c + 2 * half), jnp.float32),
         ],
@@ -400,20 +513,25 @@
     toward += [(rows - 1, rows - 2), (0, 1)]
     onward_pairs = [(target, source) for source, target in toward]
 
+    tie = lax.optimization_barrier
+
+    def core(values):
+        return [exchange(value, "row", rows, 1) for value in values]
+
     low, high = specimen[:, :, :half], specimen[:, :, tile_c - half :]
     pair_rim = lax.ppermute(jnp.where(col_odd == 0, high, low), "col", pairs)
     other_rim = lax.ppermute(jnp.where(col_odd == 0, low, high), "col", others)
-    beyond = lax.ppermute(specimen, "row", toward)
-    rim = jnp.stack([pair_rim, other_rim])
-    beyond_rim = lax.ppermute(rim, "row", toward)
-    near = exchange(specimen, "row", rows, 1)
-    near_rim = exchange(rim, "row", rows, 1)
-    far = exchange(beyond, "row", rows, 1)
-    far_rim = exchange(beyond_rim, "row", rows, 1)
-
+    late, pair_rim = tie((magnitudes[0, 0], pair_rim))
+    staged = stage(late)
+    beyond = [lax.ppermute(block, "row", toward) for block in (specimen, pair_rim)]
+    other_rim, staged, beyond = tie((other_rim, staged, beyond))
+    own = [specimen, pair_rim, other_rim]
+    beyond += [lax.ppermute(other_rim, "row", toward)]
+    probe_late, other_rim = tie((probe_field, other_rim))
+    light = lighting(scan_offsets, live_counts, probe_late, tile_r, tile_c)
+    beyond[2], light = tie((beyond[2], light))
     kept, given, own_probe, delta = exit_update(
-        scan_offsets, live_counts, probe_field, magnitudes[0, 0],
-        specimen, rim, near, near_rim, far, far_rim,
+        scan_offsets, live_counts, probe_field, staged, own + core(own) + core(beyond)
     )
 
     def pick(condition, first, second):
@@ -428,53 +546,45 @@
             jnp.concatenate([got, value], 1),
         )
 
-    tie = lax.optimization_barrier
-    got = exchange(given, "row", rows, 1)
-    center, close, onward, center_rim, close_rim, onward_rim = place(
-        scan_offsets, probe_field, delta, tile_r, tile_c
+    kept, given = fold(kept, exchange(given, "row", rows, 1), "row", 2)
+    given, delta = tie((given, delta))
+    parts = place(scan_offsets, probe_field, delta, tile_r, tile_c)
+    center, close, onward = parts[:4], parts[4:8], parts[8:]
+    got_close, got_onward = core(close), core(onward)
+    got = exchange(given, "row", rows, 2)
+    kept, given = fold(kept, got, "col", 1)
+    given, got_close, got_onward = tie((given, got_close, got_onward))
+    beyond = [lax.ppermute(block, "row", onward_pairs) for block in got_onward]
+    inside = (row_place + 2 * row_odd - 1 >= 0) & (row_place + 2 * row_odd - 1 < rows)
+    value = kept + exchange(given, "col", cols, 1)
+    value, *beyond[2:] = tie((value, *beyond[2:]))
+    pair_part, other_part = (
+        first + second + pick(inside, third, 0.0)
+        for first, second, third in zip(center[2:], got_close[2:], beyond[2:])
     )
-    got, close, onward, close_rim, onward_rim = tie((got, close, onward, close_rim, onward_rim))
-    kept, given = fold(kept, got, "row", 2)
-    got_close_rim = exchange(close_rim, "row", rows, 1)
-    got_onward_rim = exchange(onward_rim, "row", rows, 1)
-    got_close = exchange(close, "row", rows, 1)
-    got_onward = exchange(onward, "row", rows, 1)
-    probe_late, given = tie((probe_field, given))
-    light = lighting(scan_offsets, live_counts, probe_late, tile_r, tile_c)
-    got = exchange(given, "row", rows, 2)
-    got, got_onward_rim, got_onward, light = tie((got, got_onward_rim, got_onward, light))
-    kept, given = fold(kept, got, "col", 1)
-    value = kept + exchange(given, "col", cols, 1)
-    value, got_onward_rim, got_onward = tie((value, got_onward_rim, got_onward))
-    beyond_rim = lax.ppermute(got_onward_rim, "row", onward_pairs)
-    beyond = lax.ppermute(got_onward, "row", onward_pairs)
-    for bit in (1 << k for k in range(1, cols.bit_length() - 1)):
+    other_part = lax.ppermute(other_part, "col", others)
+    filled = jnp.concatenate([value, jnp.zeros((64, LANES), jnp.float32)])
+    value = value + exchange(filled, "col", cols, 2)[: value.shape[0]]
+    value, beyond = tie((value, beyond))
+    for bit in (1 << k for k in range(2, cols.bit_length() - 1)):
         value = value + exchange(value, "col", cols, 2 * bit - 2)
     for bit in (1 << k for k in range(2, rows.bit_length() - 1)):
         value = value + exchange(value, "row", rows, bit)
-    value, beyond_rim = tie((value, beyond_rim))
-    inside = (row_place + 2 * row_odd - 1 >= 0) & (row_place + 2 * row_odd - 1 < rows)
-    rim_sum = center_rim + got_close_rim + pick(inside, beyond_rim, 0.0)
-    pair_part = lax.ppermute(rim_sum[0], "col", pairs)
-    other_part = lax.ppermute(rim_sum[1], "col", others)
+    value, other_part, pair_part = tie((value, other_part, pair_part))
     size = own_probe.shape[1]
     real, imag, weight, total = (value[k * size : (k + 1) * size] for k in range(4))
     update = jnp.stack([real, imag]) / (weight + probe_damping * (total[:1] / (width * width)))
     fresh = own_probe + update
     fresh = join(fresh, "col", cols, 1)
     fresh, pair_part = tie((fresh, pair_part))
+    pair_part = lax.ppermute(pair_part, "col", pairs)
     fresh = join(fresh, "row", rows, 2)
-    fresh, other_part, beyond = tie((fresh, other_part, beyond))
+    fresh, pair_part = tie((fresh, pair_part))
     got = exchange(fresh, "row", rows, 1)
-    low_part = pick(col_odd == 0, other_part, pair_part)
-    high_part = pick(col_odd == 0, pair_part, other_part)
-    middle = center + got_close + pick(inside, beyond, 0.0)
-    middle = middle + jnp.concatenate([low_part, high_part], 2)
-    specimen_next = specimen + middle / light
-    probe_next = pick(
-        row_odd == 0, jnp.concatenate([fresh, got], 2), jnp.concatenate([got, fresh], 2)
+    return finish(
+        specimen, probe_field, light, *center[:2], *got_close[:2], *beyond[:2],
+        pair_part, other_part, fresh, got,
     )
-    return (specimen_next, probe_next)
 
 
 def solution(mesh):

time: 71.8 us -> 67.8 us (0.944)
  the two profiles are of different devices: /device:TPU:11 before, /device:TPU:0 now
where the time goes in v3:
time: 67.8 us; the launch traced here: 67.6 us
  waiting for transfers between devices  34.2 us (50%)
  starting transfers between devices  19.8 us (29%)
  Pallas kernels  11.4 us (17%)
  other arithmetic  1.19 us (2%)
  between operations  0.88 us (1%)
    ppermute x22, waiting for transfers between devices, exchange(): return lax.ppermute(value, axis, [(i, i ^ bit) for i in range(count)])  25.9 us
    ppermute x22, starting transfers between devices, exchange(): return lax.ppermute(value, axis, [(i, i ^ bit) for i in range(count)])  13.4 us
    pallas_call x1, Pallas kernels, exit_update(): pl.pallas_call(delta_kernel, out_shape=[jax.ShapeDtypeStruct((3 * width +...  4.32 us
    ppermute x1, starting transfers between devices, shards(): pair_rim = lax.ppermute(jnp.where(col_odd == 0, high, low), 'col', pairs)  3.03 us
    ppermute x1, waiting for transfers between devices, shards(): pair_rim = lax.ppermute(jnp.where(col_odd == 0, high, low), 'col', pairs)  2.82 us
    ppermute x2, waiting for transfers between devices, shards(): lax.ppermute(block, 'row', toward)  2.42 us
    pallas_call x1, Pallas kernels, lighting(): pl.pallas_call(lighting_kernel, out_shape=jax.ShapeDtypeStruct((tile_r, t...  2.18 us
    pallas_call x1, Pallas kernels, stage(): pl.pallas_call(stage_kernel, out_shape=[jax.ShapeDtypeStruct(magnitudes.s...  2.13 us
  transfers between devices with their start and end apart: 33, of which 17 were waited for; matrix products, arithmetic and copies ran while one was open for 0% of the time, Pallas kernels for 9%

profile of v3, /device:TPU:0, one launch (start us, length us, event | category | flops | bytes accessed | tf_op | source)
XLA Modules:
  0.0 67.6 jit_solution(12609668998432929592)
XLA Ops:
  0.7 1.0 %slice_select_fusion = (f32[2,128,128]{2,1,0:T(8,128)S(1)}, f32[2,128,128]{2,1,0:T(8,128)S(1)}) fusion(f32[2,128,256]{2,1,0:T(8,128)} %refs_0_.1, pred[]{:T(512)S(6)} %eq.13), kind=kLoop, calls=%fused_computation.4 | loop fusion | flops 65536 | bytes 524289 | tf_op jit(solution)/shard_map/jit(_where)/select_n | solution.py:522
  1.7 3.0 %collective-permute-start.1 = (f32[2,128,128]{2,1,0:T(8,128)S(1)}, f32[2,128,128]{2,1,0:T(8,128)S(1)}, u32[]{:S(2)}, u32[]{:S(2)}) collective-permute-start(f32[2,128,128]{2,1,0:T(8,128)S(1)} %get-tuple-element.114), channel_id=1, source_target_pairs={{0,1},{1,0},{2,3},{3,2},{4,5},{5,4},{6,7},{7,6},{8,9},{9,8},{10,11... | collective-permute-start | bytes 393224 | tf_op jit(solution)/shard_map/ppermute | solution.py:522
  4.7 0.7 collective-permute-start
  5.4 2.8 %collective-permute-done.1.pair_rim = f32[2,128,128]{2,1,0:T(8,128)S(1)} collective-permute-done((f32[2,128,128]{2,1,0:T(8,128)S(1)}, f32[2,128,128]{2,1,0:T(8,128)S(1)}, u32[]{:S(2)}, u32[]{:S(2)}) %collective-permute-start.1) | collective-permute-done | bytes 131104 | tf_op jit(solution)/shard_map/ppermute | solution.py:522
  8.2 0.4 collective-permute-start.5
  8.6 2.1 %shard_map.77 = (f32[2,256,256]{2,1,0:T(8,128)S(1)}, bf16[4,2,256,256]{3,2,1,0:T(8,128)(2,1)S(1)}) custom-call(f32[2,256,256]{2,1,0:T(8,128)} %bitcast.7, bf16[4,2,256,256]{3,2,1,0:T(8,128)(2,1)} %constant.67.clone.tables), custom_call_target="tpu_custom_call" | custom-call | flops 400000000 | bytes 3000000 | tf_op jit(solution)/shard_map/pallas_call | solution.py:350
  10.8 0.4 collective-permute-done.2
  11.2 2.0 %collective-permute-done.3 = f32[2,128,128]{2,1,0:T(8,128)S(1)} collective-permute-done((f32[2,128,128]{2,1,0:T(8,128)S(1)}, f32[2,128,128]{2,1,0:T(8,128)S(1)}, u32[]{:S(2)}, u32[]{:S(2)}) %collective-permute-start.3) | collective-permute-done | bytes 131104 | tf_op jit(solution)/shard_map/ppermute | solution.py:526
  13.3 0.1 copy.8.offsets
  13.4 0.5 collective-permute-start.6
  14.0 2.2 %shard_map.78.refs_1_ = f32[128,256]{1,0:T(8,128)S(1)} custom-call(s32[4,8,2,2]{3,2,1,0:T(2,128)S(1)} %copy.8.offsets, s32[4,8]{1,0:T(4,128)S(1)} %copy-done.2, f32[2,256,256]{2,1,0:T(8,128)S(1)} %copy-done), custom_call_target="tpu_custom_call" | custom-call | flops 40000000 | bytes 8000000 | tf_op jit(solution)/shard_map/pallas_call | solution.py:145
  16.2 2.0 %collective-permute-done.4 = f32[2,128,128]{2,1,0:T(8,128)} collective-permute-done((f32[2,128,128]{2,1,0:T(8,128)S(1)}, f32[2,128,128]{2,1,0:T(8,128)}, u32[]{:S(2)}, u32[]{:S(2)}) %collective-permute-start.4) | collective-permute-done | bytes 131104 | tf_op jit(solution)/shard_map/ppermute | solution.py:529
  18.3 0.5 collective-permute-start.10
  18.8 0.8 %collective-permute-done.9.far_pair = f32[2,128,128]{2,1,0:T(8,128)S(1)} collective-permute-done((f32[2,128,128]{2,1,0:T(8,128)S(1)}, f32[2,128,128]{2,1,0:T(8,128)S(1)}, u32[]{:S(2)}, u32[]{:S(2)}) %collective-permute-start.9) | collective-permute-done | bytes 131104 | tf_op jit(solution)/shard_map/ppermute | solution.py:498
  19.6 0.4 collective-permute-done.10.far_other
  20.0 4.3 %shard_map.79 = (f32[776,128]{1,0:T(8,128)S(1)}, f32[776,128]{1,0:T(8,128)S(1)}, f32[2,64,128]{2,1,0:T(8,128)S(1)}, f32[2,2,256,256]{3,2,1,0:T(8,128)S(1)}) custom-call(s32[4,8,2,2]{3,2,1,0:T(2,128)S(1)} %copy.8.offsets, s32[4,8]{1,0:T(4,128)S(1)} %copy-done.2, f32[2,256,256]{2,1,0:T(8,128)S(1)} %copy-done, f32[2,256,256]{2,1,0:T(8,128)S(1)} %get-tuple-element.65.magnitudes, ...), custom_call_target="tpu_custom_call" | custom-call | flops 3200000000 | bytes 8000000 | tf_op jit(solution)/shard_map/pallas_call | solution.py:374
  24.3 0.4 collective-permute-start.11
  24.7 1.4 %collective-permute-done.11.got = f32[776,128]{1,0:T(8,128)S(1)} collective-permute-done((f32[776,128]{1,0:T(8,128)S(1)}, f32[776,128]{1,0:T(8,128)S(1)}, u32[]{:S(2)}, u32[]{:S(2)}) %collective-permute-start.11) | collective-permute-done | bytes 397344 | tf_op jit(solution)/shard_map/ppermute | solution.py:498
  26.2 0.3 collective-permute-start.12
  26.5 1.7 %shard_map.81 = (f32[2,128,128]{2,1,0:T(8,128)S(1)}, f32[2,128,128]{2,1,0:T(8,128)S(1)}, f32[2,128,128]{2,1,0:T(8,128)S(1)}, f32[2,128,128]{2,1,0:T(8,128)S(1)},...) custom-call(s32[4,8,2,2]{3,2,1,0:T(2,128)S(1)} %copy.8.offsets, ...), custom_call_target="tpu_custom_call" | custom-call | flops 4000000 | bytes 4000000 | tf_op jit(solution)/shard_map/pallas_call | solution.py:484
  28.2 0.2 collective-permute-start.13
  28.4 0.4 collective-permute-start.14
  28.8 0.1 collective-permute-start.15
  28.9 0.4 collective-permute-start.16
  29.3 0.3 collective-permute-done.13.refs_4_
  29.7 0.1 collective-permute-start.17
  29.8 0.3 collective-permute-start.18
  30.2 0.2 collective-permute-start.19
  30.4 3.1 %collective-permute-done.12.got = f32[392,128]{1,0:T(8,128)S(1)} collective-permute-done((f32[392,128]{1,0:T(8,128)S(1)}, f32[392,128]{1,0:T(8,128)S(1)}, u32[]{:S(2)}, u32[]{:S(2)}) %collective-permute-start.12) | collective-permute-done | bytes 200736 | tf_op jit(solution)/shard_map/ppermute | solution.py:498
  33.6 1.3 %collective-permute-done.20 = f32[2,128,128]{2,1,0:T(8,128)S(1)} collective-permute-done((f32[2,128,128]{2,1,0:T(8,128)S(1)}, f32[2,128,128]{2,1,0:T(8,128)S(1)}, u32[]{:S(2)}, u32[]{:S(2)}) %collective-permute-start.20) | collective-permute-done | bytes 131104 | tf_op jit(solution)/shard_map/ppermute | solution.py:498
  34.8 0.3 collective-permute-start.22
  35.1 0.1 collective-permute-start.23
  35.3 1.9 %collective-permute-start.21 = (f32[200,128]{1,0:T(8,128)S(1)}, f32[200,128]{1,0:T(8,128)S(1)}, u32[]{:S(2)}, u32[]{:S(2)}) collective-permute-start(f32[200,128]{1,0:T(8,128)S(1)} %get-tuple-element.91), channel_id=1, source_target_pairs={{0,1},{1,0},{2,3},{3,2},{4,5},{5,4},{6,7},{7,6},{8,9},{9,8},{10,11... | collective-permute-start | bytes 307208 | tf_op jit(solution)/shard_map/ppermute | solution.py:498
  37.1 1.4 %collective-permute-start.25 = (f32[2,128,128]{2,1,0:T(8,128)S(1)}, f32[2,128,128]{2,1,0:T(8,128)S(1)}, u32[]{:S(2)}, u32[]{:S(2)}) collective-permute-start(f32[2,128,128]{2,1,0:T(8,128)S(1)} %collective-permute-done.17), channel_id=1, source_target_pairs={{24,8},{0,16},{16,24},{8,0},{25,9},{1,17},{17,25},{9,1},{26,10},{2... | collective-permute-start | bytes 393224 | tf_op jit(solution)/shard_map/ppermute | solution.py:557
  38.5 2.0 %collective-permute-done.21 = f32[200,128]{1,0:T(8,128)S(1)} collective-permute-done((f32[200,128]{1,0:T(8,128)S(1)}, f32[200,128]{1,0:T(8,128)S(1)}, u32[]{:S(2)}, u32[]{:S(2)}) %collective-permute-start.21) | collective-permute-done | bytes 102432 | tf_op jit(solution)/shard_map/ppermute | solution.py:498
  40.6 2.7 %collective-permute-start.24 = (f32[264,128]{1,0:T(8,128)S(1)}, f32[264,128]{1,0:T(8,128)S(1)}, u32[]{:S(2)}, u32[]{:S(2)}) collective-permute-start(f32[264,128]{1,0:T(8,128)S(1)} %concatenate.15), channel_id=1, source_target_pairs={{0,2},{1,3},{2,0},{3,1},{4,6},{5,7},{6,4},{7,5},{8,10},{9,11},{10,... | collective-permute-start | bytes 405512 | tf_op jit(solution)/shard_map/ppermute | solution.py:498
  43.3 0.7 collective-permute-start.28
  44.0 2.6 %collective-permute-done.24 = f32[264,128]{1,0:T(8,128)S(1)} collective-permute-done((f32[264,128]{1,0:T(8,128)S(1)}, f32[264,128]{1,0:T(8,128)S(1)}, u32[]{:S(2)}, u32[]{:S(2)}) %collective-permute-start.24) | collective-permute-done | bytes 135200 | tf_op jit(solution)/shard_map/ppermute | solution.py:498
  46.6 3.7 %collective-permute-start.27 = (f32[200,128]{1,0:T(8,128)S(1)}, f32[200,128]{1,0:T(8,128)S(1)}, u32[]{:S(2)}, u32[]{:S(2)}) collective-permute-start(f32[200,128]{1,0:T(8,128)S(1)} %slice_add_fusion), channel_id=1, source_target_pairs={{0,6},{1,7},{2,4},{3,5},{4,2},{5,3},{6,0},{7,1},{8,14},{9,15},{10,... | collective-permute-start | bytes 307208 | tf_op jit(solution)/shard_map/ppermute | solution.py:498
  50.3 4.4 %collective-permute-done.27 = f32[200,128]{1,0:T(8,128)S(1)} collective-permute-done((f32[200,128]{1,0:T(8,128)S(1)}, f32[200,128]{1,0:T(8,128)S(1)}, u32[]{:S(2)}, u32[]{:S(2)}) %collective-permute-start.27) | collective-permute-done | bytes 102432 | tf_op jit(solution)/shard_map/ppermute | solution.py:498
  54.8 0.1 collective-permute-start.29
  54.9 4.2 %collective-permute-done.29 = f32[2,64,128]{2,1,0:T(8,128)S(1)} collective-permute-done((f32[2,64,128]{2,1,0:T(8,128)S(1)}, f32[2,64,128]{2,1,0:T(8,128)S(1)}, u32[]{:S(2)}, u32[]{:S(2)}) %collective-permute-start.29) | collective-permute-done | bytes 65568 | tf_op jit(solution)/shard_map/ppermute | solution.py:498
  59.1 1.0 %collective-permute-start.30 = (f32[2,128,128]{2,1,0:T(8,128)S(1)}, f32[2,128,128]{2,1,0:T(8,128)S(1)}, u32[]{:S(2)}, u32[]{:S(2)}) collective-permute-start(f32[2,128,128]{2,1,0:T(8,128)S(1)} %maximum_select_fusion.1), channel_id=1, source_target_pairs={{0,16},{8,24},{16,0},{24,8},{1,17},{9,25},{17,1},{25,9},{2,18},{10... | collective-permute-start | bytes 393224 | tf_op jit(solution)/shard_map/ppermute | solution.py:498
  60.1 0.1 collective-permute-start.31
  60.3 3.9 %collective-permute-done.30 = f32[2,128,128]{2,1,0:T(8,128)S(1)} collective-permute-done((f32[2,128,128]{2,1,0:T(8,128)S(1)}, f32[2,128,128]{2,1,0:T(8,128)S(1)}, u32[]{:S(2)}, u32[]{:S(2)}) %collective-permute-start.30) | collective-permute-done | bytes 131104 | tf_op jit(solution)/shard_map/ppermute | solution.py:498
  64.2 0.9 %collective-permute-done.31.refs_8_ = f32[2,128,128]{2,1,0:T(8,128)S(1)} collective-permute-done((f32[2,128,128]{2,1,0:T(8,128)S(1)}, f32[2,128,128]{2,1,0:T(8,128)S(1)}, u32[]{:S(2)}, u32[]{:S(2)}) %collective-permute-start.31) | collective-permute-done | bytes 131104 | tf_op jit(solution)/shard_map/ppermute | solution.py:580
  65.1 1.5 %collective-permute-done.32.refs_11_ = f32[2,256,128]{2,1,0:T(8,128)S(1)} collective-permute-done((f32[2,256,128]{2,1,0:T(8,128)S(1)}, f32[2,256,128]{2,1,0:T(8,128)S(1)}, u32[]{:S(2)}, u32[]{:S(2)}) %collective-permute-start.32) | collective-permute-done | bytes 262176 | tf_op jit(solution)/shard_map/ppermute | solution.py:498
  66.6 1.0 %shard_map.83 = (f32[2,128,256]{2,1,0:T(8,128)}, f32[2,256,256]{2,1,0:T(8,128)}) custom-call(f32[2,128,256]{2,1,0:T(8,128)S(1)} %copy-done.1, f32[128,256]{1,0:T(8,128)S(1)} %shard_map.78.refs_1_, f32[2,128,128]{2,1,0:T(8,128)S(1)} %get-tuple-element.75.refs_2_, f32[2,128,128]{2,1,0:T(8,128)S(1)} %get-tuple-element.76.refs_3_, ...), custom_call_target="tpu_custom_call" | custom-call | flops 1000000 | bytes 3000000 | tf_op jit(solution)/shard_map/pallas_call | solution.py:427
  (50 shorter events, 0.6 us)
Async XLA Ops:
  0.6 4.1 %copy-start.1 = (f32[2,128,256]{2,1,0:T(8,128)S(1)}, f32[2,128,256]{2,1,0:T(8,128)}, u32[]{:S(2)}) copy-start(f32[2,128,256]{2,1,0:T(8,128)} %refs_0_.1) | copy-start | bytes 786436
  1.7 6.5 %collective-permute-start.1 = (f32[2,128,128]{2,1,0:T(8,128)S(1)}, f32[2,128,128]{2,1,0:T(8,128)S(1)}, u32[]{:S(2)}, u32[]{:S(2)}) collective-permute-start(f32[2,128,128]{2,1,0:T(8,128)S(1)} %get-tuple-element.114), channel_id=1, source_target_pairs={{0,1},{1,0},{2,3},{3,2},{4,5},{5,4},{6,7},{7,6},{8,9},{9,8},{10,11... | collective-permute-start | bytes 393224 | tf_op jit(solution)/shard_map/ppermute | solution.py:522
  4.7 6.5 %collective-permute-start.2 = (f32[2,128,256]{2,1,0:T(8,128)S(1)}, f32[2,128,256]{2,1,0:T(8,128)}, u32[]{:S(2)}, u32[]{:S(2)}) collective-permute-start(f32[2,128,256]{2,1,0:T(8,128)S(1)} %copy-done.1), channel_id=1, source_target_pairs={{8,24},{16,0},{24,16},{0,8},{9,25},{17,1},{25,17},{1,9},{10,26},{1... | collective-permute-start | bytes 786440 | tf_op jit(solution)/shard_map/ppermute | solution.py:526
  4.7 6.0 %collective-permute-start = (f32[2,128,128]{2,1,0:T(8,128)S(1)}, f32[2,128,128]{2,1,0:T(8,128)S(1)}, u32[]{:S(2)}, u32[]{:S(2)}) collective-permute-start(f32[2,128,128]{2,1,0:T(8,128)S(1)} %get-tuple-element.115), channel_id=1, source_target_pairs={{1,2},{3,4},{5,6},{2,1},{4,3},{6,5},{9,10},{11,12},{13,14},{10,9},... | collective-permute-start | bytes 393224 | tf_op jit(solution)/shard_map/ppermute | solution.py:523
  8.2 5.8 %copy-start = (f32[2,256,256]{2,1,0:T(8,128)S(1)}, f32[2,256,256]{2,1,0:T(8,128)}, u32[]{:S(2)}) copy-start(f32[2,256,256]{2,1,0:T(8,128)} %probe.4) | copy-start | bytes 1572868
  8.2 5.0 %collective-permute-start.3 = (f32[2,128,128]{2,1,0:T(8,128)S(1)}, f32[2,128,128]{2,1,0:T(8,128)S(1)}, u32[]{:S(2)}, u32[]{:S(2)}) collective-permute-start(f32[2,128,128]{2,1,0:T(8,128)S(1)} %collective-permute-done.1.pair_rim), channel_id=1, source_target_pairs={{8,24},{16,0},{24,16},{0,8},{9,25},{17,1},{25,17},{1,9},{10,26},{1... | collective-permute-start | bytes 393224 | tf_op jit(solution)/shard_map/ppermute | solution.py:526
  8.2 10.1 %collective-permute-start.5 = (f32[2,128,256]{2,1,0:T(8,128)S(1)}, f32[2,128,256]{2,1,0:T(8,128)S(1)}, u32[]{:S(2)}, u32[]{:S(2)}) collective-permute-start(f32[2,128,256]{2,1,0:T(8,128)S(1)} %copy-done.1), channel_id=1, source_target_pairs={{0,8},{8,0},{16,24},{24,16},{1,9},{9,1},{17,25},{25,17},{2,10},{10... | collective-permute-start | bytes 786440 | tf_op jit(solution)/shard_map/ppermute | solution.py:498
  8.6 4.7 %copy-start.3 = (s32[4,8,2,2]{1,3,2,0:T(2,128)S(1)}, s32[4,8,2,2]{1,3,2,0:T(2,128)}, u32[]{:S(2)}) copy-start(s32[4,8,2,2]{1,3,2,0:T(2,128)} %param.8) | copy-start | bytes 1540
  13.2 0.7 %copy-start.4 = (f32[2,128,128]{2,1,0:T(8,128)}, f32[2,128,128]{2,1,0:T(8,128)S(1)}, u32[]{:S(2)}) copy-start(f32[2,128,128]{2,1,0:T(8,128)S(1)} %collective-permute-done.3) | copy-start | bytes 393220
  13.2 0.8 %copy-start.2 = (s32[4,8]{1,0:T(4,128)S(1)}, s32[4,8]{1,0:T(4,128)}, u32[]{:S(2)}) copy-start(s32[4,8]{1,0:T(4,128)} %counts.3) | copy-start | bytes 388
  13.2 5.1 %collective-permute-start.4 = (f32[2,128,128]{2,1,0:T(8,128)S(1)}, f32[2,128,128]{2,1,0:T(8,128)}, u32[]{:S(2)}, u32[]{:S(2)}) collective-permute-start(f32[2,128,128]{2,1,0:T(8,128)S(1)} %collective-permute-done.other_rim), channel_id=1, source_target_pairs={{8,24},{16,0},{24,16},{0,8},{9,25},{17,1},{25,17},{1,9},{10,26},{1... | collective-permute-start | bytes 393224 | tf_op jit(solution)/shard_map/ppermute | solution.py:529
  13.2 6.4 %collective-permute-start.8 = (f32[2,128,256]{2,1,0:T(8,128)}, f32[2,128,256]{2,1,0:T(8,128)S(1)}, u32[]{:S(2)}, u32[]{:S(2)}) collective-permute-start(f32[2,128,256]{2,1,0:T(8,128)} %collective-permute-done.2), channel_id=1, source_target_pairs={{0,8},{8,0},{16,24},{24,16},{1,9},{9,1},{17,25},{25,17},{2,10},{10... | collective-permute-start | bytes 786440 | tf_op jit(solution)/shard_map/ppermute | solution.py:498
  13.4 5.4 %collective-permute-start.6 = (f32[2,128,128]{2,1,0:T(8,128)S(1)}, f32[2,128,128]{2,1,0:T(8,128)S(1)}, u32[]{:S(2)}, u32[]{:S(2)}) collective-permute-start(f32[2,128,128]{2,1,0:T(8,128)S(1)} %collective-permute-done.1.pair_rim), channel_id=1, source_target_pairs={{0,8},{8,0},{16,24},{24,16},{1,9},{9,1},{17,25},{25,17},{2,10},{10... | collective-permute-start | bytes 393224 | tf_op jit(solution)/shard_map/ppermute | solution.py:498
  13.9 4.9 %collective-permute-start.7 = (f32[2,128,128]{2,1,0:T(8,128)S(1)}, f32[2,128,128]{2,1,0:T(8,128)S(1)}, u32[]{:S(2)}, u32[]{:S(2)}) collective-permute-start(f32[2,128,128]{2,1,0:T(8,128)S(1)} %collective-permute-done.other_rim), channel_id=1, source_target_pairs={{0,8},{8,0},{16,24},{24,16},{1,9},{9,1},{17,25},{25,17},{2,10},{10... | collective-permute-start | bytes 393224 | tf_op jit(solution)/shard_map/ppermute | solution.py:498
  14.0 4.2 %copy-start.5 = (f32[2,128,128]{2,1,0:T(8,128)S(1)}, f32[2,128,128]{2,1,0:T(8,128)}, u32[]{:S(2)}) copy-start(f32[2,128,128]{2,1,0:T(8,128)} %copy-done.4) | copy-start | bytes 393220
  18.3 1.3 %collective-permute-start.9 = (f32[2,128,128]{2,1,0:T(8,128)S(1)}, f32[2,128,128]{2,1,0:T(8,128)S(1)}, u32[]{:S(2)}, u32[]{:S(2)}) collective-permute-start(f32[2,128,128]{2,1,0:T(8,128)S(1)} %copy-done.5), channel_id=1, source_target_pairs={{0,8},{8,0},{16,24},{24,16},{1,9},{9,1},{17,25},{25,17},{2,10},{10... | collective-permute-start | bytes 393224 | tf_op jit(solution)/shard_map/ppermute | solution.py:498
  18.3 1.7 %collective-permute-start.10 = (f32[2,128,128]{2,1,0:T(8,128)}, f32[2,128,128]{2,1,0:T(8,128)S(1)}, u32[]{:S(2)}, u32[]{:S(2)}) collective-permute-start(f32[2,128,128]{2,1,0:T(8,128)} %collective-permute-done.4), channel_id=1, source_target_pairs={{0,8},{8,0},{16,24},{24,16},{1,9},{9,1},{17,25},{25,17},{2,10},{10... | collective-permute-start | bytes 393224 | tf_op jit(solution)/shard_map/ppermute | solution.py:498
  24.3 1.8 %collective-permute-start.11 = (f32[776,128]{1,0:T(8,128)S(1)}, f32[776,128]{1,0:T(8,128)S(1)}, u32[]{:S(2)}, u32[]{:S(2)}) collective-permute-start(f32[776,128]{1,0:T(8,128)S(1)} %get-tuple-element.71), channel_id=1, source_target_pairs={{0,8},{8,0},{16,24},{24,16},{1,9},{9,1},{17,25},{25,17},{2,10},{10... | collective-permute-start | bytes 1191944 | tf_op jit(solution)/shard_map/ppermute | solution.py:498
  26.2 7.3 %collective-permute-start.12 = (f32[392,128]{1,0:T(8,128)S(1)}, f32[392,128]{1,0:T(8,128)S(1)}, u32[]{:S(2)}, u32[]{:S(2)}) collective-permute-start(f32[392,128]{1,0:T(8,128)S(1)} %get-tuple-element.78), channel_id=1, source_target_pairs={{0,16},{8,24},{16,0},{24,8},{1,17},{9,25},{17,1},{25,9},{2,18},{10... | collective-permute-start | bytes 602120 | tf_op jit(solution)/shard_map/ppermute | solution.py:498
  28.2 1.4 %collective-permute-start.13 = (f32[2,128,128]{2,1,0:T(8,128)S(1)}, f32[2,128,128]{2,1,0:T(8,128)S(1)}, u32[]{:S(2)}, u32[]{:S(2)}) collective-permute-start(f32[2,128,128]{2,1,0:T(8,128)S(1)} %get-tuple-element.80), channel_id=1, source_target_pairs={{0,8},{8,0},{16,24},{24,16},{1,9},{9,1},{17,25},{25,17},{2,10},{10... | collective-permute-start | bytes 393224 | tf_op jit(solution)/shard_map/ppermute | solution.py:498
  28.4 1.4 %collective-permute-start.14 = (f32[2,128,128]{2,1,0:T(8,128)S(1)}, f32[2,128,128]{2,1,0:T(8,128)S(1)}, u32[]{:S(2)}, u32[]{:S(2)}) collective-permute-start(f32[2,128,128]{2,1,0:T(8,128)S(1)} %get-tuple-element.81), channel_id=1, source_target_pairs={{0,8},{8,0},{16,24},{24,16},{1,9},{9,1},{17,25},{25,17},{2,10},{10... | collective-permute-start | bytes 393224 | tf_op jit(solution)/shard_map/ppermute | solution.py:498
  28.8 1.4 %collective-permute-start.15 = (f32[2,128,128]{2,1,0:T(8,128)S(1)}, f32[2,128,128]{2,1,0:T(8,128)S(1)}, u32[]{:S(2)}, u32[]{:S(2)}) collective-permute-start(f32[2,128,128]{2,1,0:T(8,128)S(1)} %get-tuple-element.82), channel_id=1, source_target_pairs={{0,8},{8,0},{16,24},{24,16},{1,9},{9,1},{17,25},{25,17},{2,10},{10... | collective-permute-start | bytes 393224 | tf_op jit(solution)/shard_map/ppermute | solution.py:498
  28.9 4.6 %collective-permute-start.16 = (f32[2,128,128]{2,1,0:T(8,128)S(1)}, f32[2,128,128]{2,1,0:T(8,128)S(1)}, u32[]{:S(2)}, u32[]{:S(2)}) collective-permute-start(f32[2,128,128]{2,1,0:T(8,128)S(1)} %get-tuple-element.83), channel_id=1, source_target_pairs={{0,8},{8,0},{16,24},{24,16},{1,9},{9,1},{17,25},{25,17},{2,10},{10... | collective-permute-start | bytes 393224 | tf_op jit(solution)/shard_map/ppermute | solution.py:498
  29.7 3.9 %collective-permute-start.17 = (f32[2,128,128]{2,1,0:T(8,128)S(1)}, f32[2,128,128]{2,1,0:T(8,128)S(1)}, u32[]{:S(2)}, u32[]{:S(2)}) collective-permute-start(f32[2,128,128]{2,1,0:T(8,128)S(1)} %get-tuple-element.84), channel_id=1, source_target_pairs={{0,8},{8,0},{16,24},{24,16},{1,9},{9,1},{17,25},{25,17},{2,10},{10... | collective-permute-start | bytes 393224 | tf_op jit(solution)/shard_map/ppermute | solution.py:498
  29.8 3.7 %collective-permute-start.18 = (f32[2,128,128]{2,1,0:T(8,128)S(1)}, f32[2,128,128]{2,1,0:T(8,128)S(1)}, u32[]{:S(2)}, u32[]{:S(2)}) collective-permute-start(f32[2,128,128]{2,1,0:T(8,128)S(1)} %get-tuple-element.85), channel_id=1, source_target_pairs={{0,8},{8,0},{16,24},{24,16},{1,9},{9,1},{17,25},{25,17},{2,10},{10... | collective-permute-start | bytes 393224 | tf_op jit(solution)/shard_map/ppermute | solution.py:498
  30.2 3.4 %collective-permute-start.19 = (f32[2,128,128]{2,1,0:T(8,128)S(1)}, f32[2,128,128]{2,1,0:T(8,128)S(1)}, u32[]{:S(2)}, u32[]{:S(2)}) collective-permute-start(f32[2,128,128]{2,1,0:T(8,128)S(1)} %get-tuple-element.86), channel_id=1, source_target_pairs={{0,8},{8,0},{16,24},{24,16},{1,9},{9,1},{17,25},{25,17},{2,10},{10... | collective-permute-start | bytes 393224 | tf_op jit(solution)/shard_map/ppermute | solution.py:498
  33.5 1.3 %collective-permute-start.20 = (f32[2,128,128]{2,1,0:T(8,128)S(1)}, f32[2,128,128]{2,1,0:T(8,128)S(1)}, u32[]{:S(2)}, u32[]{:S(2)}) collective-permute-start(f32[2,128,128]{2,1,0:T(8,128)S(1)} %get-tuple-element.87), channel_id=1, source_target_pairs={{0,8},{8,0},{16,24},{24,16},{1,9},{9,1},{17,25},{25,17},{2,10},{10... | collective-permute-start | bytes 393224 | tf_op jit(solution)/shard_map/ppermute | solution.py:498
  34.8 5.7 %collective-permute-start.22 = (f32[2,128,128]{2,1,0:T(8,128)S(1)}, f32[2,128,128]{2,1,0:T(8,128)S(1)}, u32[]{:S(2)}, u32[]{:S(2)}) collective-permute-start(f32[2,128,128]{2,1,0:T(8,128)S(1)} %collective-permute-done.19), channel_id=1, source_target_pairs={{24,8},{0,16},{16,24},{8,0},{25,9},{1,17},{17,25},{9,1},{26,10},{2... | collective-permute-start | bytes 393224 | tf_op jit(solution)/shard_map/ppermute | solution.py:557
  35.1 5.4 %collective-permute-start.23 = (f32[2,128,128]{2,1,0:T(8,128)S(1)}, f32[2,128,128]{2,1,0:T(8,128)S(1)}, u32[]{:S(2)}, u32[]{:S(2)}) collective-permute-start(f32[2,128,128]{2,1,0:T(8,128)S(1)} %collective-permute-done.20), channel_id=1, source_target_pairs={{24,8},{0,16},{16,24},{8,0},{25,9},{1,17},{17,25},{9,1},{26,10},{2... | collective-permute-start | bytes 393224 | tf_op jit(solution)/shard_map/ppermute | solution.py:557
  35.3 5.2 %collective-permute-start.21 = (f32[200,128]{1,0:T(8,128)S(1)}, f32[200,128]{1,0:T(8,128)S(1)}, u32[]{:S(2)}, u32[]{:S(2)}) collective-permute-start(f32[200,128]{1,0:T(8,128)S(1)} %get-tuple-element.91), channel_id=1, source_target_pairs={{0,1},{1,0},{2,3},{3,2},{4,5},{5,4},{6,7},{7,6},{8,9},{9,8},{10,11... | collective-permute-start | bytes 307208 | tf_op jit(solution)/shard_map/ppermute | solution.py:498
  37.1 9.5 %collective-permute-start.25 = (f32[2,128,128]{2,1,0:T(8,128)S(1)}, f32[2,128,128]{2,1,0:T(8,128)S(1)}, u32[]{:S(2)}, u32[]{:S(2)}) collective-permute-start(f32[2,128,128]{2,1,0:T(8,128)S(1)} %collective-permute-done.17), channel_id=1, source_target_pairs={{24,8},{0,16},{16,24},{8,0},{25,9},{1,17},{17,25},{9,1},{26,10},{2... | collective-permute-start | bytes 393224 | tf_op jit(solution)/shard_map/ppermute | solution.py:557
  38.5 8.1 %collective-permute-start.26 = (f32[2,128,128]{2,1,0:T(8,128)S(1)}, f32[2,128,128]{2,1,0:T(8,128)S(1)}, u32[]{:S(2)}, u32[]{:S(2)}) collective-permute-start(f32[2,128,128]{2,1,0:T(8,128)S(1)} %collective-permute-done.18), channel_id=1, source_target_pairs={{24,8},{0,16},{16,24},{8,0},{25,9},{1,17},{17,25},{9,1},{26,10},{2... | collective-permute-start | bytes 393224 | tf_op jit(solution)/shard_map/ppermute | solution.py:557
  40.6 6.0 %collective-permute-start.24 = (f32[264,128]{1,0:T(8,128)S(1)}, f32[264,128]{1,0:T(8,128)S(1)}, u32[]{:S(2)}, u32[]{:S(2)}) collective-permute-start(f32[264,128]{1,0:T(8,128)S(1)} %concatenate.15), channel_id=1, source_target_pairs={{0,2},{1,3},{2,0},{3,1},{4,6},{5,7},{6,4},{7,5},{8,10},{9,11},{10,... | collective-permute-start | bytes 405512 | tf_op jit(solution)/shard_map/ppermute | solution.py:498
  43.3 11.4 %collective-permute-start.28 = (f32[2,128,128]{2,1,0:T(8,128)S(1)}, f32[2,128,128]{2,1,0:T(8,128)S(1)}, u32[]{:S(2)}, u32[]{:S(2)}) collective-permute-start(f32[2,128,128]{2,1,0:T(8,128)S(1)} %select_add_fusion.1), channel_id=1, source_target_pairs={{1,2},{3,4},{5,6},{2,1},{4,3},{6,5},{9,10},{11,12},{13,14},{10,9},... | collective-permute-start | bytes 393224 | tf_op jit(solution)/shard_map/ppermute | solution.py:565
  46.6 8.1 %collective-permute-start.27 = (f32[200,128]{1,0:T(8,128)S(1)}, f32[200,128]{1,0:T(8,128)S(1)}, u32[]{:S(2)}, u32[]{:S(2)}) collective-permute-start(f32[200,128]{1,0:T(8,128)S(1)} %slice_add_fusion), channel_id=1, source_target_pairs={{0,6},{1,7},{2,4},{3,5},{4,2},{5,3},{6,0},{7,1},{8,14},{9,15},{10,... | collective-permute-start | bytes 307208 | tf_op jit(solution)/shard_map/ppermute | solution.py:498
  54.8 4.3 %collective-permute-start.29 = (f32[2,64,128]{2,1,0:T(8,128)S(1)}, f32[2,64,128]{2,1,0:T(8,128)S(1)}, u32[]{:S(2)}, u32[]{:S(2)}) collective-permute-start(f32[2,64,128]{2,1,0:T(8,128)S(1)} %fusion), channel_id=1, source_target_pairs={{0,1},{1,0},{2,3},{3,2},{4,5},{5,4},{6,7},{7,6},{8,9},{9,8},{10,11... | collective-permute-start | bytes 196616 | tf_op jit(solution)/shard_map/ppermute | solution.py:498
  59.1 5.0 %collective-permute-start.30 = (f32[2,128,128]{2,1,0:T(8,128)S(1)}, f32[2,128,128]{2,1,0:T(8,128)S(1)}, u32[]{:S(2)}, u32[]{:S(2)}) collective-permute-start(f32[2,128,128]{2,1,0:T(8,128)S(1)} %maximum_select_fusion.1), channel_id=1, source_target_pairs={{0,16},{8,24},{16,0},{24,8},{1,17},{9,25},{17,1},{25,9},{2,18},{10... | collective-permute-start | bytes 393224 | tf_op jit(solution)/shard_map/ppermute | solution.py:498
  60.1 5.0 %collective-permute-start.31 = (f32[2,128,128]{2,1,0:T(8,128)S(1)}, f32[2,128,128]{2,1,0:T(8,128)S(1)}, u32[]{:S(2)}, u32[]{:S(2)}) collective-permute-start(f32[2,128,128]{2,1,0:T(8,128)S(1)} %select_add_fusion), channel_id=1, source_target_pairs={{0,1},{1,0},{2,3},{3,2},{4,5},{5,4},{6,7},{7,6},{8,9},{9,8},{10,11... | collective-permute-start | bytes 393224 | tf_op jit(solution)/shard_map/ppermute | solution.py:580
  65.1 1.5 %collective-permute-start.32 = (f32[2,256,128]{2,1,0:T(8,128)S(1)}, f32[2,256,128]{2,1,0:T(8,128)S(1)}, u32[]{:S(2)}, u32[]{:S(2)}) collective-permute-start(f32[2,256,128]{2,1,0:T(8,128)S(1)} %maximum_select_fusion.refs_10_), channel_id=1, source_target_pairs={{0,8},{8,0},{16,24},{24,16},{1,9},{9,1},{17,25},{25,17},{2,10},{10... | collective-permute-start | bytes 786440 | tf_op jit(solution)/shard_map/ppermute | solution.py:498

commit v4 on v3

--- a/solution.py
+++ b/solution.py
@@ -537,14 +537,13 @@
     def pick(condition, first, second):
         return jnp.where(condition, first, second)
 
-    def join(value, axis, count, bit):
-        place_here = (lax.axis_index(axis) // bit) % 2
-        got = exchange(value, axis, count, bit)
-        return pick(
-            place_here == 0,
-            jnp.concatenate([value, got], 1),
-            jnp.concatenate([got, value], 1),
-        )
+    square = [
+        (r * cols + c, (r ^ 2) * cols + (c ^ 1)) for r in range(rows) for c in range(cols)
+    ]
+
+    def all_three(across, beside, diagonal):
+        diagonal = lax.ppermute(diagonal, ("row", "col"), square)
+        return exchange(across, "row", rows, 2), exchange(beside, "col", cols, 1), diagonal
 
     kept, given = fold(kept, exchange(given, "row", rows, 1), "row", 2)
     given, delta = tie((given, delta))
@@ -575,10 +574,19 @@
     real, imag, weight, total = (value[k * size : (k + 1) * size] for k in range(4))
     update = jnp.stack([real, imag]) / (weight + probe_damping * (total[:1] / (width * width)))
     fresh = own_probe + update
-    fresh = join(fresh, "col", cols, 1)
-    fresh, pair_part = tie((fresh, pair_part))
     pair_part = lax.ppermute(pair_part, "col", pairs)
-    fresh = join(fresh, "row", rows, 2)
+    across, beside, diagonal = all_three(fresh, fresh, fresh)
+
+    def ordered(place_here, one, other):
+        return pick(
+            place_here == 0,
+            jnp.concatenate([one, other], 1),
+            jnp.concatenate([other, one], 1),
+        )
+
+    fresh = ordered(
+        (row_place // 2) % 2, ordered(col_odd, fresh, beside), ordered(col_odd, across, diagonal)
+    )
     fresh, pair_part = tie((fresh, pair_part))
     got = exchange(fresh, "row", rows, 1)
     return finish(

time: 67.8 us -> 66 us (0.973)
  waiting for transfers between devices: 34.2 us -> 30.1 us
  starting transfers between devices: 19.8 us -> 22.1 us
    ppermute x22, waiting for transfers between devices: 25.9 us -> 21 us  [exchange(): return lax.ppermute(value, axis, [(i, i ^ bit) for i in range(count)])]
    ppermute x0 -> x1, starting transfers between devices: none -> 2.38 us  [all_three(): diagonal = lax.ppermute(diagonal, ('row', 'col'), square)]
    ppermute x1, waiting for transfers between devices: 0.94 us -> 1.72 us  [shards(): pair_part = lax.ppermute(pair_part, 'col', pairs)]
  transfers between devices with their start and end apart: 33 -> 34, of which waited for: 17 -> 17; matrix products, arithmetic and copies ran while one was open for 0% -> 0% of each run, Pallas kernels for 9% -> 9%
where the time goes in v4:
time: 66 us; the launch traced here: 65.8 us
  waiting for transfers between devices  30.1 us (46%)
  starting transfers between devices  22.1 us (33%)
  Pallas kernels  11.4 us (17%)
  other arithmetic  1.21 us (2%)
  between operations  0.89 us (1%)
    ppermute x22, waiting for transfers between devices, exchange(): return lax.ppermute(value, axis, [(i, i ^ bit) for i in range(count)])  21 us
    ppermute x22, starting transfers between devices, exchange(): return lax.ppermute(value, axis, [(i, i ^ bit) for i in range(count)])  13.6 us
    pallas_call x1, Pallas kernels, exit_update(): pl.pallas_call(delta_kernel, out_shape=[jax.ShapeDtypeStruct((3 * width +...  4.32 us
    ppermute x1, starting transfers between devices, shards(): pair_rim = lax.ppermute(jnp.where(col_odd == 0, high, low), 'col', pairs)  3.03 us
    ppermute x1, waiting for transfers between devices, shards(): pair_rim = lax.ppermute(jnp.where(col_odd == 0, high, low), 'col', pairs)  2.82 us
    ppermute x2, waiting for transfers between devices, shards(): lax.ppermute(block, 'row', toward)  2.42 us
    ppermute x1, starting transfers between devices, all_three(): diagonal = lax.ppermute(diagonal, ('row', 'col'), square)  2.38 us
    pallas_call x1, Pallas kernels, lighting(): pl.pallas_call(lighting_kernel, out_shape=jax.ShapeDtypeStruct((tile_r, t...  2.18 us
  transfers between devices with their start and end apart: 34, of which 17 were waited for; matrix products, arithmetic and copies ran while one was open for 0% of the time, Pallas kernels for 9%

profile of v4, /device:TPU:0, one launch (start us, length us, event | category | flops | bytes accessed | tf_op | source)
XLA Modules:
  0.0 65.8 jit_solution(7253088358388652963)
XLA Ops:
  0.7 1.0 %slice_select_fusion = (f32[2,128,128]{2,1,0:T(8,128)S(1)}, f32[2,128,128]{2,1,0:T(8,128)S(1)}) fusion(f32[2,128,256]{2,1,0:T(8,128)} %refs_0_.1, pred[]{:T(512)S(6)} %eq.13), kind=kLoop, calls=%fused_computation.5 | loop fusion | flops 65536 | bytes 524289 | tf_op jit(solution)/shard_map/jit(_where)/select_n | solution.py:522
  1.7 3.0 %collective-permute-start.1 = (f32[2,128,128]{2,1,0:T(8,128)S(1)}, f32[2,128,128]{2,1,0:T(8,128)S(1)}, u32[]{:S(2)}, u32[]{:S(2)}) collective-permute-start(f32[2,128,128]{2,1,0:T(8,128)S(1)} %get-tuple-element.110), channel_id=1, source_target_pairs={{0,1},{1,0},{2,3},{3,2},{4,5},{5,4},{6,7},{7,6},{8,9},{9,8},{10,11... | collective-permute-start | bytes 393224 | tf_op jit(solution)/shard_map/ppermute | solution.py:522
  4.7 0.7 collective-permute-start
  5.4 2.8 %collective-permute-done.1.pair_rim = f32[2,128,128]{2,1,0:T(8,128)S(1)} collective-permute-done((f32[2,128,128]{2,1,0:T(8,128)S(1)}, f32[2,128,128]{2,1,0:T(8,128)S(1)}, u32[]{:S(2)}, u32[]{:S(2)}) %collective-permute-start.1) | collective-permute-done | bytes 131104 | tf_op jit(solution)/shard_map/ppermute | solution.py:522
  8.2 0.4 collective-permute-start.5
  8.6 2.1 %shard_map.77 = (f32[2,256,256]{2,1,0:T(8,128)S(1)}, bf16[4,2,256,256]{3,2,1,0:T(8,128)(2,1)S(1)}) custom-call(f32[2,256,256]{2,1,0:T(8,128)} %bitcast.7, bf16[4,2,256,256]{3,2,1,0:T(8,128)(2,1)} %constant.55.clone.tables), custom_call_target="tpu_custom_call" | custom-call | flops 400000000 | bytes 3000000 | tf_op jit(solution)/shard_map/pallas_call | solution.py:350
  10.8 0.4 collective-permute-done.2
  11.2 2.0 %collective-permute-done.3 = f32[2,128,128]{2,1,0:T(8,128)S(1)} collective-permute-done((f32[2,128,128]{2,1,0:T(8,128)S(1)}, f32[2,128,128]{2,1,0:T(8,128)S(1)}, u32[]{:S(2)}, u32[]{:S(2)}) %collective-permute-start.3) | collective-permute-done | bytes 131104 | tf_op jit(solution)/shard_map/ppermute | solution.py:526
  13.3 0.1 copy.8.offsets
  13.4 0.5 collective-permute-start.6
  14.0 2.2 %shard_map.78.refs_1_ = f32[128,256]{1,0:T(8,128)S(1)} custom-call(s32[4,8,2,2]{3,2,1,0:T(2,128)S(1)} %copy.8.offsets, s32[4,8]{1,0:T(4,128)S(1)} %copy-done.2, f32[2,256,256]{2,1,0:T(8,128)S(1)} %copy-done), custom_call_target="tpu_custom_call" | custom-call | flops 40000000 | bytes 8000000 | tf_op jit(solution)/shard_map/pallas_call | solution.py:145
  16.2 2.0 %collective-permute-done.4 = f32[2,128,128]{2,1,0:T(8,128)} collective-permute-done((f32[2,128,128]{2,1,0:T(8,128)S(1)}, f32[2,128,128]{2,1,0:T(8,128)}, u32[]{:S(2)}, u32[]{:S(2)}) %collective-permute-start.4) | collective-permute-done | bytes 131104 | tf_op jit(solution)/shard_map/ppermute | solution.py:529
  18.3 0.5 collective-permute-start.10
  18.8 0.8 %collective-permute-done.9.far_pair = f32[2,128,128]{2,1,0:T(8,128)S(1)} collective-permute-done((f32[2,128,128]{2,1,0:T(8,128)S(1)}, f32[2,128,128]{2,1,0:T(8,128)S(1)}, u32[]{:S(2)}, u32[]{:S(2)}) %collective-permute-start.9) | collective-permute-done | bytes 131104 | tf_op jit(solution)/shard_map/ppermute | solution.py:498
  19.6 0.4 collective-permute-done.10.far_other
  20.0 4.3 %shard_map.79 = (f32[776,128]{1,0:T(8,128)S(1)}, f32[776,128]{1,0:T(8,128)S(1)}, f32[2,64,128]{2,1,0:T(8,128)S(1)}, f32[2,2,256,256]{3,2,1,0:T(8,128)S(1)}) custom-call(s32[4,8,2,2]{3,2,1,0:T(2,128)S(1)} %copy.8.offsets, s32[4,8]{1,0:T(4,128)S(1)} %copy-done.2, f32[2,256,256]{2,1,0:T(8,128)S(1)} %copy-done, f32[2,256,256]{2,1,0:T(8,128)S(1)} %get-tuple-element.63.magnitudes, ...), custom_call_target="tpu_custom_call" | custom-call | flops 3200000000 | bytes 8000000 | tf_op jit(solution)/shard_map/pallas_call | solution.py:374
  24.3 0.4 collective-permute-start.11
  24.7 1.4 %collective-permute-done.11.got = f32[776,128]{1,0:T(8,128)S(1)} collective-permute-done((f32[776,128]{1,0:T(8,128)S(1)}, f32[776,128]{1,0:T(8,128)S(1)}, u32[]{:S(2)}, u32[]{:S(2)}) %collective-permute-start.11) | collective-permute-done | bytes 397344 | tf_op jit(solution)/shard_map/ppermute | solution.py:498
  26.2 0.5 collective-permute-start.12
  26.6 1.7 %shard_map.81 = (f32[2,128,128]{2,1,0:T(8,128)S(1)}, f32[2,128,128]{2,1,0:T(8,128)S(1)}, f32[2,128,128]{2,1,0:T(8,128)S(1)}, f32[2,128,128]{2,1,0:T(8,128)S(1)},...) custom-call(s32[4,8,2,2]{3,2,1,0:T(2,128)S(1)} %copy.8.offsets, ...), custom_call_target="tpu_custom_call" | custom-call | flops 4000000 | bytes 4000000 | tf_op jit(solution)/shard_map/pallas_call | solution.py:484
  28.4 0.1 collective-permute-start.13
  28.5 0.4 collective-permute-start.14
  29.0 0.4 collective-permute-start.16
  29.5 0.3 collective-permute-done.13.refs_4_
  29.8 0.1 collective-permute-start.17
  30.0 0.3 collective-permute-start.18
  30.3 0.2 collective-permute-start.19
  30.5 3.0 %collective-permute-done.12.got = f32[392,128]{1,0:T(8,128)S(1)} collective-permute-done((f32[392,128]{1,0:T(8,128)S(1)}, f32[392,128]{1,0:T(8,128)S(1)}, u32[]{:S(2)}, u32[]{:S(2)}) %collective-permute-start.12) | collective-permute-done | bytes 200736 | tf_op jit(solution)/shard_map/ppermute | solution.py:498
  33.5 1.3 %collective-permute-done.20 = f32[2,128,128]{2,1,0:T(8,128)S(1)} collective-permute-done((f32[2,128,128]{2,1,0:T(8,128)S(1)}, f32[2,128,128]{2,1,0:T(8,128)S(1)}, u32[]{:S(2)}, u32[]{:S(2)}) %collective-permute-start.20) | collective-permute-done | bytes 131104 | tf_op jit(solution)/shard_map/ppermute | solution.py:498
  34.8 0.4 collective-permute-start.22
  35.2 0.1 collective-permute-start.23
  35.4 2.1 %collective-permute-start.21 = (f32[200,128]{1,0:T(8,128)S(1)}, f32[200,128]{1,0:T(8,128)S(1)}, u32[]{:S(2)}, u32[]{:S(2)}) collective-permute-start(f32[200,128]{1,0:T(8,128)S(1)} %get-tuple-element.89), channel_id=1, source_target_pairs={{0,1},{1,0},{2,3},{3,2},{4,5},{5,4},{6,7},{7,6},{8,9},{9,8},{10,11... | collective-permute-start | bytes 307208 | tf_op jit(solution)/shard_map/ppermute | solution.py:498
  37.5 1.0 %collective-permute-start.25 = (f32[2,128,128]{2,1,0:T(8,128)S(1)}, f32[2,128,128]{2,1,0:T(8,128)S(1)}, u32[]{:S(2)}, u32[]{:S(2)}) collective-permute-start(f32[2,128,128]{2,1,0:T(8,128)S(1)} %collective-permute-done.17), channel_id=1, source_target_pairs={{24,8},{0,16},{16,24},{8,0},{25,9},{1,17},{17,25},{9,1},{26,10},{2... | collective-permute-start | bytes 393224 | tf_op jit(solution)/shard_map/ppermute | solution.py:556
  38.5 2.4 %collective-permute-done.21 = f32[200,128]{1,0:T(8,128)S(1)} collective-permute-done((f32[200,128]{1,0:T(8,128)S(1)}, f32[200,128]{1,0:T(8,128)S(1)}, u32[]{:S(2)}, u32[]{:S(2)}) %collective-permute-start.21) | collective-permute-done | bytes 102432 | tf_op jit(solution)/shard_map/ppermute | solution.py:498
  41.0 2.2 %collective-permute-start.24 = (f32[264,128]{1,0:T(8,128)S(1)}, f32[264,128]{1,0:T(8,128)S(1)}, u32[]{:S(2)}, u32[]{:S(2)}) collective-permute-start(f32[264,128]{1,0:T(8,128)S(1)} %concatenate.21), channel_id=1, source_target_pairs={{0,2},{1,3},{2,0},{3,1},{4,6},{5,7},{6,4},{7,5},{8,10},{9,11},{10,... | collective-permute-start | bytes 405512 | tf_op jit(solution)/shard_map/ppermute | solution.py:498
  43.2 0.7 %collective-permute-start.28 = (f32[2,128,128]{2,1,0:T(8,128)S(1)}, f32[2,128,128]{2,1,0:T(8,128)S(1)}, u32[]{:S(2)}, u32[]{:S(2)}) collective-permute-start(f32[2,128,128]{2,1,0:T(8,128)S(1)} %select_add_fusion.1), channel_id=1, source_target_pairs={{1,2},{3,4},{5,6},{2,1},{4,3},{6,5},{9,10},{11,12},{13,14},{10,9},... | collective-permute-start | bytes 393224 | tf_op jit(solution)/shard_map/ppermute | solution.py:564
  43.8 2.6 %collective-permute-done.24 = f32[264,128]{1,0:T(8,128)S(1)} collective-permute-done((f32[264,128]{1,0:T(8,128)S(1)}, f32[264,128]{1,0:T(8,128)S(1)}, u32[]{:S(2)}, u32[]{:S(2)}) %collective-permute-start.24) | collective-permute-done | bytes 135200 | tf_op jit(solution)/shard_map/ppermute | solution.py:498
  46.5 4.0 %collective-permute-start.27 = (f32[200,128]{1,0:T(8,128)S(1)}, f32[200,128]{1,0:T(8,128)S(1)}, u32[]{:S(2)}, u32[]{:S(2)}) collective-permute-start(f32[200,128]{1,0:T(8,128)S(1)} %slice_add_fusion), channel_id=1, source_target_pairs={{0,6},{1,7},{2,4},{3,5},{4,2},{5,3},{6,0},{7,1},{8,14},{9,15},{10,... | collective-permute-start | bytes 307208 | tf_op jit(solution)/shard_map/ppermute | solution.py:498
  50.4 4.2 %collective-permute-done.27 = f32[200,128]{1,0:T(8,128)S(1)} collective-permute-done((f32[200,128]{1,0:T(8,128)S(1)}, f32[200,128]{1,0:T(8,128)S(1)}, u32[]{:S(2)}, u32[]{:S(2)}) %collective-permute-start.27) | collective-permute-done | bytes 102432 | tf_op jit(solution)/shard_map/ppermute | solution.py:498
  54.8 0.1 collective-permute-start.29
  54.9 2.4 %collective-permute-start.31 = (f32[2,64,128]{2,1,0:T(8,128)S(1)}, f32[2,64,128]{2,1,0:T(8,128)S(1)}, u32[]{:S(2)}, u32[]{:S(2)}) collective-permute-start(f32[2,64,128]{2,1,0:T(8,128)S(1)} %fusion), channel_id=1, source_target_pairs={{0,17},{1,16},{2,19},{3,18},{4,21},{5,20},{6,23},{7,22},{8,25},{9,... | collective-permute-start | bytes 196616 | tf_op jit(solution)/shard_map/ppermute | solution.py:545
  57.3 1.1 %collective-permute-start.30 = (f32[2,64,128]{2,1,0:T(8,128)S(1)}, f32[2,64,128]{2,1,0:T(8,128)S(1)}, u32[]{:S(2)}, u32[]{:S(2)}) collective-permute-start(f32[2,64,128]{2,1,0:T(8,128)S(1)} %fusion), channel_id=1, source_target_pairs={{0,16},{8,24},{16,0},{24,8},{1,17},{9,25},{17,1},{25,9},{2,18},{10... | collective-permute-start | bytes 196616 | tf_op jit(solution)/shard_map/ppermute | solution.py:498
  58.3 0.1 collective-permute-start.32
  58.4 1.9 %collective-permute-done.29 = f32[2,64,128]{2,1,0:T(8,128)S(1)} collective-permute-done((f32[2,64,128]{2,1,0:T(8,128)S(1)}, f32[2,64,128]{2,1,0:T(8,128)S(1)}, u32[]{:S(2)}, u32[]{:S(2)}) %collective-permute-start.29) | collective-permute-done | bytes 65568 | tf_op jit(solution)/shard_map/ppermute | solution.py:498
  60.4 1.2 %collective-permute-done.30 = f32[2,64,128]{2,1,0:T(8,128)S(1)} collective-permute-done((f32[2,64,128]{2,1,0:T(8,128)S(1)}, f32[2,64,128]{2,1,0:T(8,128)S(1)}, u32[]{:S(2)}, u32[]{:S(2)}) %collective-permute-start.30) | collective-permute-done | bytes 65568 | tf_op jit(solution)/shard_map/ppermute | solution.py:498
  61.6 1.7 %collective-permute-done.32.refs_8_ = f32[2,128,128]{2,1,0:T(8,128)S(1)} collective-permute-done((f32[2,128,128]{2,1,0:T(8,128)S(1)}, f32[2,128,128]{2,1,0:T(8,128)S(1)}, u32[]{:S(2)}, u32[]{:S(2)}) %collective-permute-start.32) | collective-permute-done | bytes 131104 | tf_op jit(solution)/shard_map/ppermute | solution.py:577
  63.3 1.5 %collective-permute-done.33.refs_11_ = f32[2,256,128]{2,1,0:T(8,128)S(1)} collective-permute-done((f32[2,256,128]{2,1,0:T(8,128)S(1)}, f32[2,256,128]{2,1,0:T(8,128)S(1)}, u32[]{:S(2)}, u32[]{:S(2)}) %collective-permute-start.33) | collective-permute-done | bytes 262176 | tf_op jit(solution)/shard_map/ppermute | solution.py:498
  64.8 1.0 %shard_map.83 = (f32[2,128,256]{2,1,0:T(8,128)}, f32[2,256,256]{2,1,0:T(8,128)}) custom-call(f32[2,128,256]{2,1,0:T(8,128)S(1)} %copy-done.1, f32[128,256]{1,0:T(8,128)S(1)} %shard_map.78.refs_1_, f32[2,128,128]{2,1,0:T(8,128)S(1)} %get-tuple-element.73.refs_2_, f32[2,128,128]{2,1,0:T(8,128)S(1)} %get-tuple-element.74.refs_3_, ...), custom_call_target="tpu_custom_call" | custom-call | flops 1000000 | bytes 3000000 | tf_op jit(solution)/shard_map/pallas_call | solution.py:427
  (53 shorter events, 0.7 us)
Async XLA Ops:
  0.6 4.1 %copy-start.1 = (f32[2,128,256]{2,1,0:T(8,128)S(1)}, f32[2,128,256]{2,1,0:T(8,128)}, u32[]{:S(2)}) copy-start(f32[2,128,256]{2,1,0:T(8,128)} %refs_0_.1) | copy-start | bytes 786436
  1.7 6.5 %collective-permute-start.1 = (f32[2,128,128]{2,1,0:T(8,128)S(1)}, f32[2,128,128]{2,1,0:T(8,128)S(1)}, u32[]{:S(2)}, u32[]{:S(2)}) collective-permute-start(f32[2,128,128]{2,1,0:T(8,128)S(1)} %get-tuple-element.110), channel_id=1, source_target_pairs={{0,1},{1,0},{2,3},{3,2},{4,5},{5,4},{6,7},{7,6},{8,9},{9,8},{10,11... | collective-permute-start | bytes 393224 | tf_op jit(solution)/shard_map/ppermute | solution.py:522
  4.7 6.5 %collective-permute-start.2 = (f32[2,128,256]{2,1,0:T(8,128)S(1)}, f32[2,128,256]{2,1,0:T(8,128)}, u32[]{:S(2)}, u32[]{:S(2)}) collective-permute-start(f32[2,128,256]{2,1,0:T(8,128)S(1)} %copy-done.1), channel_id=1, source_target_pairs={{8,24},{16,0},{24,16},{0,8},{9,25},{17,1},{25,17},{1,9},{10,26},{1... | collective-permute-start | bytes 786440 | tf_op jit(solution)/shard_map/ppermute | solution.py:526
  4.7 6.0 %collective-permute-start = (f32[2,128,128]{2,1,0:T(8,128)S(1)}, f32[2,128,128]{2,1,0:T(8,128)S(1)}, u32[]{:S(2)}, u32[]{:S(2)}) collective-permute-start(f32[2,128,128]{2,1,0:T(8,128)S(1)} %get-tuple-element.111), channel_id=1, source_target_pairs={{1,2},{3,4},{5,6},{2,1},{4,3},{6,5},{9,10},{11,12},{13,14},{10,9},... | collective-permute-start | bytes 393224 | tf_op jit(solution)/shard_map/ppermute | solution.py:523
  8.2 5.8 %copy-start = (f32[2,256,256]{2,1,0:T(8,128)S(1)}, f32[2,256,256]{2,1,0:T(8,128)}, u32[]{:S(2)}) copy-start(f32[2,256,256]{2,1,0:T(8,128)} %probe.4) | copy-start | bytes 1572868
  8.2 5.0 %collective-permute-start.3 = (f32[2,128,128]{2,1,0:T(8,128)S(1)}, f32[2,128,128]{2,1,0:T(8,128)S(1)}, u32[]{:S(2)}, u32[]{:S(2)}) collective-permute-start(f32[2,128,128]{2,1,0:T(8,128)S(1)} %collective-permute-done.1.pair_rim), channel_id=1, source_target_pairs={{8,24},{16,0},{24,16},{0,8},{9,25},{17,1},{25,17},{1,9},{10,26},{1... | collective-permute-start | bytes 393224 | tf_op jit(solution)/shard_map/ppermute | solution.py:526
  8.2 10.1 %collective-permute-start.5 = (f32[2,128,256]{2,1,0:T(8,128)S(1)}, f32[2,128,256]{2,1,0:T(8,128)S(1)}, u32[]{:S(2)}, u32[]{:S(2)}) collective-permute-start(f32[2,128,256]{2,1,0:T(8,128)S(1)} %copy-done.1), channel_id=1, source_target_pairs={{0,8},{8,0},{16,24},{24,16},{1,9},{9,1},{17,25},{25,17},{2,10},{10... | collective-permute-start | bytes 786440 | tf_op jit(solution)/shard_map/ppermute | solution.py:498
  8.6 4.7 %copy-start.3 = (s32[4,8,2,2]{1,3,2,0:T(2,128)S(1)}, s32[4,8,2,2]{1,3,2,0:T(2,128)}, u32[]{:S(2)}) copy-start(s32[4,8,2,2]{1,3,2,0:T(2,128)} %param.8) | copy-start | bytes 1540
  13.2 0.7 %copy-start.4 = (f32[2,128,128]{2,1,0:T(8,128)}, f32[2,128,128]{2,1,0:T(8,128)S(1)}, u32[]{:S(2)}) copy-start(f32[2,128,128]{2,1,0:T(8,128)S(1)} %collective-permute-done.3) | copy-start | bytes 393220
  13.2 0.8 %copy-start.2 = (s32[4,8]{1,0:T(4,128)S(1)}, s32[4,8]{1,0:T(4,128)}, u32[]{:S(2)}) copy-start(s32[4,8]{1,0:T(4,128)} %counts.3) | copy-start | bytes 388
  13.2 5.1 %collective-permute-start.4 = (f32[2,128,128]{2,1,0:T(8,128)S(1)}, f32[2,128,128]{2,1,0:T(8,128)}, u32[]{:S(2)}, u32[]{:S(2)}) collective-permute-start(f32[2,128,128]{2,1,0:T(8,128)S(1)} %collective-permute-done.other_rim), channel_id=1, source_target_pairs={{8,24},{16,0},{24,16},{0,8},{9,25},{17,1},{25,17},{1,9},{10,26},{1... | collective-permute-start | bytes 393224 | tf_op jit(solution)/shard_map/ppermute | solution.py:529
  13.2 6.4 %collective-permute-start.8 = (f32[2,128,256]{2,1,0:T(8,128)}, f32[2,128,256]{2,1,0:T(8,128)S(1)}, u32[]{:S(2)}, u32[]{:S(2)}) collective-permute-start(f32[2,128,256]{2,1,0:T(8,128)} %collective-permute-done.2), channel_id=1, source_target_pairs={{0,8},{8,0},{16,24},{24,16},{1,9},{9,1},{17,25},{25,17},{2,10},{10... | collective-permute-start | bytes 786440 | tf_op jit(solution)/shard_map/ppermute | solution.py:498
  13.4 5.4 %collective-permute-start.6 = (f32[2,128,128]{2,1,0:T(8,128)S(1)}, f32[2,128,128]{2,1,0:T(8,128)S(1)}, u32[]{:S(2)}, u32[]{:S(2)}) collective-permute-start(f32[2,128,128]{2,1,0:T(8,128)S(1)} %collective-permute-done.1.pair_rim), channel_id=1, source_target_pairs={{0,8},{8,0},{16,24},{24,16},{1,9},{9,1},{17,25},{25,17},{2,10},{10... | collective-permute-start | bytes 393224 | tf_op jit(solution)/shard_map/ppermute | solution.py:498
  13.9 4.9 %collective-permute-start.7 = (f32[2,128,128]{2,1,0:T(8,128)S(1)}, f32[2,128,128]{2,1,0:T(8,128)S(1)}, u32[]{:S(2)}, u32[]{:S(2)}) collective-permute-start(f32[2,128,128]{2,1,0:T(8,128)S(1)} %collective-permute-done.other_rim), channel_id=1, source_target_pairs={{0,8},{8,0},{16,24},{24,16},{1,9},{9,1},{17,25},{25,17},{2,10},{10... | collective-permute-start | bytes 393224 | tf_op jit(solution)/shard_map/ppermute | solution.py:498
  14.0 4.2 %copy-start.5 = (f32[2,128,128]{2,1,0:T(8,128)S(1)}, f32[2,128,128]{2,1,0:T(8,128)}, u32[]{:S(2)}) copy-start(f32[2,128,128]{2,1,0:T(8,128)} %copy-done.4) | copy-start | bytes 393220
  18.3 1.3 %collective-permute-start.9 = (f32[2,128,128]{2,1,0:T(8,128)S(1)}, f32[2,128,128]{2,1,0:T(8,128)S(1)}, u32[]{:S(2)}, u32[]{:S(2)}) collective-permute-start(f32[2,128,128]{2,1,0:T(8,128)S(1)} %copy-done.5), channel_id=1, source_target_pairs={{0,8},{8,0},{16,24},{24,16},{1,9},{9,1},{17,25},{25,17},{2,10},{10... | collective-permute-start | bytes 393224 | tf_op jit(solution)/shard_map/ppermute | solution.py:498
  18.3 1.7 %collective-permute-start.10 = (f32[2,128,128]{2,1,0:T(8,128)}, f32[2,128,128]{2,1,0:T(8,128)S(1)}, u32[]{:S(2)}, u32[]{:S(2)}) collective-permute-start(f32[2,128,128]{2,1,0:T(8,128)} %collective-permute-done.4), channel_id=1, source_target_pairs={{0,8},{8,0},{16,24},{24,16},{1,9},{9,1},{17,25},{25,17},{2,10},{10... | collective-permute-start | bytes 393224 | tf_op jit(solution)/shard_map/ppermute | solution.py:498
  24.3 1.8 %collective-permute-start.11 = (f32[776,128]{1,0:T(8,128)S(1)}, f32[776,128]{1,0:T(8,128)S(1)}, u32[]{:S(2)}, u32[]{:S(2)}) collective-permute-start(f32[776,128]{1,0:T(8,128)S(1)} %get-tuple-element.69), channel_id=1, source_target_pairs={{0,8},{8,0},{16,24},{24,16},{1,9},{9,1},{17,25},{25,17},{2,10},{10... | collective-permute-start | bytes 1191944 | tf_op jit(solution)/shard_map/ppermute | solution.py:498
  26.2 7.3 %collective-permute-start.12 = (f32[392,128]{1,0:T(8,128)S(1)}, f32[392,128]{1,0:T(8,128)S(1)}, u32[]{:S(2)}, u32[]{:S(2)}) collective-permute-start(f32[392,128]{1,0:T(8,128)S(1)} %get-tuple-element.76), channel_id=1, source_target_pairs={{0,16},{8,24},{16,0},{24,8},{1,17},{9,25},{17,1},{25,9},{2,18},{10... | collective-permute-start | bytes 602120 | tf_op jit(solution)/shard_map/ppermute | solution.py:498
  28.4 1.4 %collective-permute-start.13 = (f32[2,128,128]{2,1,0:T(8,128)S(1)}, f32[2,128,128]{2,1,0:T(8,128)S(1)}, u32[]{:S(2)}, u32[]{:S(2)}) collective-permute-start(f32[2,128,128]{2,1,0:T(8,128)S(1)} %get-tuple-element.78), channel_id=1, source_target_pairs={{0,8},{8,0},{16,24},{24,16},{1,9},{9,1},{17,25},{25,17},{2,10},{10... | collective-permute-start | bytes 393224 | tf_op jit(solution)/shard_map/ppermute | solution.py:498
  28.5 1.5 %collective-permute-start.14 = (f32[2,128,128]{2,1,0:T(8,128)S(1)}, f32[2,128,128]{2,1,0:T(8,128)S(1)}, u32[]{:S(2)}, u32[]{:S(2)}) collective-permute-start(f32[2,128,128]{2,1,0:T(8,128)S(1)} %get-tuple-element.79), channel_id=1, source_target_pairs={{0,8},{8,0},{16,24},{24,16},{1,9},{9,1},{17,25},{25,17},{2,10},{10... | collective-permute-start | bytes 393224 | tf_op jit(solution)/shard_map/ppermute | solution.py:498
  29.0 1.4 %collective-permute-start.15 = (f32[2,128,128]{2,1,0:T(8,128)S(1)}, f32[2,128,128]{2,1,0:T(8,128)S(1)}, u32[]{:S(2)}, u32[]{:S(2)}) collective-permute-start(f32[2,128,128]{2,1,0:T(8,128)S(1)} %get-tuple-element.80), channel_id=1, source_target_pairs={{0,8},{8,0},{16,24},{24,16},{1,9},{9,1},{17,25},{25,17},{2,10},{10... | collective-permute-start | bytes 393224 | tf_op jit(solution)/shard_map/ppermute | solution.py:498
  29.0 4.5 %collective-permute-start.16 = (f32[2,128,128]{2,1,0:T(8,128)S(1)}, f32[2,128,128]{2,1,0:T(8,128)S(1)}, u32[]{:S(2)}, u32[]{:S(2)}) collective-permute-start(f32[2,128,128]{2,1,0:T(8,128)S(1)} %get-tuple-element.81), channel_id=1, source_target_pairs={{0,8},{8,0},{16,24},{24,16},{1,9},{9,1},{17,25},{25,17},{2,10},{10... | collective-permute-start | bytes 393224 | tf_op jit(solution)/shard_map/ppermute | solution.py:498
  29.8 3.7 %collective-permute-start.17 = (f32[2,128,128]{2,1,0:T(8,128)S(1)}, f32[2,128,128]{2,1,0:T(8,128)S(1)}, u32[]{:S(2)}, u32[]{:S(2)}) collective-permute-start(f32[2,128,128]{2,1,0:T(8,128)S(1)} %get-tuple-element.82), channel_id=1, source_target_pairs={{0,8},{8,0},{16,24},{24,16},{1,9},{9,1},{17,25},{25,17},{2,10},{10... | collective-permute-start | bytes 393224 | tf_op jit(solution)/shard_map/ppermute | solution.py:498
  30.0 3.5 %collective-permute-start.18 = (f32[2,128,128]{2,1,0:T(8,128)S(1)}, f32[2,128,128]{2,1,0:T(8,128)S(1)}, u32[]{:S(2)}, u32[]{:S(2)}) collective-permute-start(f32[2,128,128]{2,1,0:T(8,128)S(1)} %get-tuple-element.83), channel_id=1, source_target_pairs={{0,8},{8,0},{16,24},{24,16},{1,9},{9,1},{17,25},{25,17},{2,10},{10... | collective-permute-start | bytes 393224 | tf_op jit(solution)/shard_map/ppermute | solution.py:498
  30.3 3.2 %collective-permute-start.19 = (f32[2,128,128]{2,1,0:T(8,128)S(1)}, f32[2,128,128]{2,1,0:T(8,128)S(1)}, u32[]{:S(2)}, u32[]{:S(2)}) collective-permute-start(f32[2,128,128]{2,1,0:T(8,128)S(1)} %get-tuple-element.84), channel_id=1, source_target_pairs={{0,8},{8,0},{16,24},{24,16},{1,9},{9,1},{17,25},{25,17},{2,10},{10... | collective-permute-start | bytes 393224 | tf_op jit(solution)/shard_map/ppermute | solution.py:498
  33.5 1.3 %collective-permute-start.20 = (f32[2,128,128]{2,1,0:T(8,128)S(1)}, f32[2,128,128]{2,1,0:T(8,128)S(1)}, u32[]{:S(2)}, u32[]{:S(2)}) collective-permute-start(f32[2,128,128]{2,1,0:T(8,128)S(1)} %get-tuple-element.85), channel_id=1, source_target_pairs={{0,8},{8,0},{16,24},{24,16},{1,9},{9,1},{17,25},{25,17},{2,10},{10... | collective-permute-start | bytes 393224 | tf_op jit(solution)/shard_map/ppermute | solution.py:498
  34.8 6.1 %collective-permute-start.22 = (f32[2,128,128]{2,1,0:T(8,128)S(1)}, f32[2,128,128]{2,1,0:T(8,128)S(1)}, u32[]{:S(2)}, u32[]{:S(2)}) collective-permute-start(f32[2,128,128]{2,1,0:T(8,128)S(1)} %collective-permute-done.19), channel_id=1, source_target_pairs={{24,8},{0,16},{16,24},{8,0},{25,9},{1,17},{17,25},{9,1},{26,10},{2... | collective-permute-start | bytes 393224 | tf_op jit(solution)/shard_map/ppermute | solution.py:556
  35.2 5.7 %collective-permute-start.23 = (f32[2,128,128]{2,1,0:T(8,128)S(1)}, f32[2,128,128]{2,1,0:T(8,128)S(1)}, u32[]{:S(2)}, u32[]{:S(2)}) collective-permute-start(f32[2,128,128]{2,1,0:T(8,128)S(1)} %collective-permute-done.20), channel_id=1, source_target_pairs={{24,8},{0,16},{16,24},{8,0},{25,9},{1,17},{17,25},{9,1},{26,10},{2... | collective-permute-start | bytes 393224 | tf_op jit(solution)/shard_map/ppermute | solution.py:556
  35.4 5.5 %collective-permute-start.21 = (f32[200,128]{1,0:T(8,128)S(1)}, f32[200,128]{1,0:T(8,128)S(1)}, u32[]{:S(2)}, u32[]{:S(2)}) collective-permute-start(f32[200,128]{1,0:T(8,128)S(1)} %get-tuple-element.89), channel_id=1, source_target_pairs={{0,1},{1,0},{2,3},{3,2},{4,5},{5,4},{6,7},{7,6},{8,9},{9,8},{10,11... | collective-permute-start | bytes 307208 | tf_op jit(solution)/shard_map/ppermute | solution.py:498
  37.5 8.9 %collective-permute-start.25 = (f32[2,128,128]{2,1,0:T(8,128)S(1)}, f32[2,128,128]{2,1,0:T(8,128)S(1)}, u32[]{:S(2)}, u32[]{:S(2)}) collective-permute-start(f32[2,128,128]{2,1,0:T(8,128)S(1)} %collective-permute-done.17), channel_id=1, source_target_pairs={{24,8},{0,16},{16,24},{8,0},{25,9},{1,17},{17,25},{9,1},{26,10},{2... | collective-permute-start | bytes 393224 | tf_op jit(solution)/shard_map/ppermute | solution.py:556
  38.5 8.0 %collective-permute-start.26 = (f32[2,128,128]{2,1,0:T(8,128)S(1)}, f32[2,128,128]{2,1,0:T(8,128)S(1)}, u32[]{:S(2)}, u32[]{:S(2)}) collective-permute-start(f32[2,128,128]{2,1,0:T(8,128)S(1)} %collective-permute-done.18), channel_id=1, source_target_pairs={{24,8},{0,16},{16,24},{8,0},{25,9},{1,17},{17,25},{9,1},{26,10},{2... | collective-permute-start | bytes 393224 | tf_op jit(solution)/shard_map/ppermute | solution.py:556
  41.0 5.5 %collective-permute-start.24 = (f32[264,128]{1,0:T(8,128)S(1)}, f32[264,128]{1,0:T(8,128)S(1)}, u32[]{:S(2)}, u32[]{:S(2)}) collective-permute-start(f32[264,128]{1,0:T(8,128)S(1)} %concatenate.21), channel_id=1, source_target_pairs={{0,2},{1,3},{2,0},{3,1},{4,6},{5,7},{6,4},{7,5},{8,10},{9,11},{10,... | collective-permute-start | bytes 405512 | tf_op jit(solution)/shard_map/ppermute | solution.py:498
  43.2 11.5 %collective-permute-start.28 = (f32[2,128,128]{2,1,0:T(8,128)S(1)}, f32[2,128,128]{2,1,0:T(8,128)S(1)}, u32[]{:S(2)}, u32[]{:S(2)}) collective-permute-start(f32[2,128,128]{2,1,0:T(8,128)S(1)} %select_add_fusion.1), channel_id=1, source_target_pairs={{1,2},{3,4},{5,6},{2,1},{4,3},{6,5},{9,10},{11,12},{13,14},{10,9},... | collective-permute-start | bytes 393224 | tf_op jit(solution)/shard_map/ppermute | solution.py:564
  46.5 8.2 %collective-permute-start.27 = (f32[200,128]{1,0:T(8,128)S(1)}, f32[200,128]{1,0:T(8,128)S(1)}, u32[]{:S(2)}, u32[]{:S(2)}) collective-permute-start(f32[200,128]{1,0:T(8,128)S(1)} %slice_add_fusion), channel_id=1, source_target_pairs={{0,6},{1,7},{2,4},{3,5},{4,2},{5,3},{6,0},{7,1},{8,14},{9,15},{10,... | collective-permute-start | bytes 307208 | tf_op jit(solution)/shard_map/ppermute | solution.py:498
  54.8 5.6 %collective-permute-start.29 = (f32[2,64,128]{2,1,0:T(8,128)S(1)}, f32[2,64,128]{2,1,0:T(8,128)S(1)}, u32[]{:S(2)}, u32[]{:S(2)}) collective-permute-start(f32[2,64,128]{2,1,0:T(8,128)S(1)} %fusion), channel_id=1, source_target_pairs={{0,1},{1,0},{2,3},{3,2},{4,5},{5,4},{6,7},{7,6},{8,9},{9,8},{10,11... | collective-permute-start | bytes 196616 | tf_op jit(solution)/shard_map/ppermute | solution.py:498
  54.9 5.5 %collective-permute-start.31 = (f32[2,64,128]{2,1,0:T(8,128)S(1)}, f32[2,64,128]{2,1,0:T(8,128)S(1)}, u32[]{:S(2)}, u32[]{:S(2)}) collective-permute-start(f32[2,64,128]{2,1,0:T(8,128)S(1)} %fusion), channel_id=1, source_target_pairs={{0,17},{1,16},{2,19},{3,18},{4,21},{5,20},{6,23},{7,22},{8,25},{9,... | collective-permute-start | bytes 196616 | tf_op jit(solution)/shard_map/ppermute | solution.py:545
  57.3 4.3 %collective-permute-start.30 = (f32[2,64,128]{2,1,0:T(8,128)S(1)}, f32[2,64,128]{2,1,0:T(8,128)S(1)}, u32[]{:S(2)}, u32[]{:S(2)}) collective-permute-start(f32[2,64,128]{2,1,0:T(8,128)S(1)} %fusion), channel_id=1, source_target_pairs={{0,16},{8,24},{16,0},{24,8},{1,17},{9,25},{17,1},{25,9},{2,18},{10... | collective-permute-start | bytes 196616 | tf_op jit(solution)/shard_map/ppermute | solution.py:498
  58.3 5.0 %collective-permute-start.32 = (f32[2,128,128]{2,1,0:T(8,128)S(1)}, f32[2,128,128]{2,1,0:T(8,128)S(1)}, u32[]{:S(2)}, u32[]{:S(2)}) collective-permute-start(f32[2,128,128]{2,1,0:T(8,128)S(1)} %select_add_fusion), channel_id=1, source_target_pairs={{0,1},{1,0},{2,3},{3,2},{4,5},{5,4},{6,7},{7,6},{8,9},{9,8},{10,11... | collective-permute-start | bytes 393224 | tf_op jit(solution)/shard_map/ppermute | solution.py:577
  63.3 1.5 %collective-permute-start.33 = (f32[2,256,128]{2,1,0:T(8,128)S(1)}, f32[2,256,128]{2,1,0:T(8,128)S(1)}, u32[]{:S(2)}, u32[]{:S(2)}) collective-permute-start(f32[2,256,128]{2,1,0:T(8,128)S(1)} %maximum_select_fusion.refs_10_), channel_id=1, source_target_pairs={{0,8},{8,0},{16,24},{24,16},{1,9},{9,1},{17,25},{25,17},{2,10},{10... | collective-permute-start | bytes 786440 | tf_op jit(solution)/shard_map/ppermute | solution.py:498

commit v5 on v4

--- a/solution.py
+++ b/solution.py
@@ -279,10 +279,10 @@
 def place_kernel(
     offsets, probe, delta, *blocks_and_ext
 ):
-    *blocks, ext = blocks_and_ext
+    center_mid, center_rim, packet, ext = blocks_and_ext
     slots, width = delta.shape[0], delta.shape[2]
     half = width // 2
-    tile_r = blocks[0].shape[1]
+    tile_r = center_mid.shape[1]
     tile_c = ext.shape[2] - 2 * half
     row_place = lax.axis_index("row")
     col_place = lax.axis_index("col")
@@ -303,13 +303,17 @@
     far_row = pl.multiple_of(row_odd * (tile_r + half), half)
     pair_col = pl.multiple_of((1 - col_odd) * (tile_c + half), half)
     other_col = pl.multiple_of(col_odd * (tile_c + half), half)
-    for k, row in enumerate((half, near_row, far_row)):
-        low, high, pair, other = blocks[4 * k : 4 * k + 4]
+    middle = tile_c // 2
+    for row, rim, mid in (
+        (half, center_rim, center_mid),
+        (far_row, packet.at[0:4], packet.at[4:8]),
+        (near_row, packet.at[8:12], packet.at[12:16]),
+    ):
         at = pl.ds(row, tile_r)
-        low[...] = ext[:, at, half : half + tile_c // 2]
-        high[...] = ext[:, at, half + tile_c // 2 : half + tile_c]
-        pair[...] = ext[:, at, pl.ds(pair_col, half)]
-        other[...] = ext[:, at, pl.ds(other_col, half)]
+        mid[0:2] = ext[:, at, half : half + middle]
+        mid[2:4] = ext[:, at, half + middle : half + tile_c]
+        rim[0:2] = ext[:, at, pl.ds(pair_col, half)]
+        rim[2:4] = ext[:, at, pl.ds(other_col, half)]
 
 
 def stage_kernel(magnitudes, tables, ordered, held, measured, arrived):
@@ -396,12 +400,10 @@
     )(offsets, counts, probe, *map(in_vmem, staged), *map(in_vmem, blocks))
 
 
-def finish_kernel(*refs):
-    (
-        specimen, light, low, high, close_low, close_high, far_low, far_high, pair, other,
-        fresh, got, specimen_next, probe_next,
-    ) = refs
-    half = pair.shape[2]
+def finish_kernel(
+    specimen, light, center, close, far, both, other, fresh, got, specimen_next, probe_next
+):
+    half = other.shape[2]
     row_place = lax.axis_index("row")
     col_place = lax.axis_index("col")
     row_odd = lax.rem(row_place, 2)
@@ -409,13 +411,15 @@
     far_at = row_place + 2 * row_odd - 1
     inside = (far_at >= 0) & (far_at < lax.axis_size("row"))
     for part in range(2):
-        sides = (
-            (low, close_low, far_low, jnp.where(col_odd == 0, other[part], pair[part])),
-            (high, close_high, far_high, jnp.where(col_odd == 0, pair[part], other[part])),
+        pair = both[part]
+        rims = (
+            jnp.where(col_odd == 0, other[part], pair),
+            jnp.where(col_odd == 0, pair, other[part]),
         )
-        for side, (own, close, far, rim) in enumerate(sides):
+        for side, rim in enumerate(rims):
             at = slice(side * half, (side + 1) * half)
-            total = own[part] + close[part] + jnp.where(inside, far[part], 0.0) + rim
+            k = 2 * side + part
+            total = center[k] + close[k] + jnp.where(inside, far[k], 0.0) + rim
             specimen_next[part, :, at] = specimen[part, :, at] + total / light[:, at]
         mine, theirs = fresh[part], got[part]
         probe_next[part, :, :LANES] = jnp.where(row_odd == 0, mine, theirs)
@@ -445,30 +449,29 @@
     return pltpu.with_memory_space_constraint(value, pltpu.VMEM)
 
 
-def fold_kernel(axis, bit, kept_in, got, kept, given):
+def fold_kernel(kept, got, own, across, beside, diagonal):
     layers = 3
-    size = (kept.shape[0] - SUBLANES) // layers
-    odd = lax.rem(lax.axis_index(axis) // bit, 2)
-    for layer in range(layers):
-        first = 2 * layer * size
-        mine = pl.ds(pl.multiple_of(first + odd * size, SUBLANES), size)
-        other = pl.ds(pl.multiple_of(first + (1 - odd) * size, SUBLANES), size)
-        at = slice(layer * size, (layer + 1) * size)
-        kept[at] = kept_in[mine] + got[mine]
-        given[at] = kept_in[other] + got[other]
-    total = kept_in[2 * layers * size :] + got[2 * layers * size :]
-    kept[layers * size :] = total
-    given[layers * size :] = total
-
-
-def fold(kept, got, axis, bit):
+    size = (own.shape[0] - SUBLANES) // layers
+    here = 2 * lax.rem(lax.axis_index("row") // 2, 2) + lax.rem(lax.axis_index("col"), 2)
+    total = kept[4 * layers * size :] + got[4 * layers * size :]
+    for flip, out in enumerate((own, beside, across, diagonal)):
+        row = 2 * (here // 2) + lax.rem(here, 2)
+        row = (row // 2 + flip // 2) % 2 * 2 + (row % 2 + flip % 2) % 2
+        for layer in range(layers):
+            first = pl.multiple_of((4 * layer + row) * size, SUBLANES)
+            at = pl.ds(first, size)
+            out[layer * size : (layer + 1) * size] = kept[at] + got[at]
+        out[layers * size :] = total
+
+
+def fold(kept, got):
     vmem = pl.BlockSpec(memory_space=pltpu.VMEM)
-    shape = jax.ShapeDtypeStruct(((kept.shape[0] + SUBLANES) // 2, LANES), jnp.float32)
+    rows = (kept.shape[0] - SUBLANES) // 4 + SUBLANES
     return pl.pallas_call(
-        functools.partial(fold_kernel, axis, bit),
-        out_shape=[shape] * 2,
+        fold_kernel,
+        out_shape=[jax.ShapeDtypeStruct((rows, LANES), jnp.float32)] * 4,
         in_specs=[vmem] * 2,
-        out_specs=[vmem] * 2,
+        out_specs=[vmem] * 4,
         compiler_params=pltpu.CompilerParams(vmem_limit_bytes=VMEM_LIMIT),
         cost_estimate=pl.CostEstimate(flops=100000, bytes_accessed=400000, transcendentals=0),
     )(in_vmem(kept), in_vmem(got))
@@ -479,13 +482,12 @@
     half = width // 2
     smem = pl.BlockSpec(memory_space=pltpu.SMEM)
     vmem = pl.BlockSpec(memory_space=pltpu.VMEM)
-    middle = jax.ShapeDtypeStruct((2, tile_r, tile_c // 2), jnp.float32)
-    rim = jax.ShapeDtypeStruct((2, tile_r, half), jnp.float32)
+    block = jax.ShapeDtypeStruct((4, tile_r, half), jnp.float32)
     return pl.pallas_call(
         place_kernel,
-        out_shape=[middle, middle, rim, rim] * 3,
+        out_shape=[block, block, jax.ShapeDtypeStruct((16, tile_r, half), jnp.float32)],
         in_specs=[smem, vmem, vmem],
-        out_specs=[vmem] * 12,
+        out_specs=[vmem] * 3,
         scratch_shapes=[
             pltpu.VMEM((2, tile_r + 2 * half + SUBLANES, tile_c + 2 * half), jnp.float32),
         ],
@@ -545,26 +547,23 @@
         diagonal = lax.ppermute(diagonal, ("row", "col"), square)
         return exchange(across, "row", rows, 2), exchange(beside, "col", cols, 1), diagonal
 
-    kept, given = fold(kept, exchange(given, "row", rows, 1), "row", 2)
-    given, delta = tie((given, delta))
-    parts = place(scan_offsets, probe_field, delta, tile_r, tile_c)
-    center, close, onward = parts[:4], parts[4:8], parts[8:]
-    got_close, got_onward = core(close), core(onward)
-    got = exchange(given, "row", rows, 2)
-    kept, given = fold(kept, got, "col", 1)
-    given, got_close, got_onward = tie((given, got_close, got_onward))
-    beyond = [lax.ppermute(block, "row", onward_pairs) for block in got_onward]
+    got = exchange(given, "row", rows, 1)
+    center_mid, center_rim, packet = place(scan_offsets, probe_field, delta, tile_r, tile_c)
+    got, packet = tie((got, packet))
+    packet = exchange(packet, "row", rows, 1)
+    value, across, beside, diagonal = fold(kept, got)
+    beyond_rim = lax.ppermute(packet[:4], "row", onward_pairs)
+    beyond_mid = lax.ppermute(packet[4:8], "row", onward_pairs)
+    across, beside, diagonal = all_three(across, beside, diagonal)
+    value = (value + across) + (beside + diagonal)
+    value, beyond_rim = tie((value, beyond_rim))
     inside = (row_place + 2 * row_odd - 1 >= 0) & (row_place + 2 * row_odd - 1 < rows)
-    value = kept + exchange(given, "col", cols, 1)
-    value, *beyond[2:] = tie((value, *beyond[2:]))
-    pair_part, other_part = (
-        first + second + pick(inside, third, 0.0)
-        for first, second, third in zip(center[2:], got_close[2:], beyond[2:])
-    )
-    other_part = lax.ppermute(other_part, "col", others)
+    rim = center_rim + packet[8:12] + pick(inside, beyond_rim, 0.0)
+    pair_part = rim[:2]
+    other_part = lax.ppermute(rim[2:], "col", others)
     filled = jnp.concatenate([value, jnp.zeros((64, LANES), jnp.float32)])
     value = value + exchange(filled, "col", cols, 2)[: value.shape[0]]
-    value, beyond = tie((value, beyond))
+    value, beyond_mid = tie((value, beyond_mid))
     for bit in (1 << k for k in range(2, cols.bit_length() - 1)):
         value = value + exchange(value, "col", cols, 2 * bit - 2)
     for bit in (1 << k for k in range(2, rows.bit_length() - 1)):
@@ -574,8 +573,11 @@
     real, imag, weight, total = (value[k * size : (k + 1) * size] for k in range(4))
     update = jnp.stack([real, imag]) / (weight + probe_damping * (total[:1] / (width * width)))
     fresh = own_probe + update
-    pair_part = lax.ppermute(pair_part, "col", pairs)
-    across, beside, diagonal = all_three(fresh, fresh, fresh)
+    size = fresh.size // LANES
+    both = jnp.concatenate([fresh.reshape(size, LANES), pair_part.reshape(-1, LANES)])
+    across, both, diagonal = all_three(fresh, both, fresh)
+    beside = both[:size].reshape(fresh.shape)
+    pair_part = both[size:].reshape(pair_part.shape)
 
     def ordered(place_here, one, other):
         return pick(
@@ -587,10 +589,9 @@
     fresh = ordered(
         (row_place // 2) % 2, ordered(col_odd, fresh, beside), ordered(col_odd, across, diagonal)
     )
-    fresh, pair_part = tie((fresh, pair_part))
     got = exchange(fresh, "row", rows, 1)
     return finish(
-        specimen, probe_field, light, *center[:2], *got_close[:2], *beyond[:2],
+        specimen, probe_field, light, center_mid, packet[12:], beyond_mid,
         pair_part, other_part, fresh, got,
     )
 

time: 66 us -> 63.1 us (0.956)
  waiting for transfers between devices: 30.1 us -> 28 us
  starting transfers between devices: 22.1 us -> 21.2 us
    ppermute x22 -> x15, waiting for transfers between devices: 21 us -> 13.4 us  [exchange(): return lax.ppermute(value, axis, [(i, i ^ bit) for i in range(count)])]
    ppermute x1 -> x2, waiting for transfers between devices: 0.01 us -> 4.15 us  [all_three(): diagonal = lax.ppermute(diagonal, ('row', 'col'), square)]
    ppermute x22 -> x15, starting transfers between devices: 13.6 us -> 11.4 us  [exchange(): return lax.ppermute(value, axis, [(i, i ^ bit) for i in range(count)])]
    ppermute x6 -> x3, waiting for transfers between devices: 1.73 us -> 3.05 us  [the longest x1 2.93 us: shards(): beyond_mid = lax.ppermute(packet[4:8], 'row', onward_pairs)]
    ppermute x6 -> x3, starting transfers between devices: 2.36 us -> 3.62 us  [the longest x1 2.5 us: shards(): beyond_mid = lax.ppermute(packet[4:8], 'row', onward_pairs)]
    ppermute x1 -> x2, starting transfers between devices: 2.38 us -> 2.51 us  [all_three(): diagonal = lax.ppermute(diagonal, ('row', 'col'), square)]
    pallas_call x3 -> x2, Pallas kernels: 1.8 us -> 1.82 us  [the longest x1 1.76 us: place(): pl.pallas_call(place_kernel, out_shape=[block, block, jax.ShapeDtypeStruc...]
  transfers between devices with their start and end apart: 34 -> 25, of which waited for: 17 -> 17; matrix products, arithmetic and copies ran while one was open for 0% -> 1% of each run, Pallas kernels for 9% -> 10%
where the time goes in v5:
time: 63.1 us; the launch traced here: 62.9 us
  waiting for transfers between devices  28 us (44%)
  starting transfers between devices  21.2 us (34%)
  Pallas kernels  11.4 us (18%)
  other arithmetic  1.25 us (2%)
  between operations  0.84 us (1%)
    ppermute x15, waiting for transfers between devices, exchange(): return lax.ppermute(value, axis, [(i, i ^ bit) for i in range(count)])  13.4 us
    ppermute x15, starting transfers between devices, exchange(): return lax.ppermute(value, axis, [(i, i ^ bit) for i in range(count)])  11.4 us
    pallas_call x1, Pallas kernels, exit_update(): pl.pallas_call(delta_kernel, out_shape=[jax.ShapeDtypeStruct((3 * width +...  4.3 us
    ppermute x2, waiting for transfers between devices, all_three(): diagonal = lax.ppermute(diagonal, ('row', 'col'), square)  4.15 us
    ppermute x1, starting transfers between devices, shards(): pair_rim = lax.ppermute(jnp.where(col_odd == 0, high, low), 'col', pairs)  3.03 us
    ppermute x1, waiting for transfers between devices, shards(): beyond_mid = lax.ppermute(packet[4:8], 'row', onward_pairs)  2.93 us
    ppermute x1, waiting for transfers between devices, shards(): pair_rim = lax.ppermute(jnp.where(col_odd == 0, high, low), 'col', pairs)  2.82 us
    ppermute x2, starting transfers between devices, all_three(): diagonal = lax.ppermute(diagonal, ('row', 'col'), square)  2.51 us
  transfers between devices with their start and end apart: 25, of which 17 were waited for; matrix products, arithmetic and copies ran while one was open for 1% of the time, Pallas kernels for 10%

profile of v5, /device:TPU:0, one launch (start us, length us, event | category | flops | bytes accessed | tf_op | source)
XLA Modules:
  0.0 62.9 jit_solution(5567427943052458183)
XLA Ops:
  0.7 1.0 %slice_select_fusion = (f32[2,128,128]{2,1,0:T(8,128)S(1)}, f32[2,128,128]{2,1,0:T(8,128)S(1)}) fusion(f32[2,128,256]{2,1,0:T(8,128)} %specimen.1, pred[]{:T(512)S(6)} %eq.13), kind=kLoop, calls=%fused_computation.6 | loop fusion | flops 65536 | bytes 524289 | tf_op jit(solution)/shard_map/jit(_where)/select_n | solution.py:524
  1.7 3.0 %collective-permute-start.1 = (f32[2,128,128]{2,1,0:T(8,128)S(1)}, f32[2,128,128]{2,1,0:T(8,128)S(1)}, u32[]{:S(2)}, u32[]{:S(2)}) collective-permute-start(f32[2,128,128]{2,1,0:T(8,128)S(1)} %get-tuple-element.71), channel_id=1, source_target_pairs={{0,1},{1,0},{2,3},{3,2},{4,5},{5,4},{6,7},{7,6},{8,9},{9,8},{10,11... | collective-permute-start | bytes 393224 | tf_op jit(solution)/shard_map/ppermute | solution.py:524
  4.7 0.0 collective-permute-start.2
  4.7 0.7 %collective-permute-start = (f32[2,128,128]{2,1,0:T(8,128)S(1)}, f32[2,128,128]{2,1,0:T(8,128)S(1)}, u32[]{:S(2)}, u32[]{:S(2)}) collective-permute-start(f32[2,128,128]{2,1,0:T(8,128)S(1)} %get-tuple-element.72), channel_id=1, source_target_pairs={{1,2},{3,4},{5,6},{2,1},{4,3},{6,5},{9,10},{11,12},{13,14},{10,9},... | collective-permute-start | bytes 393224 | tf_op jit(solution)/shard_map/ppermute | solution.py:525
  5.4 2.8 %collective-permute-done.1.pair_rim = f32[2,128,128]{2,1,0:T(8,128)S(1)} collective-permute-done((f32[2,128,128]{2,1,0:T(8,128)S(1)}, f32[2,128,128]{2,1,0:T(8,128)S(1)}, u32[]{:S(2)}, u32[]{:S(2)}) %collective-permute-start.1) | collective-permute-done | bytes 131104 | tf_op jit(solution)/shard_map/ppermute | solution.py:524
  8.2 0.4 collective-permute-start.5
  8.6 2.1 %shard_map.77 = (f32[2,256,256]{2,1,0:T(8,128)S(1)}, bf16[4,2,256,256]{3,2,1,0:T(8,128)(2,1)S(1)}) custom-call(f32[2,256,256]{2,1,0:T(8,128)} %bitcast.13, bf16[4,2,256,256]{3,2,1,0:T(8,128)(2,1)} %constant.55.clone.tables), custom_call_target="tpu_custom_call" | custom-call | flops 400000000 | bytes 3000000 | tf_op jit(solution)/shard_map/pallas_call | solution.py:354
  10.8 0.0 collective-permute-done.other_rim
  10.8 0.4 collective-permute-done.2
  11.2 2.0 %collective-permute-done.3 = f32[2,128,128]{2,1,0:T(8,128)S(1)} collective-permute-done((f32[2,128,128]{2,1,0:T(8,128)S(1)}, f32[2,128,128]{2,1,0:T(8,128)S(1)}, u32[]{:S(2)}, u32[]{:S(2)}) %collective-permute-start.3) | collective-permute-done | bytes 131104 | tf_op jit(solution)/shard_map/ppermute | solution.py:528
  13.2 0.1 copy.8.offsets
  13.3 0.5 collective-permute-start.6
  13.9 0.1 collective-permute-start.7
  14.0 2.2 %shard_map.78.light = f32[128,256]{1,0:T(8,128)S(1)} custom-call(s32[4,8,2,2]{3,2,1,0:T(2,128)S(1)} %copy.8.offsets, s32[4,8]{1,0:T(4,128)S(1)} %copy-done.2, f32[2,256,256]{2,1,0:T(8,128)S(1)} %copy-done), custom_call_target="tpu_custom_call" | custom-call | flops 40000000 | bytes 8000000 | tf_op jit(solution)/shard_map/pallas_call | solution.py:145
  16.1 2.1 %collective-permute-done.4 = f32[2,128,128]{2,1,0:T(8,128)} collective-permute-done((f32[2,128,128]{2,1,0:T(8,128)S(1)}, f32[2,128,128]{2,1,0:T(8,128)}, u32[]{:S(2)}, u32[]{:S(2)}) %collective-permute-start.4) | collective-permute-done | bytes 131104 | tf_op jit(solution)/shard_map/ppermute | solution.py:531
  18.3 0.5 collective-permute-start.10
  18.8 0.9 %collective-permute-done.9.far_pair = f32[2,128,128]{2,1,0:T(8,128)S(1)} collective-permute-done((f32[2,128,128]{2,1,0:T(8,128)S(1)}, f32[2,128,128]{2,1,0:T(8,128)S(1)}, u32[]{:S(2)}, u32[]{:S(2)}) %collective-permute-start.9) | collective-permute-done | bytes 131104 | tf_op jit(solution)/shard_map/ppermute | solution.py:500
  19.7 0.3 collective-permute-done.10.far_other
  20.0 4.3 %shard_map.79 = (f32[776,128]{1,0:T(8,128)S(1)}, f32[776,128]{1,0:T(8,128)S(1)}, f32[2,64,128]{2,1,0:T(8,128)S(1)}, f32[2,2,256,256]{3,2,1,0:T(8,128)S(1)}) custom-call(s32[4,8,2,2]{3,2,1,0:T(2,128)S(1)} %copy.8.offsets, s32[4,8]{1,0:T(4,128)S(1)} %copy-done.2, f32[2,256,256]{2,1,0:T(8,128)S(1)} %copy-done, f32[2,256,256]{2,1,0:T(8,128)S(1)} %get-tuple-element.41.magnitudes, ...), custom_call_target="tpu_custom_call" | custom-call | flops 3200000000 | bytes 8000000 | tf_op jit(solution)/shard_map/pallas_call | solution.py:378
  24.3 0.4 collective-permute-start.11
  24.7 1.8 %shard_map.80 = (f32[4,128,128]{2,1,0:T(8,128)S(1)}, f32[4,128,128]{2,1,0:T(8,128)S(1)}, f32[16,128,128]{2,1,0:T(8,128)S(1)}) custom-call(s32[4,8,2,2]{3,2,1,0:T(2,128)S(1)} %copy.8.offsets, f32[2,256,256]{2,1,0:T(8,128)S(1)} %copy-done, f32[2,2,256,256]{3,2,1,0:T(8,128)S(1)} %get-tuple-element.46.delta), custom_call_target="tpu_custom_call" | custom-call | flops 4000000 | bytes 4000000 | tf_op jit(solution)/shard_map/pallas_call | solution.py:486
  26.5 0.2 collective-permute-start.12
  26.7 0.1 shard_map.81
  26.8 1.8 %collective-permute-start.14 = (f32[200,128]{1,0:T(8,128)S(1)}, f32[200,128]{1,0:T(8,128)S(1)}, u32[]{:S(2)}, u32[]{:S(2)}) collective-permute-start(f32[200,128]{1,0:T(8,128)S(1)} %get-tuple-element.55), channel_id=1, source_target_pairs={{0,1},{1,0},{2,3},{3,2},{4,5},{5,4},{6,7},{7,6},{8,9},{9,8},{10,11... | collective-permute-start | bytes 307208 | tf_op jit(solution)/shard_map/ppermute | solution.py:500
  28.6 0.2 collective-permute-start.15
  28.8 1.6 %collective-permute-start.13 = (f32[200,128]{1,0:T(8,128)S(1)}, f32[200,128]{1,0:T(8,128)S(1)}, u32[]{:S(2)}, u32[]{:S(2)}) collective-permute-start(f32[200,128]{1,0:T(8,128)S(1)} %get-tuple-element.54), channel_id=1, source_target_pairs={{0,16},{8,24},{16,0},{24,8},{1,17},{9,25},{17,1},{25,9},{2,18},{10... | collective-permute-start | bytes 307208 | tf_op jit(solution)/shard_map/ppermute | solution.py:500
  30.4 0.5 collective-permute-start.16
  30.8 2.6 %collective-permute-done.14 = f32[200,128]{1,0:T(8,128)S(1)} collective-permute-done((f32[200,128]{1,0:T(8,128)S(1)}, f32[200,128]{1,0:T(8,128)S(1)}, u32[]{:S(2)}, u32[]{:S(2)}) %collective-permute-start.14) | collective-permute-done | bytes 102432 | tf_op jit(solution)/shard_map/ppermute | solution.py:500
  33.4 1.8 %collective-permute-done.15 = f32[200,128]{1,0:T(8,128)S(1)} collective-permute-done((f32[200,128]{1,0:T(8,128)S(1)}, f32[200,128]{1,0:T(8,128)S(1)}, u32[]{:S(2)}, u32[]{:S(2)}) %collective-permute-start.15) | collective-permute-done | bytes 102432 | tf_op jit(solution)/shard_map/ppermute | solution.py:547
  35.2 1.1 %collective-permute-done.13 = f32[200,128]{1,0:T(8,128)S(1)} collective-permute-done((f32[200,128]{1,0:T(8,128)S(1)}, f32[200,128]{1,0:T(8,128)S(1)}, u32[]{:S(2)}, u32[]{:S(2)}) %collective-permute-start.13) | collective-permute-done | bytes 102432 | tf_op jit(solution)/shard_map/ppermute | solution.py:500
  36.3 0.1 collective-permute-done.16
  36.4 2.1 %collective-permute-start.17 = (f32[264,128]{1,0:T(8,128)S(1)}, f32[264,128]{1,0:T(8,128)S(1)}, u32[]{:S(2)}, u32[]{:S(2)}) collective-permute-start(f32[264,128]{1,0:T(8,128)S(1)} %concatenate.24), channel_id=1, source_target_pairs={{0,2},{1,3},{2,0},{3,1},{4,6},{5,7},{6,4},{7,5},{8,10},{9,11},{10,... | collective-permute-start | bytes 405512 | tf_op jit(solution)/shard_map/ppermute | solution.py:500
  38.5 0.1 fusion
  38.6 2.5 %collective-permute-start.18 = (f32[4,128,128]{2,1,0:T(8,128)S(1)}, f32[4,128,128]{2,1,0:T(8,128)S(1)}, u32[]{:S(2)}, u32[]{:S(2)}) collective-permute-start(f32[4,128,128]{2,1,0:T(8,128)S(1)} %get-tuple-element.67), channel_id=1, source_target_pairs={{24,8},{0,16},{16,24},{8,0},{25,9},{1,17},{17,25},{9,1},{26,10},{2... | collective-permute-start | bytes 786440 | tf_op jit(solution)/shard_map/ppermute | solution.py:556
  41.1 0.7 %collective-permute-start.20 = (f32[2,128,128]{2,1,0:T(8,128)S(1)}, f32[2,128,128]{2,1,0:T(8,128)S(1)}, u32[]{:S(2)}, u32[]{:S(2)}) collective-permute-start(f32[2,128,128]{2,1,0:T(8,128)S(1)} %get-tuple-element.70), channel_id=1, source_target_pairs={{1,2},{3,4},{5,6},{2,1},{4,3},{6,5},{9,10},{11,12},{13,14},{10,9},... | collective-permute-start | bytes 393224 | tf_op jit(solution)/shard_map/ppermute | solution.py:563
  41.8 0.2 collective-permute-done.17
  42.0 2.9 %collective-permute-done.18.far = f32[4,128,128]{2,1,0:T(8,128)S(1)} collective-permute-done((f32[4,128,128]{2,1,0:T(8,128)S(1)}, f32[4,128,128]{2,1,0:T(8,128)S(1)}, u32[]{:S(2)}, u32[]{:S(2)}) %collective-permute-start.18) | collective-permute-done | bytes 262176 | tf_op jit(solution)/shard_map/ppermute | solution.py:556
  45.0 2.5 %collective-permute-start.19 = (f32[200,128]{1,0:T(8,128)S(1)}, f32[200,128]{1,0:T(8,128)S(1)}, u32[]{:S(2)}, u32[]{:S(2)}) collective-permute-start(f32[200,128]{1,0:T(8,128)S(1)} %slice_add_fusion.1), channel_id=1, source_target_pairs={{0,6},{1,7},{2,4},{3,5},{4,2},{5,3},{6,0},{7,1},{8,14},{9,15},{10,... | collective-permute-start | bytes 307208 | tf_op jit(solution)/shard_map/ppermute | solution.py:500
  47.5 5.1 %collective-permute-done.19 = f32[200,128]{1,0:T(8,128)S(1)} collective-permute-done((f32[200,128]{1,0:T(8,128)S(1)}, f32[200,128]{1,0:T(8,128)S(1)}, u32[]{:S(2)}, u32[]{:S(2)}) %collective-permute-start.19) | collective-permute-done | bytes 102432 | tf_op jit(solution)/shard_map/ppermute | solution.py:500
  52.6 0.7 %collective-permute-start.21 = (f32[384,128]{1,0:T(8,128)S(1)}, f32[384,128]{1,0:T(8,128)S(1)}, u32[]{:S(2)}, u32[]{:S(2)}) collective-permute-start(f32[384,128]{1,0:T(8,128)S(1)} %pad_maximum_fusion), channel_id=1, source_target_pairs={{0,1},{1,0},{2,3},{3,2},{4,5},{5,4},{6,7},{7,6},{8,9},{9,8},{10,11... | collective-permute-start | bytes 589832 | tf_op jit(solution)/shard_map/ppermute | solution.py:500
  53.3 2.3 %collective-permute-start.23 = (f32[2,64,128]{2,1,0:T(8,128)S(1)}, f32[2,64,128]{2,1,0:T(8,128)S(1)}, u32[]{:S(2)}, u32[]{:S(2)}) collective-permute-start(f32[2,64,128]{2,1,0:T(8,128)S(1)} %fusion.1), channel_id=1, source_target_pairs={{0,17},{1,16},{2,19},{3,18},{4,21},{5,20},{6,23},{7,22},{8,25},{9,... | collective-permute-start | bytes 196616 | tf_op jit(solution)/shard_map/ppermute | solution.py:547
  55.6 0.6 collective-permute-start.22
  56.2 2.4 %collective-permute-done.23 = f32[2,64,128]{2,1,0:T(8,128)S(1)} collective-permute-done((f32[2,64,128]{2,1,0:T(8,128)S(1)}, f32[2,64,128]{2,1,0:T(8,128)S(1)}, u32[]{:S(2)}, u32[]{:S(2)}) %collective-permute-start.23) | collective-permute-done | bytes 65568 | tf_op jit(solution)/shard_map/ppermute | solution.py:547
  58.6 1.3 %collective-permute-done.22 = f32[2,64,128]{2,1,0:T(8,128)S(1)} collective-permute-done((f32[2,64,128]{2,1,0:T(8,128)S(1)}, f32[2,64,128]{2,1,0:T(8,128)S(1)}, u32[]{:S(2)}, u32[]{:S(2)}) %collective-permute-start.22) | collective-permute-done | bytes 65568 | tf_op jit(solution)/shard_map/ppermute | solution.py:500
  59.9 0.3 collective-permute-done.21
  60.3 0.1 collective-permute-start.24
  60.4 1.5 %collective-permute-done.24.got = f32[2,256,128]{2,1,0:T(8,128)S(1)} collective-permute-done((f32[2,256,128]{2,1,0:T(8,128)S(1)}, f32[2,256,128]{2,1,0:T(8,128)S(1)}, u32[]{:S(2)}, u32[]{:S(2)}) %collective-permute-start.24) | collective-permute-done | bytes 262176 | tf_op jit(solution)/shard_map/ppermute | solution.py:500
  61.9 1.0 %shard_map.82 = (f32[2,128,256]{2,1,0:T(8,128)}, f32[2,256,256]{2,1,0:T(8,128)}) custom-call(f32[2,128,256]{2,1,0:T(8,128)S(1)} %copy-done.1, f32[128,256]{1,0:T(8,128)S(1)} %shard_map.78.light, f32[4,128,128]{2,1,0:T(8,128)S(1)} %get-tuple-element.47.center, f32[4,128,128]{2,1,0:T(8,128)S(1)} %get-tuple-element.68.close, ...), custom_call_target="tpu_custom_call" | custom-call | flops 1000000 | bytes 3000000 | tf_op jit(solution)/shard_map/pallas_call | solution.py:431
  (34 shorter events, 0.3 us)
Async XLA Ops:
  0.6 4.1 %copy-start.1 = (f32[2,128,256]{2,1,0:T(8,128)S(1)}, f32[2,128,256]{2,1,0:T(8,128)}, u32[]{:S(2)}) copy-start(f32[2,128,256]{2,1,0:T(8,128)} %specimen.1) | copy-start | bytes 786436
  1.7 6.5 %collective-permute-start.1 = (f32[2,128,128]{2,1,0:T(8,128)S(1)}, f32[2,128,128]{2,1,0:T(8,128)S(1)}, u32[]{:S(2)}, u32[]{:S(2)}) collective-permute-start(f32[2,128,128]{2,1,0:T(8,128)S(1)} %get-tuple-element.71), channel_id=1, source_target_pairs={{0,1},{1,0},{2,3},{3,2},{4,5},{5,4},{6,7},{7,6},{8,9},{9,8},{10,11... | collective-permute-start | bytes 393224 | tf_op jit(solution)/shard_map/ppermute | solution.py:524
  4.7 6.5 %collective-permute-start.2 = (f32[2,128,256]{2,1,0:T(8,128)S(1)}, f32[2,128,256]{2,1,0:T(8,128)}, u32[]{:S(2)}, u32[]{:S(2)}) collective-permute-start(f32[2,128,256]{2,1,0:T(8,128)S(1)} %copy-done.1), channel_id=1, source_target_pairs={{8,24},{16,0},{24,16},{0,8},{9,25},{17,1},{25,17},{1,9},{10,26},{1... | collective-permute-start | bytes 786440 | tf_op jit(solution)/shard_map/ppermute | solution.py:528
  4.7 6.0 %collective-permute-start = (f32[2,128,128]{2,1,0:T(8,128)S(1)}, f32[2,128,128]{2,1,0:T(8,128)S(1)}, u32[]{:S(2)}, u32[]{:S(2)}) collective-permute-start(f32[2,128,128]{2,1,0:T(8,128)S(1)} %get-tuple-element.72), channel_id=1, source_target_pairs={{1,2},{3,4},{5,6},{2,1},{4,3},{6,5},{9,10},{11,12},{13,14},{10,9},... | collective-permute-start | bytes 393224 | tf_op jit(solution)/shard_map/ppermute | solution.py:525
  8.2 5.7 %copy-start = (f32[2,256,256]{2,1,0:T(8,128)S(1)}, f32[2,256,256]{2,1,0:T(8,128)}, u32[]{:S(2)}) copy-start(f32[2,256,256]{2,1,0:T(8,128)} %probe.4) | copy-start | bytes 1572868
  8.2 5.0 %collective-permute-start.3 = (f32[2,128,128]{2,1,0:T(8,128)S(1)}, f32[2,128,128]{2,1,0:T(8,128)S(1)}, u32[]{:S(2)}, u32[]{:S(2)}) collective-permute-start(f32[2,128,128]{2,1,0:T(8,128)S(1)} %collective-permute-done.1.pair_rim), channel_id=1, source_target_pairs={{8,24},{16,0},{24,16},{0,8},{9,25},{17,1},{25,17},{1,9},{10,26},{1... | collective-permute-start | bytes 393224 | tf_op jit(solution)/shard_map/ppermute | solution.py:528
  8.2 10.0 %collective-permute-start.5 = (f32[2,128,256]{2,1,0:T(8,128)S(1)}, f32[2,128,256]{2,1,0:T(8,128)S(1)}, u32[]{:S(2)}, u32[]{:S(2)}) collective-permute-start(f32[2,128,256]{2,1,0:T(8,128)S(1)} %copy-done.1), channel_id=1, source_target_pairs={{0,8},{8,0},{16,24},{24,16},{1,9},{9,1},{17,25},{25,17},{2,10},{10... | collective-permute-start | bytes 786440 | tf_op jit(solution)/shard_map/ppermute | solution.py:500
  8.6 4.6 %copy-start.3 = (s32[4,8,2,2]{1,3,2,0:T(2,128)S(1)}, s32[4,8,2,2]{1,3,2,0:T(2,128)}, u32[]{:S(2)}) copy-start(s32[4,8,2,2]{1,3,2,0:T(2,128)} %param.8) | copy-start | bytes 1540
  13.2 0.8 %copy-start.2 = (s32[4,8]{1,0:T(4,128)S(1)}, s32[4,8]{1,0:T(4,128)}, u32[]{:S(2)}) copy-start(s32[4,8]{1,0:T(4,128)} %counts.3) | copy-start | bytes 388
  13.2 5.1 %collective-permute-start.4 = (f32[2,128,128]{2,1,0:T(8,128)S(1)}, f32[2,128,128]{2,1,0:T(8,128)}, u32[]{:S(2)}, u32[]{:S(2)}) collective-permute-start(f32[2,128,128]{2,1,0:T(8,128)S(1)} %collective-permute-done.other_rim), channel_id=1, source_target_pairs={{8,24},{16,0},{24,16},{0,8},{9,25},{17,1},{25,17},{1,9},{10,26},{1... | collective-permute-start | bytes 393224 | tf_op jit(solution)/shard_map/ppermute | solution.py:531
  13.2 6.5 %collective-permute-start.8 = (f32[2,128,256]{2,1,0:T(8,128)}, f32[2,128,256]{2,1,0:T(8,128)S(1)}, u32[]{:S(2)}, u32[]{:S(2)}) collective-permute-start(f32[2,128,256]{2,1,0:T(8,128)} %collective-permute-done.2), channel_id=1, source_target_pairs={{0,8},{8,0},{16,24},{24,16},{1,9},{9,1},{17,25},{25,17},{2,10},{10... | collective-permute-start | bytes 786440 | tf_op jit(solution)/shard_map/ppermute | solution.py:500
  13.3 5.4 %collective-permute-start.6 = (f32[2,128,128]{2,1,0:T(8,128)S(1)}, f32[2,128,128]{2,1,0:T(8,128)S(1)}, u32[]{:S(2)}, u32[]{:S(2)}) collective-permute-start(f32[2,128,128]{2,1,0:T(8,128)S(1)} %collective-permute-done.1.pair_rim), channel_id=1, source_target_pairs={{0,8},{8,0},{16,24},{24,16},{1,9},{9,1},{17,25},{25,17},{2,10},{10... | collective-permute-start | bytes 393224 | tf_op jit(solution)/shard_map/ppermute | solution.py:500
  13.9 4.9 %collective-permute-start.7 = (f32[2,128,128]{2,1,0:T(8,128)S(1)}, f32[2,128,128]{2,1,0:T(8,128)S(1)}, u32[]{:S(2)}, u32[]{:S(2)}) collective-permute-start(f32[2,128,128]{2,1,0:T(8,128)S(1)} %collective-permute-done.other_rim), channel_id=1, source_target_pairs={{0,8},{8,0},{16,24},{24,16},{1,9},{9,1},{17,25},{25,17},{2,10},{10... | collective-permute-start | bytes 393224 | tf_op jit(solution)/shard_map/ppermute | solution.py:500
  18.3 1.5 %collective-permute-start.9 = (f32[2,128,128]{2,1,0:T(8,128)S(1)}, f32[2,128,128]{2,1,0:T(8,128)S(1)}, u32[]{:S(2)}, u32[]{:S(2)}) collective-permute-start(f32[2,128,128]{2,1,0:T(8,128)S(1)} %collective-permute-done.3), channel_id=1, source_target_pairs={{0,8},{8,0},{16,24},{24,16},{1,9},{9,1},{17,25},{25,17},{2,10},{10... | collective-permute-start | bytes 393224 | tf_op jit(solution)/shard_map/ppermute | solution.py:500
  18.3 1.7 %collective-permute-start.10 = (f32[2,128,128]{2,1,0:T(8,128)}, f32[2,128,128]{2,1,0:T(8,128)S(1)}, u32[]{:S(2)}, u32[]{:S(2)}) collective-permute-start(f32[2,128,128]{2,1,0:T(8,128)} %collective-permute-done.4), channel_id=1, source_target_pairs={{0,8},{8,0},{16,24},{24,16},{1,9},{9,1},{17,25},{25,17},{2,10},{10... | collective-permute-start | bytes 393224 | tf_op jit(solution)/shard_map/ppermute | solution.py:500
  24.3 2.2 %collective-permute-start.11 = (f32[776,128]{1,0:T(8,128)S(1)}, f32[776,128]{1,0:T(8,128)S(1)}, u32[]{:S(2)}, u32[]{:S(2)}) collective-permute-start(f32[776,128]{1,0:T(8,128)S(1)} %get-tuple-element.48), channel_id=1, source_target_pairs={{0,8},{8,0},{16,24},{24,16},{1,9},{9,1},{17,25},{25,17},{2,10},{10... | collective-permute-start | bytes 1191944 | tf_op jit(solution)/shard_map/ppermute | solution.py:500
  26.5 3.9 %collective-permute-start.12 = (f32[16,128,128]{2,1,0:T(8,128)S(1)}, f32[16,128,128]{2,1,0:T(8,128)S(1)}, u32[]{:S(2)}, u32[]{:S(2)}) collective-permute-start(f32[16,128,128]{2,1,0:T(8,128)S(1)} %get-tuple-element.50), channel_id=1, source_target_pairs={{0,8},{8,0},{16,24},{24,16},{1,9},{9,1},{17,25},{25,17},{2,10},{10... | collective-permute-start | bytes 3145736 | tf_op jit(solution)/shard_map/ppermute | solution.py:500
  26.8 6.7 %collective-permute-start.14 = (f32[200,128]{1,0:T(8,128)S(1)}, f32[200,128]{1,0:T(8,128)S(1)}, u32[]{:S(2)}, u32[]{:S(2)}) collective-permute-start(f32[200,128]{1,0:T(8,128)S(1)} %get-tuple-element.55), channel_id=1, source_target_pairs={{0,1},{1,0},{2,3},{3,2},{4,5},{5,4},{6,7},{7,6},{8,9},{9,8},{10,11... | collective-permute-start | bytes 307208 | tf_op jit(solution)/shard_map/ppermute | solution.py:500
  28.6 6.6 %collective-permute-start.15 = (f32[200,128]{1,0:T(8,128)S(1)}, f32[200,128]{1,0:T(8,128)S(1)}, u32[]{:S(2)}, u32[]{:S(2)}) collective-permute-start(f32[200,128]{1,0:T(8,128)S(1)} %get-tuple-element.56), channel_id=1, source_target_pairs={{0,17},{1,16},{2,19},{3,18},{4,21},{5,20},{6,23},{7,22},{8,25},{9,... | collective-permute-start | bytes 307208 | tf_op jit(solution)/shard_map/ppermute | solution.py:547
  28.8 7.5 %collective-permute-start.13 = (f32[200,128]{1,0:T(8,128)S(1)}, f32[200,128]{1,0:T(8,128)S(1)}, u32[]{:S(2)}, u32[]{:S(2)}) collective-permute-start(f32[200,128]{1,0:T(8,128)S(1)} %get-tuple-element.54), channel_id=1, source_target_pairs={{0,16},{8,24},{16,0},{24,8},{1,17},{9,25},{17,1},{25,9},{2,18},{10... | collective-permute-start | bytes 307208 | tf_op jit(solution)/shard_map/ppermute | solution.py:500
  30.4 6.1 %collective-permute-start.16 = (f32[4,128,128]{2,1,0:T(8,128)S(1)}, f32[4,128,128]{2,1,0:T(8,128)S(1)}, u32[]{:S(2)}, u32[]{:S(2)}) collective-permute-start(f32[4,128,128]{2,1,0:T(8,128)S(1)} %slice.63), channel_id=1, source_target_pairs={{24,8},{0,16},{16,24},{8,0},{25,9},{1,17},{17,25},{9,1},{26,10},{2... | collective-permute-start | bytes 786440 | tf_op jit(solution)/shard_map/ppermute | solution.py:555
  36.4 5.6 %collective-permute-start.17 = (f32[264,128]{1,0:T(8,128)S(1)}, f32[264,128]{1,0:T(8,128)S(1)}, u32[]{:S(2)}, u32[]{:S(2)}) collective-permute-start(f32[264,128]{1,0:T(8,128)S(1)} %concatenate.24), channel_id=1, source_target_pairs={{0,2},{1,3},{2,0},{3,1},{4,6},{5,7},{6,4},{7,5},{8,10},{9,11},{10,... | collective-permute-start | bytes 405512 | tf_op jit(solution)/shard_map/ppermute | solution.py:500
  38.6 6.4 %collective-permute-start.18 = (f32[4,128,128]{2,1,0:T(8,128)S(1)}, f32[4,128,128]{2,1,0:T(8,128)S(1)}, u32[]{:S(2)}, u32[]{:S(2)}) collective-permute-start(f32[4,128,128]{2,1,0:T(8,128)S(1)} %get-tuple-element.67), channel_id=1, source_target_pairs={{24,8},{0,16},{16,24},{8,0},{25,9},{1,17},{17,25},{9,1},{26,10},{2... | collective-permute-start | bytes 786440 | tf_op jit(solution)/shard_map/ppermute | solution.py:556
  41.1 11.4 %collective-permute-start.20 = (f32[2,128,128]{2,1,0:T(8,128)S(1)}, f32[2,128,128]{2,1,0:T(8,128)S(1)}, u32[]{:S(2)}, u32[]{:S(2)}) collective-permute-start(f32[2,128,128]{2,1,0:T(8,128)S(1)} %get-tuple-element.70), channel_id=1, source_target_pairs={{1,2},{3,4},{5,6},{2,1},{4,3},{6,5},{9,10},{11,12},{13,14},{10,9},... | collective-permute-start | bytes 393224 | tf_op jit(solution)/shard_map/ppermute | solution.py:563
  45.0 7.5 %collective-permute-start.19 = (f32[200,128]{1,0:T(8,128)S(1)}, f32[200,128]{1,0:T(8,128)S(1)}, u32[]{:S(2)}, u32[]{:S(2)}) collective-permute-start(f32[200,128]{1,0:T(8,128)S(1)} %slice_add_fusion.1), channel_id=1, source_target_pairs={{0,6},{1,7},{2,4},{3,5},{4,2},{5,3},{6,0},{7,1},{8,14},{9,15},{10,... | collective-permute-start | bytes 307208 | tf_op jit(solution)/shard_map/ppermute | solution.py:500
  52.6 7.6 %collective-permute-start.21 = (f32[384,128]{1,0:T(8,128)S(1)}, f32[384,128]{1,0:T(8,128)S(1)}, u32[]{:S(2)}, u32[]{:S(2)}) collective-permute-start(f32[384,128]{1,0:T(8,128)S(1)} %pad_maximum_fusion), channel_id=1, source_target_pairs={{0,1},{1,0},{2,3},{3,2},{4,5},{5,4},{6,7},{7,6},{8,9},{9,8},{10,11... | collective-permute-start | bytes 589832 | tf_op jit(solution)/shard_map/ppermute | solution.py:500
  53.3 5.3 %collective-permute-start.23 = (f32[2,64,128]{2,1,0:T(8,128)S(1)}, f32[2,64,128]{2,1,0:T(8,128)S(1)}, u32[]{:S(2)}, u32[]{:S(2)}) collective-permute-start(f32[2,64,128]{2,1,0:T(8,128)S(1)} %fusion.1), channel_id=1, source_target_pairs={{0,17},{1,16},{2,19},{3,18},{4,21},{5,20},{6,23},{7,22},{8,25},{9,... | collective-permute-start | bytes 196616 | tf_op jit(solution)/shard_map/ppermute | solution.py:547
  55.6 4.3 %collective-permute-start.22 = (f32[2,64,128]{2,1,0:T(8,128)S(1)}, f32[2,64,128]{2,1,0:T(8,128)S(1)}, u32[]{:S(2)}, u32[]{:S(2)}) collective-permute-start(f32[2,64,128]{2,1,0:T(8,128)S(1)} %fusion.1), channel_id=1, source_target_pairs={{0,16},{8,24},{16,0},{24,8},{1,17},{9,25},{17,1},{25,9},{2,18},{10... | collective-permute-start | bytes 196616 | tf_op jit(solution)/shard_map/ppermute | solution.py:500
  60.3 1.6 %collective-permute-start.24 = (f32[2,256,128]{2,1,0:T(8,128)S(1)}, f32[2,256,128]{2,1,0:T(8,128)S(1)}, u32[]{:S(2)}, u32[]{:S(2)}) collective-permute-start(f32[2,256,128]{2,1,0:T(8,128)S(1)} %maximum_select_fusion.fresh), channel_id=1, source_target_pairs={{0,8},{8,0},{16,24},{24,16},{1,9},{9,1},{17,25},{25,17},{2,10},{10... | collective-permute-start | bytes 786440 | tf_op jit(solution)/shard_map/ppermute | solution.py:500

commit v6 on v5

--- a/solution.py
+++ b/solution.py
@@ -410,11 +410,13 @@
     col_odd = lax.rem(col_place, 2)
     far_at = row_place + 2 * row_odd - 1
     inside = (far_at >= 0) & (far_at < lax.axis_size("row"))
+    other_at = col_place + 2 * col_odd - 1
+    beside = (other_at >= 0) & (other_at < lax.axis_size("col"))
     for part in range(2):
-        pair = both[part]
+        pair, apart = both[part], jnp.where(beside, other[part], 0.0)
         rims = (
-            jnp.where(col_odd == 0, other[part], pair),
-            jnp.where(col_odd == 0, pair, other[part]),
+            jnp.where(col_odd == 0, apart, pair),
+            jnp.where(col_odd == 0, pair, apart),
         )
         for side, rim in enumerate(rims):
             at = slice(side * half, (side + 1) * half)
@@ -560,15 +562,15 @@
     inside = (row_place + 2 * row_odd - 1 >= 0) & (row_place + 2 * row_odd - 1 < rows)
     rim = center_rim + packet[8:12] + pick(inside, beyond_rim, 0.0)
     pair_part = rim[:2]
-    other_part = lax.ppermute(rim[2:], "col", others)
-    filled = jnp.concatenate([value, jnp.zeros((64, LANES), jnp.float32)])
-    value = value + exchange(filled, "col", cols, 2)[: value.shape[0]]
-    value, beyond_mid = tie((value, beyond_mid))
+    other_part = lax.ppermute(rim[2:], "col", others + [(0, cols - 1), (cols - 1, 0)])
+    value = value + exchange(value, "col", cols, 2)
     for bit in (1 << k for k in range(2, cols.bit_length() - 1)):
         value = value + exchange(value, "col", cols, 2 * bit - 2)
     for bit in (1 << k for k in range(2, rows.bit_length() - 1)):
         value = value + exchange(value, "row", rows, bit)
-    value, other_part, pair_part = tie((value, other_part, pair_part))
+    value, other_part, pair_part, beyond_mid = tie(
+        (value, other_part, pair_part, beyond_mid)
+    )
     size = own_probe.shape[1]
     real, imag, weight, total = (value[k * size : (k + 1) * size] for k in range(4))
     update = jnp.stack([real, imag]) / (weight + probe_damping * (total[:1] / (width * width)))

time: 63.1 us -> 61 us (0.967)
  waiting for transfers between devices: 28 us -> 24.1 us
  starting transfers between devices: 21.2 us -> 22.7 us
    ppermute x1, waiting for transfers between devices: 2.93 us -> 0.01 us  [shards(): beyond_mid = lax.ppermute(packet[4:8], 'row', onward_pairs)]
    ppermute x1, starting transfers between devices: 0.67 us -> 3.48 us  [shards(): lax.ppermute(rim[2:], 'col', others + [(0, cols - 1), (cols - 1, 0)])]
    ppermute x15, starting transfers between devices: 11.4 us -> 10.2 us  [exchange(): return lax.ppermute(value, axis, [(i, i ^ bit) for i in range(count)])]
    ppermute x15, waiting for transfers between devices: 13.4 us -> 12.3 us  [exchange(): return lax.ppermute(value, axis, [(i, i ^ bit) for i in range(count)])]
  transfers between devices with their start and end apart: 25 -> 25, of which waited for: 17 -> 14; matrix products, arithmetic and copies ran while one was open for 1% -> 1% of each run, Pallas kernels for 10% -> 10%
where the time goes in v6:
time: 61 us; the launch traced here: 60.4 us
  waiting for transfers between devices  24.1 us (40%)
  starting transfers between devices  22.7 us (37%)
  Pallas kernels  11.4 us (19%)
  other arithmetic  1.25 us (2%)
  between operations  0.85 us (1%)
    ppermute x15, waiting for transfers between devices, exchange(): return lax.ppermute(value, axis, [(i, i ^ bit) for i in range(count)])  12.3 us
    ppermute x15, starting transfers between devices, exchange(): return lax.ppermute(value, axis, [(i, i ^ bit) for i in range(count)])  10.2 us
    pallas_call x1, Pallas kernels, exit_update(): pl.pallas_call(delta_kernel, out_shape=[jax.ShapeDtypeStruct((3 * width +...  4.29 us
    ppermute x2, waiting for transfers between devices, all_three(): diagonal = lax.ppermute(diagonal, ('row', 'col'), square)  3.97 us
    ppermute x1, starting transfers between devices, shards(): lax.ppermute(rim[2:], 'col', others + [(0, cols - 1), (cols - 1, 0)])  3.48 us
    ppermute x1, starting transfers between devices, shards(): pair_rim = lax.ppermute(jnp.where(col_odd == 0, high, low), 'col', pairs)  3.03 us
    ppermute x1, waiting for transfers between devices, shards(): pair_rim = lax.ppermute(jnp.where(col_odd == 0, high, low), 'col', pairs)  2.82 us
    ppermute x1, starting transfers between devices, shards(): beyond_mid = lax.ppermute(packet[4:8], 'row', onward_pairs)  2.43 us
  transfers between devices with their start and end apart: 25, of which 14 were waited for; matrix products, arithmetic and copies ran while one was open for 1% of the time, Pallas kernels for 10%

profile of v6, /device:TPU:0, one launch (start us, length us, event | category | flops | bytes accessed | tf_op | source)
XLA Modules:
  0.0 60.4 jit_solution(17954729278748790139)
XLA Ops:
  0.7 1.0 %slice_select_fusion = (f32[2,128,128]{2,1,0:T(8,128)S(1)}, f32[2,128,128]{2,1,0:T(8,128)S(1)}) fusion(f32[2,128,256]{2,1,0:T(8,128)} %specimen.1, pred[]{:T(512)S(6)} %eq.13), kind=kLoop, calls=%fused_computation.6 | loop fusion | flops 65536 | bytes 524289 | tf_op jit(solution)/shard_map/jit(_where)/select_n | solution.py:526
  1.7 3.0 %collective-permute-start.1 = (f32[2,128,128]{2,1,0:T(8,128)S(1)}, f32[2,128,128]{2,1,0:T(8,128)S(1)}, u32[]{:S(2)}, u32[]{:S(2)}) collective-permute-start(f32[2,128,128]{2,1,0:T(8,128)S(1)} %get-tuple-element.69), channel_id=1, source_target_pairs={{0,1},{1,0},{2,3},{3,2},{4,5},{5,4},{6,7},{7,6},{8,9},{9,8},{10,11... | collective-permute-start | bytes 393224 | tf_op jit(solution)/shard_map/ppermute | solution.py:526
  4.7 0.7 %collective-permute-start = (f32[2,128,128]{2,1,0:T(8,128)S(1)}, f32[2,128,128]{2,1,0:T(8,128)S(1)}, u32[]{:S(2)}, u32[]{:S(2)}) collective-permute-start(f32[2,128,128]{2,1,0:T(8,128)S(1)} %get-tuple-element.70), channel_id=1, source_target_pairs={{1,2},{3,4},{5,6},{2,1},{4,3},{6,5},{9,10},{11,12},{13,14},{10,9},... | collective-permute-start | bytes 393224 | tf_op jit(solution)/shard_map/ppermute | solution.py:527
  5.4 2.8 %collective-permute-done.1.pair_rim = f32[2,128,128]{2,1,0:T(8,128)S(1)} collective-permute-done((f32[2,128,128]{2,1,0:T(8,128)S(1)}, f32[2,128,128]{2,1,0:T(8,128)S(1)}, u32[]{:S(2)}, u32[]{:S(2)}) %collective-permute-start.1) | collective-permute-done | bytes 131104 | tf_op jit(solution)/shard_map/ppermute | solution.py:526
  8.2 0.4 collective-permute-start.5
  8.6 2.1 %shard_map.77 = (f32[2,256,256]{2,1,0:T(8,128)S(1)}, bf16[4,2,256,256]{3,2,1,0:T(8,128)(2,1)S(1)}) custom-call(f32[2,256,256]{2,1,0:T(8,128)} %bitcast.13, bf16[4,2,256,256]{3,2,1,0:T(8,128)(2,1)} %constant.54.clone.tables), custom_call_target="tpu_custom_call" | custom-call | flops 400000000 | bytes 3000000 | tf_op jit(solution)/shard_map/pallas_call | solution.py:354
  10.8 0.0 collective-permute-done.other_rim
  10.8 0.4 collective-permute-done.2
  11.2 2.0 %collective-permute-done.3 = f32[2,128,128]{2,1,0:T(8,128)S(1)} collective-permute-done((f32[2,128,128]{2,1,0:T(8,128)S(1)}, f32[2,128,128]{2,1,0:T(8,128)S(1)}, u32[]{:S(2)}, u32[]{:S(2)}) %collective-permute-start.3) | collective-permute-done | bytes 131104 | tf_op jit(solution)/shard_map/ppermute | solution.py:530
  13.2 0.0 collective-permute-start.4
  13.2 0.1 copy.8.offsets
  13.3 0.5 collective-permute-start.6
  13.9 0.1 collective-permute-start.7
  14.0 2.2 %shard_map.78.light = f32[128,256]{1,0:T(8,128)S(1)} custom-call(s32[4,8,2,2]{3,2,1,0:T(2,128)S(1)} %copy.8.offsets, s32[4,8]{1,0:T(4,128)S(1)} %copy-done.2, f32[2,256,256]{2,1,0:T(8,128)S(1)} %copy-done), custom_call_target="tpu_custom_call" | custom-call | flops 40000000 | bytes 8000000 | tf_op jit(solution)/shard_map/pallas_call | solution.py:145
  16.1 2.1 %collective-permute-done.4 = f32[2,128,128]{2,1,0:T(8,128)} collective-permute-done((f32[2,128,128]{2,1,0:T(8,128)S(1)}, f32[2,128,128]{2,1,0:T(8,128)}, u32[]{:S(2)}, u32[]{:S(2)}) %collective-permute-start.4) | collective-permute-done | bytes 131104 | tf_op jit(solution)/shard_map/ppermute | solution.py:533
  18.3 0.0 collective-permute-start.9
  18.3 0.0 collective-permute-done.5.near
  18.3 0.5 collective-permute-start.10
  18.8 0.0 collective-permute-done.6.near_pair
  18.8 0.9 %collective-permute-done.9.far_pair = f32[2,128,128]{2,1,0:T(8,128)S(1)} collective-permute-done((f32[2,128,128]{2,1,0:T(8,128)S(1)}, f32[2,128,128]{2,1,0:T(8,128)S(1)}, u32[]{:S(2)}, u32[]{:S(2)}) %collective-permute-start.9) | collective-permute-done | bytes 131104 | tf_op jit(solution)/shard_map/ppermute | solution.py:502
  19.7 0.3 collective-permute-done.10.far_other
  20.0 4.3 %shard_map.79 = (f32[776,128]{1,0:T(8,128)S(1)}, f32[776,128]{1,0:T(8,128)S(1)}, f32[2,64,128]{2,1,0:T(8,128)S(1)}, f32[2,2,256,256]{3,2,1,0:T(8,128)S(1)}) custom-call(s32[4,8,2,2]{3,2,1,0:T(2,128)S(1)} %copy.8.offsets, s32[4,8]{1,0:T(4,128)S(1)} %copy-done.2, f32[2,256,256]{2,1,0:T(8,128)S(1)} %copy-done, f32[2,256,256]{2,1,0:T(8,128)S(1)} %get-tuple-element.40.magnitudes, ...), custom_call_target="tpu_custom_call" | custom-call | flops 3200000000 | bytes 8000000 | tf_op jit(solution)/shard_map/pallas_call | solution.py:378
  24.3 0.4 collective-permute-start.11
  24.7 1.8 %shard_map.80 = (f32[4,128,128]{2,1,0:T(8,128)S(1)}, f32[4,128,128]{2,1,0:T(8,128)S(1)}, f32[16,128,128]{2,1,0:T(8,128)S(1)}) custom-call(s32[4,8,2,2]{3,2,1,0:T(2,128)S(1)} %copy.8.offsets, f32[2,256,256]{2,1,0:T(8,128)S(1)} %copy-done, f32[2,2,256,256]{3,2,1,0:T(8,128)S(1)} %get-tuple-element.45.delta), custom_call_target="tpu_custom_call" | custom-call | flops 4000000 | bytes 4000000 | tf_op jit(solution)/shard_map/pallas_call | solution.py:488
  26.5 0.3 collective-permute-start.12
  26.7 0.1 shard_map.81
  26.8 1.8 %collective-permute-start.14 = (f32[200,128]{1,0:T(8,128)S(1)}, f32[200,128]{1,0:T(8,128)S(1)}, u32[]{:S(2)}, u32[]{:S(2)}) collective-permute-start(f32[200,128]{1,0:T(8,128)S(1)} %get-tuple-element.54), channel_id=1, source_target_pairs={{0,1},{1,0},{2,3},{3,2},{4,5},{5,4},{6,7},{7,6},{8,9},{9,8},{10,11... | collective-permute-start | bytes 307208 | tf_op jit(solution)/shard_map/ppermute | solution.py:502
  28.6 0.4 collective-permute-start.15
  29.0 1.3 %collective-permute-start.13 = (f32[200,128]{1,0:T(8,128)S(1)}, f32[200,128]{1,0:T(8,128)S(1)}, u32[]{:S(2)}, u32[]{:S(2)}) collective-permute-start(f32[200,128]{1,0:T(8,128)S(1)} %get-tuple-element.53), channel_id=1, source_target_pairs={{0,16},{8,24},{16,0},{24,8},{1,17},{9,25},{17,1},{25,9},{2,18},{10... | collective-permute-start | bytes 307208 | tf_op jit(solution)/shard_map/ppermute | solution.py:502
  30.4 0.7 %collective-permute-start.16 = (f32[4,128,128]{2,1,0:T(8,128)S(1)}, f32[4,128,128]{2,1,0:T(8,128)S(1)}, u32[]{:S(2)}, u32[]{:S(2)}) collective-permute-start(f32[4,128,128]{2,1,0:T(8,128)S(1)} %slice.59), channel_id=1, source_target_pairs={{24,8},{0,16},{16,24},{8,0},{25,9},{1,17},{17,25},{9,1},{26,10},{2... | collective-permute-start | bytes 786440 | tf_op jit(solution)/shard_map/ppermute | solution.py:557
  31.1 2.4 %collective-permute-done.14 = f32[200,128]{1,0:T(8,128)S(1)} collective-permute-done((f32[200,128]{1,0:T(8,128)S(1)}, f32[200,128]{1,0:T(8,128)S(1)}, u32[]{:S(2)}, u32[]{:S(2)}) %collective-permute-start.14) | collective-permute-done | bytes 102432 | tf_op jit(solution)/shard_map/ppermute | solution.py:502
  33.5 1.8 %collective-permute-done.15 = f32[200,128]{1,0:T(8,128)S(1)} collective-permute-done((f32[200,128]{1,0:T(8,128)S(1)}, f32[200,128]{1,0:T(8,128)S(1)}, u32[]{:S(2)}, u32[]{:S(2)}) %collective-permute-start.15) | collective-permute-done | bytes 102432 | tf_op jit(solution)/shard_map/ppermute | solution.py:549
  35.2 1.0 %collective-permute-done.13 = f32[200,128]{1,0:T(8,128)S(1)} collective-permute-done((f32[200,128]{1,0:T(8,128)S(1)}, f32[200,128]{1,0:T(8,128)S(1)}, u32[]{:S(2)}, u32[]{:S(2)}) %collective-permute-start.13) | collective-permute-done | bytes 102432 | tf_op jit(solution)/shard_map/ppermute | solution.py:502
  36.3 0.4 collective-permute-done.16
  36.7 1.8 %collective-permute-start.17 = (f32[200,128]{1,0:T(8,128)S(1)}, f32[200,128]{1,0:T(8,128)S(1)}, u32[]{:S(2)}, u32[]{:S(2)}) collective-permute-start(f32[200,128]{1,0:T(8,128)S(1)} %add_add_fusion), channel_id=1, source_target_pairs={{0,2},{1,3},{2,0},{3,1},{4,6},{5,7},{6,4},{7,5},{8,10},{9,11},{10,... | collective-permute-start | bytes 307208 | tf_op jit(solution)/shard_map/ppermute | solution.py:502
  38.5 0.1 fusion.2
  38.6 2.4 %collective-permute-start.20 = (f32[4,128,128]{2,1,0:T(8,128)S(1)}, f32[4,128,128]{2,1,0:T(8,128)S(1)}, u32[]{:S(2)}, u32[]{:S(2)}) collective-permute-start(f32[4,128,128]{2,1,0:T(8,128)S(1)} %get-tuple-element.64), channel_id=1, source_target_pairs={{24,8},{0,16},{16,24},{8,0},{25,9},{1,17},{17,25},{9,1},{26,10},{2... | collective-permute-start | bytes 786440 | tf_op jit(solution)/shard_map/ppermute | solution.py:558
  41.0 3.5 %collective-permute-start.19 = (f32[2,128,128]{2,1,0:T(8,128)S(1)}, f32[2,128,128]{2,1,0:T(8,128)S(1)}, u32[]{:S(2)}, u32[]{:S(2)}) collective-permute-start(f32[2,128,128]{2,1,0:T(8,128)S(1)} %get-tuple-element.68), channel_id=1, source_target_pairs={{1,2},{3,4},{5,6},{2,1},{4,3},{6,5},{0,7},{7,0},{9,10},{11,12},{13... | collective-permute-start | bytes 393224 | tf_op jit(solution)/shard_map/ppermute | solution.py:565
  44.5 1.2 %collective-permute-start.18 = (f32[200,128]{1,0:T(8,128)S(1)}, f32[200,128]{1,0:T(8,128)S(1)}, u32[]{:S(2)}, u32[]{:S(2)}) collective-permute-start(f32[200,128]{1,0:T(8,128)S(1)} %add.54), channel_id=1, source_target_pairs={{0,6},{1,7},{2,4},{3,5},{4,2},{5,3},{6,0},{7,1},{8,14},{9,15},{10,... | collective-permute-start | bytes 307208 | tf_op jit(solution)/shard_map/ppermute | solution.py:502
  45.7 5.4 %collective-permute-done.18 = f32[200,128]{1,0:T(8,128)S(1)} collective-permute-done((f32[200,128]{1,0:T(8,128)S(1)}, f32[200,128]{1,0:T(8,128)S(1)}, u32[]{:S(2)}, u32[]{:S(2)}) %collective-permute-start.18) | collective-permute-done | bytes 102432 | tf_op jit(solution)/shard_map/ppermute | solution.py:502
  51.3 0.5 collective-permute-start.21
  51.7 1.7 %collective-permute-start.23 = (f32[2,64,128]{2,1,0:T(8,128)S(1)}, f32[2,64,128]{2,1,0:T(8,128)S(1)}, u32[]{:S(2)}, u32[]{:S(2)}) collective-permute-start(f32[2,64,128]{2,1,0:T(8,128)S(1)} %fusion.1), channel_id=1, source_target_pairs={{0,17},{1,16},{2,19},{3,18},{4,21},{5,20},{6,23},{7,22},{8,25},{9,... | collective-permute-start | bytes 196616 | tf_op jit(solution)/shard_map/ppermute | solution.py:549
  53.5 1.4 %collective-permute-start.22 = (f32[2,64,128]{2,1,0:T(8,128)S(1)}, f32[2,64,128]{2,1,0:T(8,128)S(1)}, u32[]{:S(2)}, u32[]{:S(2)}) collective-permute-start(f32[2,64,128]{2,1,0:T(8,128)S(1)} %fusion.1), channel_id=1, source_target_pairs={{0,16},{8,24},{16,0},{24,8},{1,17},{9,25},{17,1},{25,9},{2,18},{10... | collective-permute-start | bytes 196616 | tf_op jit(solution)/shard_map/ppermute | solution.py:502
  54.8 2.2 %collective-permute-done.23 = f32[2,64,128]{2,1,0:T(8,128)S(1)} collective-permute-done((f32[2,64,128]{2,1,0:T(8,128)S(1)}, f32[2,64,128]{2,1,0:T(8,128)S(1)}, u32[]{:S(2)}, u32[]{:S(2)}) %collective-permute-start.23) | collective-permute-done | bytes 65568 | tf_op jit(solution)/shard_map/ppermute | solution.py:549
  57.0 0.7 %collective-permute-done.22 = f32[2,64,128]{2,1,0:T(8,128)S(1)} collective-permute-done((f32[2,64,128]{2,1,0:T(8,128)S(1)}, f32[2,64,128]{2,1,0:T(8,128)S(1)}, u32[]{:S(2)}, u32[]{:S(2)}) %collective-permute-start.22) | collective-permute-done | bytes 65568 | tf_op jit(solution)/shard_map/ppermute | solution.py:502
  57.9 0.1 collective-permute-start.24
  57.9 1.5 %collective-permute-done.24.got = f32[2,256,128]{2,1,0:T(8,128)S(1)} collective-permute-done((f32[2,256,128]{2,1,0:T(8,128)S(1)}, f32[2,256,128]{2,1,0:T(8,128)S(1)}, u32[]{:S(2)}, u32[]{:S(2)}) %collective-permute-start.24) | collective-permute-done | bytes 262176 | tf_op jit(solution)/shard_map/ppermute | solution.py:502
  59.5 1.0 %shard_map.82 = (f32[2,128,256]{2,1,0:T(8,128)}, f32[2,256,256]{2,1,0:T(8,128)}) custom-call(f32[2,128,256]{2,1,0:T(8,128)S(1)} %copy-done.1, f32[128,256]{1,0:T(8,128)S(1)} %shard_map.78.light, f32[4,128,128]{2,1,0:T(8,128)S(1)} %get-tuple-element.46.center, f32[4,128,128]{2,1,0:T(8,128)S(1)} %get-tuple-element.66.close, ...), custom_call_target="tpu_custom_call" | custom-call | flops 1000000 | bytes 3000000 | tf_op jit(solution)/shard_map/pallas_call | solution.py:433
  (33 shorter events, 0.2 us)
Async XLA Ops:
  0.6 4.1 %copy-start.1 = (f32[2,128,256]{2,1,0:T(8,128)S(1)}, f32[2,128,256]{2,1,0:T(8,128)}, u32[]{:S(2)}) copy-start(f32[2,128,256]{2,1,0:T(8,128)} %specimen.1) | copy-start | bytes 786436
  1.7 6.5 %collective-permute-start.1 = (f32[2,128,128]{2,1,0:T(8,128)S(1)}, f32[2,128,128]{2,1,0:T(8,128)S(1)}, u32[]{:S(2)}, u32[]{:S(2)}) collective-permute-start(f32[2,128,128]{2,1,0:T(8,128)S(1)} %get-tuple-element.69), channel_id=1, source_target_pairs={{0,1},{1,0},{2,3},{3,2},{4,5},{5,4},{6,7},{7,6},{8,9},{9,8},{10,11... | collective-permute-start | bytes 393224 | tf_op jit(solution)/shard_map/ppermute | solution.py:526
  4.7 6.5 %collective-permute-start.2 = (f32[2,128,256]{2,1,0:T(8,128)S(1)}, f32[2,128,256]{2,1,0:T(8,128)}, u32[]{:S(2)}, u32[]{:S(2)}) collective-permute-start(f32[2,128,256]{2,1,0:T(8,128)S(1)} %copy-done.1), channel_id=1, source_target_pairs={{8,24},{16,0},{24,16},{0,8},{9,25},{17,1},{25,17},{1,9},{10,26},{1... | collective-permute-start | bytes 786440 | tf_op jit(solution)/shard_map/ppermute | solution.py:530
  4.7 6.0 %collective-permute-start = (f32[2,128,128]{2,1,0:T(8,128)S(1)}, f32[2,128,128]{2,1,0:T(8,128)S(1)}, u32[]{:S(2)}, u32[]{:S(2)}) collective-permute-start(f32[2,128,128]{2,1,0:T(8,128)S(1)} %get-tuple-element.70), channel_id=1, source_target_pairs={{1,2},{3,4},{5,6},{2,1},{4,3},{6,5},{9,10},{11,12},{13,14},{10,9},... | collective-permute-start | bytes 393224 | tf_op jit(solution)/shard_map/ppermute | solution.py:527
  8.2 5.7 %copy-start = (f32[2,256,256]{2,1,0:T(8,128)S(1)}, f32[2,256,256]{2,1,0:T(8,128)}, u32[]{:S(2)}) copy-start(f32[2,256,256]{2,1,0:T(8,128)} %probe.4) | copy-start | bytes 1572868
  8.2 5.0 %collective-permute-start.3 = (f32[2,128,128]{2,1,0:T(8,128)S(1)}, f32[2,128,128]{2,1,0:T(8,128)S(1)}, u32[]{:S(2)}, u32[]{:S(2)}) collective-permute-start(f32[2,128,128]{2,1,0:T(8,128)S(1)} %collective-permute-done.1.pair_rim), channel_id=1, source_target_pairs={{8,24},{16,0},{24,16},{0,8},{9,25},{17,1},{25,17},{1,9},{10,26},{1... | collective-permute-start | bytes 393224 | tf_op jit(solution)/shard_map/ppermute | solution.py:530
  8.2 10.0 %collective-permute-start.5 = (f32[2,128,256]{2,1,0:T(8,128)S(1)}, f32[2,128,256]{2,1,0:T(8,128)S(1)}, u32[]{:S(2)}, u32[]{:S(2)}) collective-permute-start(f32[2,128,256]{2,1,0:T(8,128)S(1)} %copy-done.1), channel_id=1, source_target_pairs={{0,8},{8,0},{16,24},{24,16},{1,9},{9,1},{17,25},{25,17},{2,10},{10... | collective-permute-start | bytes 786440 | tf_op jit(solution)/shard_map/ppermute | solution.py:502
  8.6 4.6 %copy-start.3 = (s32[4,8,2,2]{1,3,2,0:T(2,128)S(1)}, s32[4,8,2,2]{1,3,2,0:T(2,128)}, u32[]{:S(2)}) copy-start(s32[4,8,2,2]{1,3,2,0:T(2,128)} %param.8) | copy-start | bytes 1540
  13.2 0.8 %copy-start.2 = (s32[4,8]{1,0:T(4,128)S(1)}, s32[4,8]{1,0:T(4,128)}, u32[]{:S(2)}) copy-start(s32[4,8]{1,0:T(4,128)} %counts.3) | copy-start | bytes 388
  13.2 5.1 %collective-permute-start.4 = (f32[2,128,128]{2,1,0:T(8,128)S(1)}, f32[2,128,128]{2,1,0:T(8,128)}, u32[]{:S(2)}, u32[]{:S(2)}) collective-permute-start(f32[2,128,128]{2,1,0:T(8,128)S(1)} %collective-permute-done.other_rim), channel_id=1, source_target_pairs={{8,24},{16,0},{24,16},{0,8},{9,25},{17,1},{25,17},{1,9},{10,26},{1... | collective-permute-start | bytes 393224 | tf_op jit(solution)/shard_map/ppermute | solution.py:533
  13.2 6.5 %collective-permute-start.8 = (f32[2,128,256]{2,1,0:T(8,128)}, f32[2,128,256]{2,1,0:T(8,128)S(1)}, u32[]{:S(2)}, u32[]{:S(2)}) collective-permute-start(f32[2,128,256]{2,1,0:T(8,128)} %collective-permute-done.2), channel_id=1, source_target_pairs={{0,8},{8,0},{16,24},{24,16},{1,9},{9,1},{17,25},{25,17},{2,10},{10... | collective-permute-start | bytes 786440 | tf_op jit(solution)/shard_map/ppermute | solution.py:502
  13.3 5.4 %collective-permute-start.6 = (f32[2,128,128]{2,1,0:T(8,128)S(1)}, f32[2,128,128]{2,1,0:T(8,128)S(1)}, u32[]{:S(2)}, u32[]{:S(2)}) collective-permute-start(f32[2,128,128]{2,1,0:T(8,128)S(1)} %collective-permute-done.1.pair_rim), channel_id=1, source_target_pairs={{0,8},{8,0},{16,24},{24,16},{1,9},{9,1},{17,25},{25,17},{2,10},{10... | collective-permute-start | bytes 393224 | tf_op jit(solution)/shard_map/ppermute | solution.py:502
  13.9 4.9 %collective-permute-start.7 = (f32[2,128,128]{2,1,0:T(8,128)S(1)}, f32[2,128,128]{2,1,0:T(8,128)S(1)}, u32[]{:S(2)}, u32[]{:S(2)}) collective-permute-start(f32[2,128,128]{2,1,0:T(8,128)S(1)} %collective-permute-done.other_rim), channel_id=1, source_target_pairs={{0,8},{8,0},{16,24},{24,16},{1,9},{9,1},{17,25},{25,17},{2,10},{10... | collective-permute-start | bytes 393224 | tf_op jit(solution)/shard_map/ppermute | solution.py:502
  18.3 1.5 %collective-permute-start.9 = (f32[2,128,128]{2,1,0:T(8,128)S(1)}, f32[2,128,128]{2,1,0:T(8,128)S(1)}, u32[]{:S(2)}, u32[]{:S(2)}) collective-permute-start(f32[2,128,128]{2,1,0:T(8,128)S(1)} %collective-permute-done.3), channel_id=1, source_target_pairs={{0,8},{8,0},{16,24},{24,16},{1,9},{9,1},{17,25},{25,17},{2,10},{10... | collective-permute-start | bytes 393224 | tf_op jit(solution)/shard_map/ppermute | solution.py:502
  18.3 1.7 %collective-permute-start.10 = (f32[2,128,128]{2,1,0:T(8,128)}, f32[2,128,128]{2,1,0:T(8,128)S(1)}, u32[]{:S(2)}, u32[]{:S(2)}) collective-permute-start(f32[2,128,128]{2,1,0:T(8,128)} %collective-permute-done.4), channel_id=1, source_target_pairs={{0,8},{8,0},{16,24},{24,16},{1,9},{9,1},{17,25},{25,17},{2,10},{10... | collective-permute-start | bytes 393224 | tf_op jit(solution)/shard_map/ppermute | solution.py:502
  24.3 2.2 %collective-permute-start.11 = (f32[776,128]{1,0:T(8,128)S(1)}, f32[776,128]{1,0:T(8,128)S(1)}, u32[]{:S(2)}, u32[]{:S(2)}) collective-permute-start(f32[776,128]{1,0:T(8,128)S(1)} %get-tuple-element.47), channel_id=1, source_target_pairs={{0,8},{8,0},{16,24},{24,16},{1,9},{9,1},{17,25},{25,17},{2,10},{10... | collective-permute-start | bytes 1191944 | tf_op jit(solution)/shard_map/ppermute | solution.py:502
  26.5 3.9 %collective-permute-start.12 = (f32[16,128,128]{2,1,0:T(8,128)S(1)}, f32[16,128,128]{2,1,0:T(8,128)S(1)}, u32[]{:S(2)}, u32[]{:S(2)}) collective-permute-start(f32[16,128,128]{2,1,0:T(8,128)S(1)} %get-tuple-element.49), channel_id=1, source_target_pairs={{0,8},{8,0},{16,24},{24,16},{1,9},{9,1},{17,25},{25,17},{2,10},{10... | collective-permute-start | bytes 3145736 | tf_op jit(solution)/shard_map/ppermute | solution.py:502
  26.8 6.7 %collective-permute-start.14 = (f32[200,128]{1,0:T(8,128)S(1)}, f32[200,128]{1,0:T(8,128)S(1)}, u32[]{:S(2)}, u32[]{:S(2)}) collective-permute-start(f32[200,128]{1,0:T(8,128)S(1)} %get-tuple-element.54), channel_id=1, source_target_pairs={{0,1},{1,0},{2,3},{3,2},{4,5},{5,4},{6,7},{7,6},{8,9},{9,8},{10,11... | collective-permute-start | bytes 307208 | tf_op jit(solution)/shard_map/ppermute | solution.py:502
  28.6 6.6 %collective-permute-start.15 = (f32[200,128]{1,0:T(8,128)S(1)}, f32[200,128]{1,0:T(8,128)S(1)}, u32[]{:S(2)}, u32[]{:S(2)}) collective-permute-start(f32[200,128]{1,0:T(8,128)S(1)} %get-tuple-element.55), channel_id=1, source_target_pairs={{0,17},{1,16},{2,19},{3,18},{4,21},{5,20},{6,23},{7,22},{8,25},{9,... | collective-permute-start | bytes 307208 | tf_op jit(solution)/shard_map/ppermute | solution.py:549
  29.0 7.3 %collective-permute-start.13 = (f32[200,128]{1,0:T(8,128)S(1)}, f32[200,128]{1,0:T(8,128)S(1)}, u32[]{:S(2)}, u32[]{:S(2)}) collective-permute-start(f32[200,128]{1,0:T(8,128)S(1)} %get-tuple-element.53), channel_id=1, source_target_pairs={{0,16},{8,24},{16,0},{24,8},{1,17},{9,25},{17,1},{25,9},{2,18},{10... | collective-permute-start | bytes 307208 | tf_op jit(solution)/shard_map/ppermute | solution.py:502
  30.4 6.3 %collective-permute-start.16 = (f32[4,128,128]{2,1,0:T(8,128)S(1)}, f32[4,128,128]{2,1,0:T(8,128)S(1)}, u32[]{:S(2)}, u32[]{:S(2)}) collective-permute-start(f32[4,128,128]{2,1,0:T(8,128)S(1)} %slice.59), channel_id=1, source_target_pairs={{24,8},{0,16},{16,24},{8,0},{25,9},{1,17},{17,25},{9,1},{26,10},{2... | collective-permute-start | bytes 786440 | tf_op jit(solution)/shard_map/ppermute | solution.py:557
  36.7 7.8 %collective-permute-start.17 = (f32[200,128]{1,0:T(8,128)S(1)}, f32[200,128]{1,0:T(8,128)S(1)}, u32[]{:S(2)}, u32[]{:S(2)}) collective-permute-start(f32[200,128]{1,0:T(8,128)S(1)} %add_add_fusion), channel_id=1, source_target_pairs={{0,2},{1,3},{2,0},{3,1},{4,6},{5,7},{6,4},{7,5},{8,10},{9,11},{10,... | collective-permute-start | bytes 307208 | tf_op jit(solution)/shard_map/ppermute | solution.py:502
  38.6 12.6 %collective-permute-start.20 = (f32[4,128,128]{2,1,0:T(8,128)S(1)}, f32[4,128,128]{2,1,0:T(8,128)S(1)}, u32[]{:S(2)}, u32[]{:S(2)}) collective-permute-start(f32[4,128,128]{2,1,0:T(8,128)S(1)} %get-tuple-element.64), channel_id=1, source_target_pairs={{24,8},{0,16},{16,24},{8,0},{25,9},{1,17},{17,25},{9,1},{26,10},{2... | collective-permute-start | bytes 786440 | tf_op jit(solution)/shard_map/ppermute | solution.py:558
  41.0 10.2 %collective-permute-start.19 = (f32[2,128,128]{2,1,0:T(8,128)S(1)}, f32[2,128,128]{2,1,0:T(8,128)S(1)}, u32[]{:S(2)}, u32[]{:S(2)}) collective-permute-start(f32[2,128,128]{2,1,0:T(8,128)S(1)} %get-tuple-element.68), channel_id=1, source_target_pairs={{1,2},{3,4},{5,6},{2,1},{4,3},{6,5},{0,7},{7,0},{9,10},{11,12},{13... | collective-permute-start | bytes 393224 | tf_op jit(solution)/shard_map/ppermute | solution.py:565
  44.5 6.6 %collective-permute-start.18 = (f32[200,128]{1,0:T(8,128)S(1)}, f32[200,128]{1,0:T(8,128)S(1)}, u32[]{:S(2)}, u32[]{:S(2)}) collective-permute-start(f32[200,128]{1,0:T(8,128)S(1)} %add.54), channel_id=1, source_target_pairs={{0,6},{1,7},{2,4},{3,5},{4,2},{5,3},{6,0},{7,1},{8,14},{9,15},{10,... | collective-permute-start | bytes 307208 | tf_op jit(solution)/shard_map/ppermute | solution.py:502
  51.3 6.5 %collective-permute-start.21 = (f32[384,128]{1,0:T(8,128)S(1)}, f32[384,128]{1,0:T(8,128)S(1)}, u32[]{:S(2)}, u32[]{:S(2)}) collective-permute-start(f32[384,128]{1,0:T(8,128)S(1)} %pad_maximum_fusion), channel_id=1, source_target_pairs={{0,1},{1,0},{2,3},{3,2},{4,5},{5,4},{6,7},{7,6},{8,9},{9,8},{10,11... | collective-permute-start | bytes 589832 | tf_op jit(solution)/shard_map/ppermute | solution.py:502
  51.7 5.3 %collective-permute-start.23 = (f32[2,64,128]{2,1,0:T(8,128)S(1)}, f32[2,64,128]{2,1,0:T(8,128)S(1)}, u32[]{:S(2)}, u32[]{:S(2)}) collective-permute-start(f32[2,64,128]{2,1,0:T(8,128)S(1)} %fusion.1), channel_id=1, source_target_pairs={{0,17},{1,16},{2,19},{3,18},{4,21},{5,20},{6,23},{7,22},{8,25},{9,... | collective-permute-start | bytes 196616 | tf_op jit(solution)/shard_map/ppermute | solution.py:549
  53.5 4.3 %collective-permute-start.22 = (f32[2,64,128]{2,1,0:T(8,128)S(1)}, f32[2,64,128]{2,1,0:T(8,128)S(1)}, u32[]{:S(2)}, u32[]{:S(2)}) collective-permute-start(f32[2,64,128]{2,1,0:T(8,128)S(1)} %fusion.1), channel_id=1, source_target_pairs={{0,16},{8,24},{16,0},{24,8},{1,17},{9,25},{17,1},{25,9},{2,18},{10... | collective-permute-start | bytes 196616 | tf_op jit(solution)/shard_map/ppermute | solution.py:502
  57.9 1.6 %collective-permute-start.24 = (f32[2,256,128]{2,1,0:T(8,128)S(1)}, f32[2,256,128]{2,1,0:T(8,128)S(1)}, u32[]{:S(2)}, u32[]{:S(2)}) collective-permute-start(f32[2,256,128]{2,1,0:T(8,128)S(1)} %maximum_select_fusion.fresh), channel_id=1, source_target_pairs={{0,8},{8,0},{16,24},{24,16},{1,9},{9,1},{17,25},{25,17},{2,10},{10... | collective-permute-start | bytes 786440 | tf_op jit(solution)/shard_map/ppermute | solution.py:502

commit v7 on v6

--- a/solution.py
+++ b/solution.py
@@ -534,8 +534,10 @@
     probe_late, other_rim = tie((probe_field, other_rim))
     light = lighting(scan_offsets, live_counts, probe_late, tile_r, tile_c)
     beyond[2], light = tie((beyond[2], light))
+    far_rims = core([jnp.concatenate(beyond[1:])])[0]
+    far = [*core(beyond[:1]), far_rims[:2], far_rims[2:]]
     kept, given, own_probe, delta = exit_update(
-        scan_offsets, live_counts, probe_field, staged, own + core(own) + core(beyond)
+        scan_offsets, live_counts, probe_field, staged, own + core(own) + far
     )
 
     def pick(condition, first, second):

time: 61 us -> 62.1 us (1.018)
    ppermute x15 -> x14, starting transfers between devices: 10.2 us -> 11.9 us  [exchange(): return lax.ppermute(value, axis, [(i, i ^ bit) for i in range(count)])]
    ppermute x2, waiting for transfers between devices: 3.97 us -> 4.91 us  [all_three(): diagonal = lax.ppermute(diagonal, ('row', 'col'), square)]
    ppermute x1, starting transfers between devices: 3.48 us -> 2.55 us  [shards(): lax.ppermute(rim[2:], 'col', others + [(0, cols - 1), (cols - 1, 0)])]
    ppermute x15 -> x14, waiting for transfers between devices: 12.3 us -> 11.9 us  [exchange(): return lax.ppermute(value, axis, [(i, i ^ bit) for i in range(count)])]
  transfers between devices with their start and end apart: 25 -> 24, of which waited for: 14 -> 16; matrix products, arithmetic and copies ran while one was open for 1% -> 1% of each run, Pallas kernels for 10% -> 10%
where the time goes in v7:
time: 62.1 us; the launch traced here: 61.3 us
  waiting for transfers between devices  24.5 us (39%)
  starting transfers between devices  22.5 us (36%)
  Pallas kernels  11.4 us (18%)
  other arithmetic  1.27 us (2%)
  between operations  0.85 us (1%)
  local copies, waits for them, and re-layouts  0.75 us (1%)
    ppermute x14, waiting for transfers between devices, exchange(): return lax.ppermute(value, axis, [(i, i ^ bit) for i in range(count)])  11.9 us
    ppermute x14, starting transfers between devices, exchange(): return lax.ppermute(value, axis, [(i, i ^ bit) for i in range(count)])  11.9 us
    ppermute x2, waiting for transfers between devices, all_three(): diagonal = lax.ppermute(diagonal, ('row', 'col'), square)  4.91 us
    pallas_call x1, Pallas kernels, exit_update(): pl.pallas_call(delta_kernel, out_shape=[jax.ShapeDtypeStruct((3 * width +...  4.29 us
    ppermute x1, starting transfers between devices, shards(): pair_rim = lax.ppermute(jnp.where(col_odd == 0, high, low), 'col', pairs)  3.03 us
    ppermute x1, waiting for transfers between devices, shards(): pair_rim = lax.ppermute(jnp.where(col_odd == 0, high, low), 'col', pairs)  2.82 us
    ppermute x2, waiting for transfers between devices, shards(): lax.ppermute(block, 'row', toward)  2.75 us
    ppermute x1, starting transfers between devices, shards(): lax.ppermute(rim[2:], 'col', others + [(0, cols - 1), (cols - 1, 0)])  2.55 us
  transfers between devices with their start and end apart: 24, of which 16 were waited for; matrix products, arithmetic and copies ran while one was open for 1% of the time, Pallas kernels for 10%

profile of v7, /device:TPU:0, one launch (start us, length us, event | category | flops | bytes accessed | tf_op | source)
XLA Modules:
  0.0 61.3 jit_solution(14292601323767273789)
XLA Ops:
  0.7 1.0 %slice_select_fusion = (f32[2,128,128]{2,1,0:T(8,128)S(1)}, f32[2,128,128]{2,1,0:T(8,128)S(1)}) fusion(f32[2,128,256]{2,1,0:T(8,128)} %specimen.1, pred[]{:T(512)S(6)} %eq.13), kind=kLoop, calls=%fused_computation.7 | loop fusion | flops 65536 | bytes 524289 | tf_op jit(solution)/shard_map/jit(_where)/select_n | solution.py:526
  1.7 3.0 %collective-permute-start.1 = (f32[2,128,128]{2,1,0:T(8,128)S(1)}, f32[2,128,128]{2,1,0:T(8,128)S(1)}, u32[]{:S(2)}, u32[]{:S(2)}) collective-permute-start(f32[2,128,128]{2,1,0:T(8,128)S(1)} %get-tuple-element.71), channel_id=1, source_target_pairs={{0,1},{1,0},{2,3},{3,2},{4,5},{5,4},{6,7},{7,6},{8,9},{9,8},{10,11... | collective-permute-start | bytes 393224 | tf_op jit(solution)/shard_map/ppermute | solution.py:526
  4.7 0.7 %collective-permute-start = (f32[2,128,128]{2,1,0:T(8,128)S(1)}, f32[2,128,128]{2,1,0:T(8,128)S(1)}, u32[]{:S(2)}, u32[]{:S(2)}) collective-permute-start(f32[2,128,128]{2,1,0:T(8,128)S(1)} %get-tuple-element.72), channel_id=1, source_target_pairs={{1,2},{3,4},{5,6},{2,1},{4,3},{6,5},{9,10},{11,12},{13,14},{10,9},... | collective-permute-start | bytes 393224 | tf_op jit(solution)/shard_map/ppermute | solution.py:527
  5.4 2.8 %collective-permute-done.1.pair_rim = f32[2,128,128]{2,1,0:T(8,128)S(1)} collective-permute-done((f32[2,128,128]{2,1,0:T(8,128)S(1)}, f32[2,128,128]{2,1,0:T(8,128)S(1)}, u32[]{:S(2)}, u32[]{:S(2)}) %collective-permute-start.1) | collective-permute-done | bytes 131104 | tf_op jit(solution)/shard_map/ppermute | solution.py:526
  8.2 0.0 collective-permute-start.3
  8.2 2.2 %shard_map.77 = (f32[2,256,256]{2,1,0:T(8,128)S(1)}, bf16[4,2,256,256]{3,2,1,0:T(8,128)(2,1)S(1)}) custom-call(f32[2,256,256]{2,1,0:T(8,128)} %bitcast.13, bf16[4,2,256,256]{3,2,1,0:T(8,128)(2,1)} %constant.54.clone.tables), custom_call_target="tpu_custom_call" | custom-call | flops 400000000 | bytes 3000000 | tf_op jit(solution)/shard_map/pallas_call | solution.py:354
  10.4 0.7 %collective-permute-done.2 = f32[2,128,256]{2,1,0:T(8,128)S(1)} collective-permute-done((f32[2,128,256]{2,1,0:T(8,128)S(1)}, f32[2,128,256]{2,1,0:T(8,128)S(1)}, u32[]{:S(2)}, u32[]{:S(2)}) %collective-permute-start.2) | collective-permute-done | bytes 262176 | tf_op jit(solution)/shard_map/ppermute | solution.py:530
  11.1 2.1 %collective-permute-done.3 = f32[2,128,128]{2,1,0:T(8,128)S(1)} collective-permute-done((f32[2,128,128]{2,1,0:T(8,128)S(1)}, f32[2,128,128]{2,1,0:T(8,128)S(1)}, u32[]{:S(2)}, u32[]{:S(2)}) %collective-permute-start.3) | collective-permute-done | bytes 131104 | tf_op jit(solution)/shard_map/ppermute | solution.py:530
  13.2 0.1 copy.8.offsets
  13.3 0.5 copy-done.2
  13.9 2.2 %shard_map.78.light = f32[128,256]{1,0:T(8,128)S(1)} custom-call(s32[4,8,2,2]{3,2,1,0:T(2,128)S(1)} %copy.8.offsets, s32[4,8]{1,0:T(4,128)S(1)} %copy-done.2, f32[2,256,256]{2,1,0:T(8,128)S(1)} %copy-done), custom_call_target="tpu_custom_call" | custom-call | flops 40000000 | bytes 8000000 | tf_op jit(solution)/shard_map/pallas_call | solution.py:145
  16.1 2.1 %collective-permute-done.4 = f32[2,128,128]{2,1,0:T(8,128)S(1)} collective-permute-done((f32[2,128,128]{2,1,0:T(8,128)S(1)}, f32[2,128,128]{2,1,0:T(8,128)S(1)}, u32[]{:S(2)}, u32[]{:S(2)}) %collective-permute-start.4) | collective-permute-done | bytes 131104 | tf_op jit(solution)/shard_map/ppermute | solution.py:533
  18.2 0.1 collective-permute-start.9
  18.3 0.5 collective-permute-start.5
  18.8 0.1 collective-permute-start.8
  18.8 0.4 collective-permute-start.6
  19.3 0.1 collective-permute-start.7
  19.3 0.4 collective-permute-done.9
  19.8 0.4 collective-permute-done.5.near
  20.2 0.6 collective-permute-done.6.near_pair
  20.7 0.2 collective-permute-done.7.near_other
  20.9 4.3 %shard_map.79 = (f32[776,128]{1,0:T(8,128)S(1)}, f32[776,128]{1,0:T(8,128)S(1)}, f32[2,64,128]{2,1,0:T(8,128)S(1)}, f32[2,2,256,256]{3,2,1,0:T(8,128)S(1)}) custom-call(s32[4,8,2,2]{3,2,1,0:T(2,128)S(1)} %copy.8.offsets, s32[4,8]{1,0:T(4,128)S(1)} %copy-done.2, f32[2,256,256]{2,1,0:T(8,128)S(1)} %copy-done, f32[2,256,256]{2,1,0:T(8,128)S(1)} %get-tuple-element.40.magnitudes, ...), custom_call_target="tpu_custom_call" | custom-call | flops 3200000000 | bytes 8000000 | tf_op jit(solution)/shard_map/pallas_call | solution.py:378
  25.2 0.2 collective-permute-start.10
  25.4 1.7 %shard_map.80 = (f32[4,128,128]{2,1,0:T(8,128)S(1)}, f32[4,128,128]{2,1,0:T(8,128)S(1)}, f32[16,128,128]{2,1,0:T(8,128)S(1)}) custom-call(s32[4,8,2,2]{3,2,1,0:T(2,128)S(1)} %copy.8.offsets, f32[2,256,256]{2,1,0:T(8,128)S(1)} %copy-done, f32[2,2,256,256]{3,2,1,0:T(8,128)S(1)} %get-tuple-element.45.delta), custom_call_target="tpu_custom_call" | custom-call | flops 4000000 | bytes 4000000 | tf_op jit(solution)/shard_map/pallas_call | solution.py:488
  27.2 0.0 collective-permute-done.10.got
  27.2 0.4 collective-permute-start.11
  27.6 0.1 shard_map.81
  27.7 1.8 %collective-permute-start.13 = (f32[200,128]{1,0:T(8,128)S(1)}, f32[200,128]{1,0:T(8,128)S(1)}, u32[]{:S(2)}, u32[]{:S(2)}) collective-permute-start(f32[200,128]{1,0:T(8,128)S(1)} %get-tuple-element.54), channel_id=1, source_target_pairs={{0,1},{1,0},{2,3},{3,2},{4,5},{5,4},{6,7},{7,6},{8,9},{9,8},{10,11... | collective-permute-start | bytes 307208 | tf_op jit(solution)/shard_map/ppermute | solution.py:502
  29.5 1.8 %collective-permute-start.12 = (f32[200,128]{1,0:T(8,128)S(1)}, f32[200,128]{1,0:T(8,128)S(1)}, u32[]{:S(2)}, u32[]{:S(2)}) collective-permute-start(f32[200,128]{1,0:T(8,128)S(1)} %get-tuple-element.53), channel_id=1, source_target_pairs={{0,16},{8,24},{16,0},{24,8},{1,17},{9,25},{17,1},{25,9},{2,18},{10... | collective-permute-start | bytes 307208 | tf_op jit(solution)/shard_map/ppermute | solution.py:502
  31.3 0.3 collective-permute-start.15
  31.5 2.6 %collective-permute-done.13 = f32[200,128]{1,0:T(8,128)S(1)} collective-permute-done((f32[200,128]{1,0:T(8,128)S(1)}, f32[200,128]{1,0:T(8,128)S(1)}, u32[]{:S(2)}, u32[]{:S(2)}) %collective-permute-start.13) | collective-permute-done | bytes 102432 | tf_op jit(solution)/shard_map/ppermute | solution.py:502
  34.1 2.0 %collective-permute-done.14 = f32[200,128]{1,0:T(8,128)S(1)} collective-permute-done((f32[200,128]{1,0:T(8,128)S(1)}, f32[200,128]{1,0:T(8,128)S(1)}, u32[]{:S(2)}, u32[]{:S(2)}) %collective-permute-start.14) | collective-permute-done | bytes 102432 | tf_op jit(solution)/shard_map/ppermute | solution.py:551
  36.1 1.0 %collective-permute-done.12 = f32[200,128]{1,0:T(8,128)S(1)} collective-permute-done((f32[200,128]{1,0:T(8,128)S(1)}, f32[200,128]{1,0:T(8,128)S(1)}, u32[]{:S(2)}, u32[]{:S(2)}) %collective-permute-start.12) | collective-permute-done | bytes 102432 | tf_op jit(solution)/shard_map/ppermute | solution.py:502
  37.2 2.2 %collective-permute-start.16 = (f32[200,128]{1,0:T(8,128)S(1)}, f32[200,128]{1,0:T(8,128)S(1)}, u32[]{:S(2)}, u32[]{:S(2)}) collective-permute-start(f32[200,128]{1,0:T(8,128)S(1)} %add_add_fusion), channel_id=1, source_target_pairs={{0,2},{1,3},{2,0},{3,1},{4,6},{5,7},{6,4},{7,5},{8,10},{9,11},{10,... | collective-permute-start | bytes 307208 | tf_op jit(solution)/shard_map/ppermute | solution.py:502
  39.3 0.1 fusion.2
  39.4 2.1 %collective-permute-start.19 = (f32[4,128,128]{2,1,0:T(8,128)S(1)}, f32[4,128,128]{2,1,0:T(8,128)S(1)}, u32[]{:S(2)}, u32[]{:S(2)}) collective-permute-start(f32[4,128,128]{2,1,0:T(8,128)S(1)} %get-tuple-element.64), channel_id=1, source_target_pairs={{24,8},{0,16},{16,24},{8,0},{25,9},{1,17},{17,25},{9,1},{26,10},{2... | collective-permute-start | bytes 786440 | tf_op jit(solution)/shard_map/ppermute | solution.py:560
  41.6 2.5 %collective-permute-start.18 = (f32[2,128,128]{2,1,0:T(8,128)S(1)}, f32[2,128,128]{2,1,0:T(8,128)S(1)}, u32[]{:S(2)}, u32[]{:S(2)}) collective-permute-start(f32[2,128,128]{2,1,0:T(8,128)S(1)} %get-tuple-element.68), channel_id=1, source_target_pairs={{1,2},{3,4},{5,6},{2,1},{4,3},{6,5},{0,7},{7,0},{9,10},{11,12},{13... | collective-permute-start | bytes 393224 | tf_op jit(solution)/shard_map/ppermute | solution.py:567
  44.1 2.7 %collective-permute-start.17 = (f32[200,128]{1,0:T(8,128)S(1)}, f32[200,128]{1,0:T(8,128)S(1)}, u32[]{:S(2)}, u32[]{:S(2)}) collective-permute-start(f32[200,128]{1,0:T(8,128)S(1)} %add.54), channel_id=1, source_target_pairs={{0,6},{1,7},{2,4},{3,5},{4,2},{5,3},{6,0},{7,1},{8,14},{9,15},{10,... | collective-permute-start | bytes 307208 | tf_op jit(solution)/shard_map/ppermute | solution.py:502
  46.8 4.4 %collective-permute-done.17 = f32[200,128]{1,0:T(8,128)S(1)} collective-permute-done((f32[200,128]{1,0:T(8,128)S(1)}, f32[200,128]{1,0:T(8,128)S(1)}, u32[]{:S(2)}, u32[]{:S(2)}) %collective-permute-start.17) | collective-permute-done | bytes 102432 | tf_op jit(solution)/shard_map/ppermute | solution.py:502
  51.4 1.0 %collective-permute-start.20 = (f32[384,128]{1,0:T(8,128)S(1)}, f32[384,128]{1,0:T(8,128)S(1)}, u32[]{:S(2)}, u32[]{:S(2)}) collective-permute-start(f32[384,128]{1,0:T(8,128)S(1)} %pad_maximum_fusion.1), channel_id=1, source_target_pairs={{0,1},{1,0},{2,3},{3,2},{4,5},{5,4},{6,7},{7,6},{8,9},{9,8},{10,11... | collective-permute-start | bytes 589832 | tf_op jit(solution)/shard_map/ppermute | solution.py:502
  52.3 1.9 %collective-permute-start.22 = (f32[2,64,128]{2,1,0:T(8,128)S(1)}, f32[2,64,128]{2,1,0:T(8,128)S(1)}, u32[]{:S(2)}, u32[]{:S(2)}) collective-permute-start(f32[2,64,128]{2,1,0:T(8,128)S(1)} %fusion.1), channel_id=1, source_target_pairs={{0,17},{1,16},{2,19},{3,18},{4,21},{5,20},{6,23},{7,22},{8,25},{9,... | collective-permute-start | bytes 196616 | tf_op jit(solution)/shard_map/ppermute | solution.py:551
  54.3 0.7 %collective-permute-start.21 = (f32[2,64,128]{2,1,0:T(8,128)S(1)}, f32[2,64,128]{2,1,0:T(8,128)S(1)}, u32[]{:S(2)}, u32[]{:S(2)}) collective-permute-start(f32[2,64,128]{2,1,0:T(8,128)S(1)} %fusion.1), channel_id=1, source_target_pairs={{0,16},{8,24},{16,0},{24,8},{1,17},{9,25},{17,1},{25,9},{2,18},{10... | collective-permute-start | bytes 196616 | tf_op jit(solution)/shard_map/ppermute | solution.py:502
  54.9 2.9 %collective-permute-done.22 = f32[2,64,128]{2,1,0:T(8,128)S(1)} collective-permute-done((f32[2,64,128]{2,1,0:T(8,128)S(1)}, f32[2,64,128]{2,1,0:T(8,128)S(1)}, u32[]{:S(2)}, u32[]{:S(2)}) %collective-permute-start.22) | collective-permute-done | bytes 65568 | tf_op jit(solution)/shard_map/ppermute | solution.py:551
  57.8 0.7 %collective-permute-done.21 = f32[2,64,128]{2,1,0:T(8,128)S(1)} collective-permute-done((f32[2,64,128]{2,1,0:T(8,128)S(1)}, f32[2,64,128]{2,1,0:T(8,128)S(1)}, u32[]{:S(2)}, u32[]{:S(2)}) %collective-permute-start.21) | collective-permute-done | bytes 65568 | tf_op jit(solution)/shard_map/ppermute | solution.py:502
  58.5 0.2 collective-permute-done.20
  58.7 0.1 collective-permute-start.23
  58.8 1.5 %collective-permute-done.23.got = f32[2,256,128]{2,1,0:T(8,128)S(1)} collective-permute-done((f32[2,256,128]{2,1,0:T(8,128)S(1)}, f32[2,256,128]{2,1,0:T(8,128)S(1)}, u32[]{:S(2)}, u32[]{:S(2)}) %collective-permute-start.23) | collective-permute-done | bytes 262176 | tf_op jit(solution)/shard_map/ppermute | solution.py:502
  60.3 1.0 %shard_map.82 = (f32[2,128,256]{2,1,0:T(8,128)}, f32[2,256,256]{2,1,0:T(8,128)}) custom-call(f32[2,128,256]{2,1,0:T(8,128)S(1)} %copy-done.1, f32[128,256]{1,0:T(8,128)S(1)} %shard_map.78.light, f32[4,128,128]{2,1,0:T(8,128)S(1)} %get-tuple-element.46.center, f32[4,128,128]{2,1,0:T(8,128)S(1)} %get-tuple-element.66.close, ...), custom_call_target="tpu_custom_call" | custom-call | flops 1000000 | bytes 3000000 | tf_op jit(solution)/shard_map/pallas_call | solution.py:433
  (33 shorter events, 0.3 us)
Async XLA Ops:
  0.6 4.1 %copy-start.1 = (f32[2,128,256]{2,1,0:T(8,128)S(1)}, f32[2,128,256]{2,1,0:T(8,128)}, u32[]{:S(2)}) copy-start(f32[2,128,256]{2,1,0:T(8,128)} %specimen.1) | copy-start | bytes 786436
  1.7 6.5 %collective-permute-start.1 = (f32[2,128,128]{2,1,0:T(8,128)S(1)}, f32[2,128,128]{2,1,0:T(8,128)S(1)}, u32[]{:S(2)}, u32[]{:S(2)}) collective-permute-start(f32[2,128,128]{2,1,0:T(8,128)S(1)} %get-tuple-element.71), channel_id=1, source_target_pairs={{0,1},{1,0},{2,3},{3,2},{4,5},{5,4},{6,7},{7,6},{8,9},{9,8},{10,11... | collective-permute-start | bytes 393224 | tf_op jit(solution)/shard_map/ppermute | solution.py:526
  4.7 6.4 %collective-permute-start.2 = (f32[2,128,256]{2,1,0:T(8,128)S(1)}, f32[2,128,256]{2,1,0:T(8,128)S(1)}, u32[]{:S(2)}, u32[]{:S(2)}) collective-permute-start(f32[2,128,256]{2,1,0:T(8,128)S(1)} %copy-done.1), channel_id=1, source_target_pairs={{8,24},{16,0},{24,16},{0,8},{9,25},{17,1},{25,17},{1,9},{10,26},{1... | collective-permute-start | bytes 786440 | tf_op jit(solution)/shard_map/ppermute | solution.py:530
  4.7 5.7 %collective-permute-start = (f32[2,128,128]{2,1,0:T(8,128)S(1)}, f32[2,128,128]{2,1,0:T(8,128)S(1)}, u32[]{:S(2)}, u32[]{:S(2)}) collective-permute-start(f32[2,128,128]{2,1,0:T(8,128)S(1)} %get-tuple-element.72), channel_id=1, source_target_pairs={{1,2},{3,4},{5,6},{2,1},{4,3},{6,5},{9,10},{11,12},{13,14},{10,9},... | collective-permute-start | bytes 393224 | tf_op jit(solution)/shard_map/ppermute | solution.py:527
  8.2 5.1 %copy-start = (f32[2,256,256]{2,1,0:T(8,128)S(1)}, f32[2,256,256]{2,1,0:T(8,128)}, u32[]{:S(2)}) copy-start(f32[2,256,256]{2,1,0:T(8,128)} %probe.4) | copy-start | bytes 1572868
  8.2 5.0 %collective-permute-start.3 = (f32[2,128,128]{2,1,0:T(8,128)S(1)}, f32[2,128,128]{2,1,0:T(8,128)S(1)}, u32[]{:S(2)}, u32[]{:S(2)}) collective-permute-start(f32[2,128,128]{2,1,0:T(8,128)S(1)} %collective-permute-done.1.pair_rim), channel_id=1, source_target_pairs={{8,24},{16,0},{24,16},{0,8},{9,25},{17,1},{25,17},{1,9},{10,26},{1... | collective-permute-start | bytes 393224 | tf_op jit(solution)/shard_map/ppermute | solution.py:530
  8.2 5.0 %copy-start.3 = (s32[4,8,2,2]{1,3,2,0:T(2,128)S(1)}, s32[4,8,2,2]{1,3,2,0:T(2,128)}, u32[]{:S(2)}) copy-start(s32[4,8,2,2]{1,3,2,0:T(2,128)} %param.8) | copy-start | bytes 1540
  13.2 0.7 %copy-start.2 = (s32[4,8]{1,0:T(4,128)S(1)}, s32[4,8]{1,0:T(4,128)}, u32[]{:S(2)}) copy-start(s32[4,8]{1,0:T(4,128)} %counts.3) | copy-start | bytes 388
  13.2 5.0 %collective-permute-start.4 = (f32[2,128,128]{2,1,0:T(8,128)S(1)}, f32[2,128,128]{2,1,0:T(8,128)S(1)}, u32[]{:S(2)}, u32[]{:S(2)}) collective-permute-start(f32[2,128,128]{2,1,0:T(8,128)S(1)} %collective-permute-done.other_rim), channel_id=1, source_target_pairs={{8,24},{16,0},{24,16},{0,8},{9,25},{17,1},{25,17},{1,9},{10,26},{1... | collective-permute-start | bytes 393224 | tf_op jit(solution)/shard_map/ppermute | solution.py:533
  18.2 1.6 %collective-permute-start.9 = (f32[4,128,128]{2,1,0:T(8,128)S(1)}, f32[4,128,128]{2,1,0:T(8,128)S(1)}, u32[]{:S(2)}, u32[]{:S(2)}) collective-permute-start(f32[4,128,128]{2,1,0:T(8,128)S(1)} %pad_maximum_fusion), channel_id=1, source_target_pairs={{0,8},{8,0},{16,24},{24,16},{1,9},{9,1},{17,25},{25,17},{2,10},{10... | collective-permute-start | bytes 786440 | tf_op jit(solution)/shard_map/ppermute | solution.py:502
  18.3 1.9 %collective-permute-start.5 = (f32[2,128,256]{2,1,0:T(8,128)S(1)}, f32[2,128,256]{2,1,0:T(8,128)S(1)}, u32[]{:S(2)}, u32[]{:S(2)}) collective-permute-start(f32[2,128,256]{2,1,0:T(8,128)S(1)} %copy-done.1), channel_id=1, source_target_pairs={{0,8},{8,0},{16,24},{24,16},{1,9},{9,1},{17,25},{25,17},{2,10},{10... | collective-permute-start | bytes 786440 | tf_op jit(solution)/shard_map/ppermute | solution.py:502
  18.8 2.2 %collective-permute-start.8 = (f32[2,128,256]{2,1,0:T(8,128)S(1)}, f32[2,128,256]{2,1,0:T(8,128)S(1)}, u32[]{:S(2)}, u32[]{:S(2)}) collective-permute-start(f32[2,128,256]{2,1,0:T(8,128)S(1)} %collective-permute-done.2), channel_id=1, source_target_pairs={{0,8},{8,0},{16,24},{24,16},{1,9},{9,1},{17,25},{25,17},{2,10},{10... | collective-permute-start | bytes 786440 | tf_op jit(solution)/shard_map/ppermute | solution.py:502
  18.8 1.9 %collective-permute-start.6 = (f32[2,128,128]{2,1,0:T(8,128)S(1)}, f32[2,128,128]{2,1,0:T(8,128)S(1)}, u32[]{:S(2)}, u32[]{:S(2)}) collective-permute-start(f32[2,128,128]{2,1,0:T(8,128)S(1)} %collective-permute-done.1.pair_rim), channel_id=1, source_target_pairs={{0,8},{8,0},{16,24},{24,16},{1,9},{9,1},{17,25},{25,17},{2,10},{10... | collective-permute-start | bytes 393224 | tf_op jit(solution)/shard_map/ppermute | solution.py:502
  19.3 1.6 %collective-permute-start.7 = (f32[2,128,128]{2,1,0:T(8,128)S(1)}, f32[2,128,128]{2,1,0:T(8,128)S(1)}, u32[]{:S(2)}, u32[]{:S(2)}) collective-permute-start(f32[2,128,128]{2,1,0:T(8,128)S(1)} %collective-permute-done.other_rim), channel_id=1, source_target_pairs={{0,8},{8,0},{16,24},{24,16},{1,9},{9,1},{17,25},{25,17},{2,10},{10... | collective-permute-start | bytes 393224 | tf_op jit(solution)/shard_map/ppermute | solution.py:502
  25.2 2.0 %collective-permute-start.10 = (f32[776,128]{1,0:T(8,128)S(1)}, f32[776,128]{1,0:T(8,128)S(1)}, u32[]{:S(2)}, u32[]{:S(2)}) collective-permute-start(f32[776,128]{1,0:T(8,128)S(1)} %get-tuple-element.47), channel_id=1, source_target_pairs={{0,8},{8,0},{16,24},{24,16},{1,9},{9,1},{17,25},{25,17},{2,10},{10... | collective-permute-start | bytes 1191944 | tf_op jit(solution)/shard_map/ppermute | solution.py:502
  27.2 4.1 %collective-permute-start.11 = (f32[16,128,128]{2,1,0:T(8,128)S(1)}, f32[16,128,128]{2,1,0:T(8,128)S(1)}, u32[]{:S(2)}, u32[]{:S(2)}) collective-permute-start(f32[16,128,128]{2,1,0:T(8,128)S(1)} %get-tuple-element.49), channel_id=1, source_target_pairs={{0,8},{8,0},{16,24},{24,16},{1,9},{9,1},{17,25},{25,17},{2,10},{10... | collective-permute-start | bytes 3145736 | tf_op jit(solution)/shard_map/ppermute | solution.py:502
  27.7 6.4 %collective-permute-start.13 = (f32[200,128]{1,0:T(8,128)S(1)}, f32[200,128]{1,0:T(8,128)S(1)}, u32[]{:S(2)}, u32[]{:S(2)}) collective-permute-start(f32[200,128]{1,0:T(8,128)S(1)} %get-tuple-element.54), channel_id=1, source_target_pairs={{0,1},{1,0},{2,3},{3,2},{4,5},{5,4},{6,7},{7,6},{8,9},{9,8},{10,11... | collective-permute-start | bytes 307208 | tf_op jit(solution)/shard_map/ppermute | solution.py:502
  29.5 6.7 %collective-permute-start.14 = (f32[200,128]{1,0:T(8,128)S(1)}, f32[200,128]{1,0:T(8,128)S(1)}, u32[]{:S(2)}, u32[]{:S(2)}) collective-permute-start(f32[200,128]{1,0:T(8,128)S(1)} %get-tuple-element.55), channel_id=1, source_target_pairs={{0,17},{1,16},{2,19},{3,18},{4,21},{5,20},{6,23},{7,22},{8,25},{9,... | collective-permute-start | bytes 307208 | tf_op jit(solution)/shard_map/ppermute | solution.py:551
  29.5 7.7 %collective-permute-start.12 = (f32[200,128]{1,0:T(8,128)S(1)}, f32[200,128]{1,0:T(8,128)S(1)}, u32[]{:S(2)}, u32[]{:S(2)}) collective-permute-start(f32[200,128]{1,0:T(8,128)S(1)} %get-tuple-element.53), channel_id=1, source_target_pairs={{0,16},{8,24},{16,0},{24,8},{1,17},{9,25},{17,1},{25,9},{2,18},{10... | collective-permute-start | bytes 307208 | tf_op jit(solution)/shard_map/ppermute | solution.py:502
  31.3 5.9 %collective-permute-start.15 = (f32[4,128,128]{2,1,0:T(8,128)S(1)}, f32[4,128,128]{2,1,0:T(8,128)S(1)}, u32[]{:S(2)}, u32[]{:S(2)}) collective-permute-start(f32[4,128,128]{2,1,0:T(8,128)S(1)} %slice.69), channel_id=1, source_target_pairs={{24,8},{0,16},{16,24},{8,0},{25,9},{1,17},{17,25},{9,1},{26,10},{2... | collective-permute-start | bytes 786440 | tf_op jit(solution)/shard_map/ppermute | solution.py:559
  37.2 6.9 %collective-permute-start.16 = (f32[200,128]{1,0:T(8,128)S(1)}, f32[200,128]{1,0:T(8,128)S(1)}, u32[]{:S(2)}, u32[]{:S(2)}) collective-permute-start(f32[200,128]{1,0:T(8,128)S(1)} %add_add_fusion), channel_id=1, source_target_pairs={{0,2},{1,3},{2,0},{3,1},{4,6},{5,7},{6,4},{7,5},{8,10},{9,11},{10,... | collective-permute-start | bytes 307208 | tf_op jit(solution)/shard_map/ppermute | solution.py:502
  39.4 11.9 %collective-permute-start.19 = (f32[4,128,128]{2,1,0:T(8,128)S(1)}, f32[4,128,128]{2,1,0:T(8,128)S(1)}, u32[]{:S(2)}, u32[]{:S(2)}) collective-permute-start(f32[4,128,128]{2,1,0:T(8,128)S(1)} %get-tuple-element.64), channel_id=1, source_target_pairs={{24,8},{0,16},{16,24},{8,0},{25,9},{1,17},{17,25},{9,1},{26,10},{2... | collective-permute-start | bytes 786440 | tf_op jit(solution)/shard_map/ppermute | solution.py:560
  41.6 9.7 %collective-permute-start.18 = (f32[2,128,128]{2,1,0:T(8,128)S(1)}, f32[2,128,128]{2,1,0:T(8,128)S(1)}, u32[]{:S(2)}, u32[]{:S(2)}) collective-permute-start(f32[2,128,128]{2,1,0:T(8,128)S(1)} %get-tuple-element.68), channel_id=1, source_target_pairs={{1,2},{3,4},{5,6},{2,1},{4,3},{6,5},{0,7},{7,0},{9,10},{11,12},{13... | collective-permute-start | bytes 393224 | tf_op jit(solution)/shard_map/ppermute | solution.py:567
  44.1 7.1 %collective-permute-start.17 = (f32[200,128]{1,0:T(8,128)S(1)}, f32[200,128]{1,0:T(8,128)S(1)}, u32[]{:S(2)}, u32[]{:S(2)}) collective-permute-start(f32[200,128]{1,0:T(8,128)S(1)} %add.54), channel_id=1, source_target_pairs={{0,6},{1,7},{2,4},{3,5},{4,2},{5,3},{6,0},{7,1},{8,14},{9,15},{10,... | collective-permute-start | bytes 307208 | tf_op jit(solution)/shard_map/ppermute | solution.py:502
  51.4 7.3 %collective-permute-start.20 = (f32[384,128]{1,0:T(8,128)S(1)}, f32[384,128]{1,0:T(8,128)S(1)}, u32[]{:S(2)}, u32[]{:S(2)}) collective-permute-start(f32[384,128]{1,0:T(8,128)S(1)} %pad_maximum_fusion.1), channel_id=1, source_target_pairs={{0,1},{1,0},{2,3},{3,2},{4,5},{5,4},{6,7},{7,6},{8,9},{9,8},{10,11... | collective-permute-start | bytes 589832 | tf_op jit(solution)/shard_map/ppermute | solution.py:502
  52.3 5.5 %collective-permute-start.22 = (f32[2,64,128]{2,1,0:T(8,128)S(1)}, f32[2,64,128]{2,1,0:T(8,128)S(1)}, u32[]{:S(2)}, u32[]{:S(2)}) collective-permute-start(f32[2,64,128]{2,1,0:T(8,128)S(1)} %fusion.1), channel_id=1, source_target_pairs={{0,17},{1,16},{2,19},{3,18},{4,21},{5,20},{6,23},{7,22},{8,25},{9,... | collective-permute-start | bytes 196616 | tf_op jit(solution)/shard_map/ppermute | solution.py:551
  54.3 4.3 %collective-permute-start.21 = (f32[2,64,128]{2,1,0:T(8,128)S(1)}, f32[2,64,128]{2,1,0:T(8,128)S(1)}, u32[]{:S(2)}, u32[]{:S(2)}) collective-permute-start(f32[2,64,128]{2,1,0:T(8,128)S(1)} %fusion.1), channel_id=1, source_target_pairs={{0,16},{8,24},{16,0},{24,8},{1,17},{9,25},{17,1},{25,9},{2,18},{10... | collective-permute-start | bytes 196616 | tf_op jit(solution)/shard_map/ppermute | solution.py:502
  58.7 1.6 %collective-permute-start.23 = (f32[2,256,128]{2,1,0:T(8,128)S(1)}, f32[2,256,128]{2,1,0:T(8,128)S(1)}, u32[]{:S(2)}, u32[]{:S(2)}) collective-permute-start(f32[2,256,128]{2,1,0:T(8,128)S(1)} %maximum_select_fusion.fresh), channel_id=1, source_target_pairs={{0,8},{8,0},{16,24},{24,16},{1,9},{9,1},{17,25},{25,17},{2,10},{10... | collective-permute-start | bytes 786440 | tf_op jit(solution)/shard_map/ppermute | solution.py:502
